TPU v7x, 32 devices: a whole 2x2x4 slice. The times are simulated.
32 devices in a mesh: dp: 8 (over z, x), tensor: 4 (over y, core).
Axes of the slice: x: 2, y: 2, z: 4, core: 2. Of those that a mesh axis runs over, the one named last changes fastest.
Arguments:
- activations: bfloat16 [8192, 4096], P('dp', 'tensor'), may hold values from -6 to 6
- out_grad: bfloat16 [8192, 4096], P('dp', 'tensor'), may hold values from -6 to 6
- weight: bfloat16 [4096, 4096], P(None, 'tensor'), may hold values from -0.09375 to 0.09375
- error: float32 [8, 4096, 4096], P('dp', None, 'tensor'), may hold values from -6 to 6
- q_start: float32 [4096, 32], P('tensor'), may hold values from -0.09375 to 0.09375
Outputs:
- input_grad: float32 [8192, 4096], P('dp', 'tensor')
- new_error: float32 [8, 4096, 4096], P('dp', None, 'tensor')
- q_factor: float32 [4096, 32], P('tensor')
All inputs are finite; a program needn't handle non-finite values.
Results may differ from a plain program's by a relative error of at most 0.0003.
Values may be sent and summed in bfloat16 or wider, within the bound.
No kernel may reach another device: no remote copies, remote signals or barrier semaphores. Data moves between devices by JAX's collectives and lax.ppermute only.
A program may use at most 128 MiB of HBM per device.

v0:
```python
import math

import jax
import jax.numpy as jnp
from jax import lax
from jax.sharding import PartitionSpec as P

TOK_DEV = 1024


def per_device(activations, out_grad, weight, error, q_start):
    grad_scale = 1.0 / math.sqrt(TOK_DEV)
    replicas = lax.axis_size("dp")
    local_grad = lax.dot_general(
        lax.all_gather(activations, "tensor", axis=1, tiled=True),
        out_grad,
        (((0,), (0,)), ((), ())),
        preferred_element_type=jnp.float32,
    )
    merged = local_grad * grad_scale + error[0]
    input_t = lax.psum_scatter(
        lax.dot_general(
            weight, out_grad, (((1,), (1,)), ((), ())), preferred_element_type=jnp.float32
        ),
        "tensor",
        scatter_dimension=0,
        tiled=True,
    )
    input_grad = input_t.T
    local_sketch = jnp.dot(merged, q_start, precision=lax.Precision.HIGHEST)
    sketch = lax.psum(local_sketch, ("dp", "tensor")) / replicas
    gram = jnp.dot(sketch.T, sketch, precision=lax.Precision.HIGHEST)
    factor_low = jnp.linalg.cholesky(gram)
    basis = lax.linalg.triangular_solve(
        factor_low, sketch, left_side=False, lower=True, transpose_a=True
    )
    local_right = jnp.dot(merged.T, basis, precision=lax.Precision.HIGHEST)
    q_factor = lax.psum(local_right, "dp") / replicas
    approx = jnp.dot(basis, q_factor.T, precision=lax.Precision.HIGHEST)
    new_error = (merged - approx)[None]
    return (input_grad, new_error, q_factor)


def solution(mesh):
    placed = (
        P("dp", "tensor"),
        P("dp", "tensor"),
        P(None, "tensor"),
        P("dp", None, "tensor"),
        P("tensor", None),
    )
    return jax.shard_map(
        per_device,
        mesh=mesh,
        in_specs=placed,
        out_specs=(P("dp", "tensor"), P("dp", None, "tensor"), P("tensor", None)),
        check_vma=False,
    )
```

profile of v0, /device:TPU:0, one launch (start us, length us, event | category | flops | bytes accessed | tf_op | source)
XLA Modules:
  0.0 469.6 jit_solution(7117676047183901718)
XLA Ops:
  7.2 0.0 all-gather.2.cloned.1.call-start
  7.2 0.7 all-gather.2.cloned.1.call-update
  7.9 0.0 all-reduce.3.cloned.1.call-start
  8.0 62.6 %all-gather.2.cloned.1.call-done = bf16[1024,4096]{1,0:T(8,128)(2,1)} async-done(((bf16[1024,1024]{1,0:T(8,128)(2,1)}), bf16[1024,4096]{1,0:T(8,128)(2,1)}) %all-gather.2.cloned.1.call-update) | async-done | bytes 8388624 | tf_op jit(solution)/shard_map/all_gather | solution.py:15
  70.6 18.4 %bitcast_add_fusion = f32[4096,1024]{1,0:T(8,128)} fusion(f32[1,4096,1024]{2,1,0:T(8,128)} %param.8, bf16[1024,4096]{1,0:T(8,128)(2,1)} %all-gather.2.cloned.1.call-done, bf16[1024,1024]{1,0:T(8,128)(2,1)S(1)} %copy-done), kind=kOutput, calls=%fused_computation | convolution fusion | flops 8598323200 | bytes 44040192 | tf_op jit(solution)/shard_map/dot_general | solution.py:14
  89.0 19.6 %fusion.12 = f32[4096,32]{0,1:T(8,128)} fusion(f32[4096,1024]{1,0:T(8,128)} %bitcast_add_fusion, f32[1024,32]{0,1:T(8,128)S(1)} %copy-done.2), kind=kOutput, calls=%fused_computation.21 | convolution fusion | flops 1610612736 | bytes 17432576 | tf_op jit(solution)/shard_map/dot_general | solution.py:30
  108.6 0.2 all-reduce.5.cloned.1.call-start
  108.8 127.8 %all-reduce.3.cloned.1.call-done = f32[4096,32]{0,1:T(8,128)} async-done(((f32[4096,32]{0,1:T(8,128)}), f32[4096,32]{0,1:T(8,128)}) %all-reduce.3.cloned.1.call-update) | async-done | bytes 524304 | tf_op jit(solution)/shard_map/psum | solution.py:31
  236.6 1.8 fusion.2
  238.4 0.1 copy.8
  238.5 2.9 cholesky.16
  241.4 0.6 compare_reduce_fusion
  242.0 0.7 fusion.6
  242.7 2.4 custom-call.6
  245.1 1.7 fusion
  246.8 14.1 %fusion.13 = f32[1024,32]{0,1:T(8,128)} fusion(f32[4096,1024]{1,0:T(8,128)} %bitcast_add_fusion, f32[4096,32]{0,1:T(8,128)S(1)} %fusion), kind=kOutput, calls=%fused_computation.22 | convolution fusion | flops 1610612736 | bytes 17432576 | tf_op jit(solution)/shard_map/dot_general | solution.py:37
  261.0 0.0 all-reduce.5.cloned.1.call-update
  261.0 0.3 reduce-scatter.2.cloned.1.call-start
  261.3 14.5 %fusion.11 = f32[4096,1024]{1,0:T(8,128)} fusion(bf16[4096,1024]{1,0:T(8,128)(2,1)} %param.7, bf16[1024,1024]{1,0:T(8,128)(2,1)S(1)} %copy-done), kind=kOutput, calls=%fused_computation.20 | convolution fusion | flops 8589934592 | bytes 27262976 | tf_op jit(solution)/shard_map/dot_general | solution.py:22
  275.8 54.1 %all-reduce.5.cloned.1.call-done = f32[1024,32]{0,1:T(8,128)} async-done(((f32[1024,32]{0,1:T(8,128)}), f32[1024,32]{0,1:T(8,128)}) %all-reduce.5.cloned.1.call-update) | async-done | bytes 131088 | tf_op jit(solution)/shard_map/psum | solution.py:38
  329.9 0.9 broadcast_multiply_fusion
  330.8 19.9 %subtract_bitcast_fusion = f32[1,4096,1024]{2,1,0:T(8,128)} fusion(f32[4096,1024]{1,0:T(8,128)} %bitcast_add_fusion, f32[4096,32]{0,1:T(8,128)S(1)} %fusion, f32[1024,32]{0,1:T(8,128)S(1)} %broadcast_multiply_fusion), kind=kOutput, calls=%fused_computation.1 | convolution fusion | flops 1614807040 | bytes 34209792 | tf_op jit(solution)/shard_map/dot_general | solution.py:39
  350.8 107.0 %reduce-scatter.2.cloned.1.call-done = f32[1024,1024]{1,0:T(8,128)} async-done(((f32[4096,1024]{1,0:T(8,128)}), f32[1024,1024]{1,0:T(8,128)}) %reduce-scatter.2.cloned.1.call-update) | async-done | bytes 4194320 | tf_op jit(solution)/shard_map/reduce_scatter | solution.py:21
  457.7 5.3 %copy.9 = f32[1024,1024]{1,0:T(8,128)} copy(f32[1024,1024]{0,1:T(8,128)} %bitcast.24) | data formatting | bytes 8388608
  (10 shorter events, 0.1 us)
Async XLA Ops:
  7.2 63.4 %copy-start = (bf16[1024,1024]{1,0:T(8,128)(2,1)S(1)}, bf16[1024,1024]{1,0:T(8,128)(2,1)}, u32[]{:S(2)}) copy-start(bf16[1024,1024]{1,0:T(8,128)(2,1)} %param.6) | copy-start | bytes 6291460
  7.2 63.4 %all-gather.2.cloned.1.call-start = ((), (), s32[]{:S(2)}) async-start(), calls=%async_computation.2 | async-start | bytes 10485760 | tf_op jit(solution)/shard_map/all_gather | solution.py:15
  7.9 81.1 %copy-start.2 = (f32[1024,32]{0,1:T(8,128)S(1)}, f32[1024,32]{0,1:T(8,128)}, u32[]{:S(2)}) copy-start(f32[1024,32]{0,1:T(8,128)} %param.9) | copy-start | bytes 393220
  7.9 228.7 %all-reduce.3.cloned.1.call-start = ((), (), s32[]{:S(2)}) async-start(), calls=%async_computation.3 | async-start | bytes 1048576 | tf_op jit(solution)/shard_map/psum | solution.py:31
  108.6 221.3 %all-reduce.5.cloned.1.call-start = ((), (), s32[]{:S(2)}) async-start(), calls=%async_computation.4 | async-start | bytes 262144 | tf_op jit(solution)/shard_map/psum | solution.py:38
  261.0 196.7 %reduce-scatter.2.cloned.1.call-start = ((), (), s32[]{:S(2)}) async-start(), calls=%async_computation.1 | async-start | bytes 20971520 | tf_op jit(solution)/shard_map/reduce_scatter | solution.py:21
  330.8 19.9 %copy-start.1 = (f32[1024,32]{0,1:T(8,128)}, f32[1024,32]{0,1:T(8,128)S(1)}, u32[]{:S(2)}) copy-start(f32[1024,32]{0,1:T(8,128)S(1)} %broadcast_multiply_fusion) | copy-start | bytes 393220
Sparse Core Ops, SparseCore 0:
  9.6 60.9 all-gather.1
  108.7 127.8 all-reduce.2
  261.1 68.7 all-reduce.4
  332.3 125.3 reduce-scatter.1
where the time goes:
time: 470 us
  waiting for transfers between devices  352 us (75%)
  matrix products  90.1 us (19%)
  between operations  13.8 us (3%)
  other arithmetic  7.6 us (2%)
  local copies, waits for them, and re-layouts  5.43 us (1%)
    psum x1, waiting for transfers between devices, per_device(): sketch = lax.psum(local_sketch, ('dp', 'tensor')) / replicas  128 us
    reduce_scatter x1, waiting for transfers between devices, per_device(): lax.psum_scatter(lax.dot_general(weight, out_grad, (((1,), (1,)), ((), ()...  107 us
    all_gather x1, waiting for transfers between devices, per_device(): lax.all_gather(activations, 'tensor', axis=1, tiled=True)  62.6 us
    psum x1, waiting for transfers between devices, per_device(): q_factor = lax.psum(local_right, 'dp') / replicas  54.1 us
    dot_general x1, matrix products, per_device(): approx = jnp.dot(basis, q_factor.T, precision=lax.Precision.HIGHEST)  19.9 us
    dot_general x1, matrix products, per_device(): local_sketch = jnp.dot(merged, q_start, precision=lax.Precision.HIGHEST)  19.6 us
    dot_general x1, matrix products, per_device(): lax.dot_general(lax.all_gather(activations, 'tensor', axis=1, tiled=True)...  18.4 us
    dot_general x1, matrix products, per_device(): lax.dot_general(weight, out_grad, (((1,), (1,)), ((), ())), preferred_ele...  14.5 us
  transfers between devices with their start and end apart: 4, of which 4 were waited for; matrix products, arithmetic and copies ran while one was open for 8% of the time, Pallas kernels for 0%

commit v1 on v0

v1 whole, which is shorter than its diff:
```python
import functools
import math

import jax
import jax.numpy as jnp
from jax import lax
from jax.experimental import pallas as pl
from jax.experimental.pallas import tpu as pltpu
from jax.sharding import PartitionSpec as P

TOK_DEV = 1024
RANK = 32
MIB = 1 << 20
F32 = jnp.float32
BF16 = jnp.bfloat16


def dot(a, b, ca, cb, precision=None):
    return lax.dot_general(
        a, b, (((ca,), (cb,)), ((), ())), precision=precision, preferred_element_type=F32
    )


def split(a):
    high = a.astype(BF16)
    return high, (a - high.astype(F32)).astype(BF16)


def params(mib):
    return pltpu.CompilerParams(vmem_limit_bytes=mib * MIB)


def cost(flops, nbytes):
    return pl.CostEstimate(flops=int(flops), bytes_accessed=int(nbytes), transcendentals=0)


def sketch_kernel(ids, e_ref, qt_ref, g_ref, send_ref, keep_ref, y_ref, qs_ref, *, tok):
    phase = pl.program_id(0)
    first = (phase == 0) & (pl.program_id(1) == 0) & (pl.program_id(2) == 0)

    @pl.when(first)
    def _():
        high, low = split(qt_ref[...])
        qs_ref[0:RANK, :] = high
        qs_ref[RANK : 2 * RANK, :] = low
        both = dot(qs_ref[...], g_ref[...], 1, 1)
        y_ref[...] = both[0:RANK, :] + both[RANK : 2 * RANK, :]

    high, low = split(e_ref[...])
    main = dot(high, qs_ref[...], 1, 1)
    rest = dot(low, qs_ref[0:RANK, :], 1, 1)
    rows = (main[:, 0:RANK] + main[:, RANK : 2 * RANK] + rest).T

    @pl.when(phase == 0)
    def _():
        send_ref[0] = rows

    @pl.when(phase == 1)
    def _():
        keep_ref[0] = rows


def local_sketch(error, q_t, out_grad, core, chips, part):
    blk = min(512, part)
    per = part // blk
    tok, outs = out_grad.shape
    last = (chips - 1, per - 1)

    def e_map(p, y, j, ids):
        return ((2 * y + jnp.where(p == 0, 1 - ids[0], ids[0])) * per + j, 0)

    def send_map(p, y, j, ids):
        return (jnp.where(p == 0, y, last[0]), 0, jnp.where(p == 0, j, last[1]))

    def keep_map(p, y, j, ids):
        return (jnp.where(p == 1, y, 0), 0, jnp.where(p == 1, j, 0))

    half = jax.ShapeDtypeStruct((chips, RANK, part), F32)
    return pl.pallas_call(
        functools.partial(sketch_kernel, tok=tok),
        grid_spec=pltpu.PrefetchScalarGridSpec(
            num_scalar_prefetch=1,
            grid=(2, chips, per),
            in_specs=[
                pl.BlockSpec((blk, outs), e_map),
                pl.BlockSpec((RANK, outs), lambda p, y, j, ids: (0, 0)),
                pl.BlockSpec((tok, outs), lambda p, y, j, ids: (0, 0)),
            ],
            out_specs=[
                pl.BlockSpec((1, RANK, blk), send_map),
                pl.BlockSpec((1, RANK, blk), keep_map),
                pl.BlockSpec((RANK, tok), lambda p, y, j, ids: (0, 0)),
            ],
            scratch_shapes=[pltpu.VMEM((2 * RANK, outs), BF16)],
        ),
        out_shape=[half, half, jax.ShapeDtypeStruct((RANK, tok), F32)],
        compiler_params=params(32),
        cost_estimate=cost(6e9, error.size * 4),
        name="error_sketch",
    )(jnp.reshape(core, (1,)), error, q_t, out_grad)


def sketch_rows_kernel(*refs, n_in, n_y, n_out, scale):
    ids = refs[0]
    e_refs = refs[1 : 1 + n_in]
    y_refs = refs[1 + n_in : 1 + n_in + n_y]
    x_ref = refs[1 + n_in + n_y]
    outs = refs[2 + n_in + n_y :]
    scr = outs[-1]
    outs = outs[:-1]
    y = sum(r[...] for r in y_refs[1:]) + y_refs[0][...]
    high, low = split(y)
    both = dot(jnp.concatenate([high, low], axis=0), x_ref[...], 1, 0)
    total = (both[0:RANK, :] + both[RANK:, :]) * scale
    for r in e_refs:
        total = total + r[...]
    scr[...] = total
    width = total.shape[1] // n_out
    for k in range(n_out):
        at = pl.multiple_of((ids[0] ^ k) * width, width)
        outs[k][...] = scr[:, pl.ds(at, width)]


def sketch_rows(me, e_list, y_list, acts, n_out, scale):
    part = acts.shape[1]
    vm = pl.BlockSpec(memory_space=pltpu.VMEM)
    n = len(e_list) + len(y_list) + 1
    return pl.pallas_call(
        functools.partial(
            sketch_rows_kernel, n_in=len(e_list), n_y=len(y_list), n_out=n_out, scale=scale
        ),
        in_specs=[pl.BlockSpec(memory_space=pltpu.SMEM)] + [vm] * n,
        out_specs=[vm] * n_out,
        out_shape=[jax.ShapeDtypeStruct((RANK, part // n_out), F32)] * n_out,
        scratch_shapes=[pltpu.VMEM((RANK, part), F32)],
        compiler_params=params(24),
        cost_estimate=cost(1e9, 3e6),
        name="sketch_rows",
    )(jnp.reshape(me, (1,)), *e_list, *y_list, acts)


def basis_kernel(*refs, n_dp, n_t, width, part, inv_n, groups):
    ids, src = refs[0], refs[1]
    pieces = refs[2 : 2 + groups]
    out = refs[2 + groups]
    sk = refs[3 + groups]
    for k in range(groups):
        for r in range(n_t):
            at = pl.multiple_of(src[r] * part + (ids[0] ^ k) * width, width)
            sk[:, pl.ds(at, width)] = pieces[k][r] * inv_n
    s = sk[...]
    gram = dot(s, s, 1, 1, lax.Precision.HIGHEST)
    row = lax.broadcasted_iota(jnp.int32, (RANK, RANK), 0)
    col = lax.broadcasted_iota(jnp.int32, (RANK, RANK), 1)
    eye = (row == col).astype(F32)
    m = jnp.concatenate([gram, eye, jnp.zeros((RANK, 2 * RANK), F32)], axis=1)
    index = lax.broadcasted_iota(jnp.int32, (RANK, 1), 0)
    for j in range(RANK - 1):
        factor = jnp.where(index > j, m[:, j : j + 1] / m[j : j + 1, j : j + 1], 0.0)
        m = m - factor * m[j : j + 1, :]
    diag = jnp.sum(jnp.where(row == col, m[:, 0:RANK], 0.0), axis=1, keepdims=True)
    inverse = m[:, RANK : 2 * RANK] / jnp.sqrt(diag)
    out[...] = dot(inverse, s, 1, 0, lax.Precision.HIGHEST)


def make_basis(me, src, pieces, n_dp, part, din):
    groups = len(pieces)
    n_t, _, width = pieces[0].shape
    vm = pl.BlockSpec(memory_space=pltpu.VMEM)
    sm = pl.BlockSpec(memory_space=pltpu.SMEM)
    return pl.pallas_call(
        functools.partial(
            basis_kernel, n_dp=n_dp, n_t=n_t, width=width, part=part, inv_n=1.0 / n_dp, groups=groups
        ),
        in_specs=[sm, sm] + [vm] * groups,
        out_specs=vm,
        out_shape=jax.ShapeDtypeStruct((RANK, din), F32),
        scratch_shapes=[pltpu.VMEM((RANK, din), F32)],
        compiler_params=params(24),
        cost_estimate=cost(6e9, 2e6),
        name="basis",
    )(jnp.reshape(me, (1,)), src, *pieces)


def right_kernel(*refs, n_t, per, n_out, scale):
    ids, src = refs[0], refs[1]
    e_ref, b_ref, g_ref = refs[2:5]
    x_refs = refs[5 : 5 + n_t]
    outs = refs[5 + n_t : 5 + n_t + n_out]
    acc, vacc = refs[5 + n_t + n_out :]
    r, j = pl.program_id(0), pl.program_id(1)

    @pl.when((r == 0) & (j == 0))
    def _():
        acc[...] = jnp.zeros_like(acc)
        vacc[...] = jnp.zeros_like(vacc)

    bh, bl = split(b_ref[...])
    both = jnp.concatenate([bh, bl], axis=0)
    eh, el = split(e_ref[...])
    main = dot(both, eh, 1, 0)
    rest = dot(bh, el, 1, 0)
    acc[...] += main[0:RANK, :] + main[RANK:, :] + rest
    for n in range(n_t):

        @pl.when(r == n)
        def _(n=n):
            v = dot(both, x_refs[n][...], 1, 0)
            vacc[...] += v[0:RANK, :] + v[RANK:, :]

    @pl.when((r == n_t - 1) & (j == per - 1))
    def _():
        vh, vl = split(vacc[...])
        w = dot(jnp.concatenate([vh, vl], axis=0), g_ref[...], 1, 0)
        acc[...] += (w[0:RANK, :] + w[RANK:, :]) * scale
        width = acc.shape[1] // n_out
        for k in range(n_out):
            at = pl.multiple_of((ids[0] ^ k) * width, width)
            outs[k][...] = acc[:, pl.ds(at, width)]


def x_map(n, per, r, j, *_):
    return (jnp.clip((r - n) * per + j, 0, per - 1), 0)


def right_factor(me, src, error, basis_t, out_grad, xts, n_out, scale):
    part = xts[0].shape[0]
    tok, outs = out_grad.shape
    n_t = len(xts)
    blk = min(512, part)
    per = part // blk
    return pl.pallas_call(
        functools.partial(right_kernel, n_t=n_t, per=per, n_out=n_out, scale=scale),
        grid_spec=pltpu.PrefetchScalarGridSpec(
            num_scalar_prefetch=2,
            grid=(n_t, per),
            in_specs=[
                pl.BlockSpec((blk, outs), lambda r, j, ids, src: (src[r] * per + j, 0)),
                pl.BlockSpec((RANK, blk), lambda r, j, ids, src: (0, src[r] * per + j)),
                pl.BlockSpec((tok, outs), lambda r, j, ids, src: (0, 0)),
            ]
            + [pl.BlockSpec((blk, tok), functools.partial(x_map, n, per)) for n in range(n_t)],
            out_specs=[pl.BlockSpec((RANK, outs // n_out), lambda r, j, ids, src: (0, 0))] * n_out,
            scratch_shapes=[pltpu.VMEM((RANK, outs), F32), pltpu.VMEM((RANK, tok), F32)],
        ),
        out_shape=[jax.ShapeDtypeStruct((RANK, outs // n_out), F32)] * n_out,
        compiler_params=params(40),
        cost_estimate=cost(9e9, error.size * 4 + n_t * part * tok * 2),
        name="right_factor",
    )(jnp.reshape(me, (1,)), src, error, basis_t, out_grad, *xts)


def update_kernel(*refs, n_t, groups, width, inv_n, scale):
    ids, src = refs[0], refs[1]
    e_ref, b_ref, g_ref = refs[2:5]
    x_refs = refs[5 : 5 + n_t]
    q_refs = refs[5 + n_t : 5 + n_t + groups]
    out, qt_out, qs = refs[5 + n_t + groups :]
    r, j = pl.program_id(0), pl.program_id(1)

    @pl.when((r == 0) & (j == 0))
    def _():
        for k in range(groups):
            at = pl.multiple_of((ids[0] ^ k) * width, width)
            qt_out[:, pl.ds(at, width)] = q_refs[k][...] * inv_n
        high, low = split(qt_out[...])
        qs[0:RANK, :] = high
        qs[RANK : 2 * RANK, :] = low
        qs[2 * RANK : 3 * RANK, :] = high

    bh, bl = split(b_ref[...].T)
    approx = dot(jnp.concatenate([bh, bh, bl], axis=1), qs[...], 1, 0)
    base = e_ref[...] - approx
    for n in range(n_t):

        @pl.when(r == n)
        def _(n=n):
            out[...] = base + dot(x_refs[n][...], g_ref[...], 1, 0) * scale


def update_error(me, src, error, basis_t, out_grad, xts, q_pieces, n_dp, scale):
    part = xts[0].shape[0]
    tok, outs = out_grad.shape
    n_t = len(xts)
    blk = min(512, part)
    per = part // blk
    groups = len(q_pieces)
    width = outs // groups
    return pl.pallas_call(
        functools.partial(
            update_kernel, n_t=n_t, groups=groups, width=width, inv_n=1.0 / n_dp, scale=scale
        ),
        grid_spec=pltpu.PrefetchScalarGridSpec(
            num_scalar_prefetch=2,
            grid=(n_t, per),
            in_specs=[
                pl.BlockSpec((blk, outs), lambda r, j, ids, src: (src[r] * per + j, 0)),
                pl.BlockSpec((RANK, blk), lambda r, j, ids, src: (0, src[r] * per + j)),
                pl.BlockSpec((tok, outs), lambda r, j, ids, src: (0, 0)),
            ]
            + [pl.BlockSpec((blk, tok), functools.partial(x_map, n, per)) for n in range(n_t)]
            + [pl.BlockSpec((RANK, width), lambda r, j, ids, src: (0, 0))] * groups,
            out_specs=[
                pl.BlockSpec((blk, outs), lambda r, j, ids, src: (src[r] * per + j, 0)),
                pl.BlockSpec((RANK, outs), lambda r, j, ids, src: (0, 0)),
            ],
            scratch_shapes=[pltpu.VMEM((3 * RANK, outs), BF16)],
        ),
        out_shape=[
            jax.ShapeDtypeStruct(error.shape, F32),
            jax.ShapeDtypeStruct((RANK, outs), F32),
        ],
        compiler_params=params(48),
        cost_estimate=cost(9e9, error.size * 8 + n_t * part * tok * 2),
        name="update_error",
    )(jnp.reshape(me, (1,)), src, error, basis_t, out_grad, *xts, *q_pieces)


def near_kernel(ids, g_ref, gs_ref, w_ref, ws_ref, out):
    out[...] = dot(g_ref[...], w_ref[...], 1, 1) + dot(gs_ref[...], ws_ref[...], 1, 1)


def near_input_grad(me_t, g_own, g_sib, weight, w_sib):
    tok, outs = g_own.shape
    part = w_sib.shape[0]
    blk = 256
    row = pl.BlockSpec((blk, outs), lambda i, ids: (i, 0))
    return pl.pallas_call(
        near_kernel,
        grid_spec=pltpu.PrefetchScalarGridSpec(
            num_scalar_prefetch=1,
            grid=(tok // blk,),
            in_specs=[
                row,
                row,
                pl.BlockSpec((part, outs), lambda i, ids: (ids[0], 0)),
                pl.BlockSpec((part, outs), lambda i, ids: (0, 0)),
            ],
            out_specs=pl.BlockSpec((blk, part), lambda i, ids: (i, 0)),
        ),
        out_shape=jax.ShapeDtypeStruct((tok, part), F32),
        compiler_params=params(32),
        cost_estimate=cost(4 * tok * outs * part, 12e6),
        name="input_grad_near",
    )(jnp.reshape(me_t, (1,)), g_own, g_sib, weight, w_sib)


def far_kernel(*refs):
    prev, w_ref = refs[0], refs[1]
    g_refs, out = refs[2:-1], refs[-1]
    width = g_refs[0].shape[1]
    total = prev[...]
    for n, g in enumerate(g_refs):
        total = total + dot(g[...], w_ref[:, n * width : (n + 1) * width], 1, 1)
    out[...] = total


def far_input_grad(prev, w_far, gs, start):
    rows, outs = gs[0].shape
    tok, part = prev.shape
    blk = 256
    row = pl.BlockSpec((blk, outs), lambda i: (i, 0))
    to = pl.BlockSpec((blk, part), lambda i: (i + start // blk, 0))
    return pl.pallas_call(
        far_kernel,
        grid=(rows // blk,),
        in_specs=[to, pl.BlockSpec(w_far.shape, lambda i: (0, 0))] + [row] * len(gs),
        out_specs=to,
        out_shape=jax.ShapeDtypeStruct((tok, part), F32),
        input_output_aliases={0: 0},
        compiler_params=params(40),
        cost_estimate=cost(2 * len(gs) * rows * outs * part, 10e6),
        name="input_grad_far",
    )(prev, w_far, *gs)


def per_device(activations, out_grad, weight, error, q_start):
    scale = 1.0 / math.sqrt(TOK_DEV)
    n_t = lax.axis_size("tensor")
    n_dp = lax.axis_size("dp")
    chips = n_t // 2
    t = lax.axis_index("tensor").astype(jnp.int32)
    d = lax.axis_index("dp").astype(jnp.int32)
    y, c = t // 2, t % 2
    tok, part = activations.shape
    outs = out_grad.shape[1]
    din = weight.shape[0]
    error = error[0]

    def to_sibling(a):
        return lax.ppermute(a, "tensor", [(i, i ^ 1) for i in range(n_t)])

    def to_chip(a, k):
        return lax.ppermute(
            a, "tensor", [(i, ((i // 2 + k) % chips) * 2 + i % 2) for i in range(n_t)]
        )

    def to_replica(a, k):
        return lax.ppermute(a, "dp", [(i, i ^ k) for i in range(n_dp)])

    src = jnp.stack([((y - k) % chips) * 2 + (c ^ e) for k in range(chips) for e in range(2)])
    src = src.astype(jnp.int32)
    steps = range(1, chips)

    x_t = activations.T
    x_far = [to_chip(x_t, k) for k in steps]
    share = part // n_dp
    w_parts = []
    for k in steps:
        for e in range(2):
            dest = ((y + k) % chips) * 2 + (c ^ e)
            piece = lax.dynamic_slice(weight, (dest * part + d * share, 0), (share, outs))
            w_parts.append(
                lax.ppermute(
                    piece,
                    "tensor",
                    [(i, ((i // 2 + k) % chips) * 2 + ((i % 2) ^ e)) for i in range(n_t)],
                )
            )
    w_far = lax.all_gather(jnp.concatenate(w_parts, axis=1), "dp", axis=0, tiled=True)
    w_sib = to_sibling(lax.dynamic_slice(weight, ((t ^ 1) * part, 0), (part, outs)))
    n_chunk = 2
    rows = tok // n_chunk
    g_far = [
        [to_chip(out_grad[i * rows : (i + 1) * rows], k) for k in steps] for i in range(n_chunk)
    ]
    g_sib = to_sibling(out_grad)

    send, keep, y_t = local_sketch(error, q_start.T, out_grad, c, chips, part)
    got = to_sibling(send)
    y_t = y_t + to_sibling(y_t)
    summed = keep + got
    e_list = [lax.dynamic_index_in_dim(summed, y, 0, keepdims=False)]
    y_list = [y_t]
    for k in steps:
        e_list.append(
            to_chip(lax.dynamic_index_in_dim(summed, (y + k) % chips, 0, keepdims=False), k)
        )
        y_list.append(to_chip(y_t, k))
    direct = part % (n_dp * 128) == 0 and outs % (n_dp * 128) == 0
    groups = n_dp if direct else 1
    me = d if direct else jnp.zeros_like(d)

    def reduce_pieces(pieces):
        if not direct:
            return lax.psum(pieces[0], "dp")
        total = pieces[0]
        for k in range(1, n_dp):
            total = total + to_replica(pieces[k], k)
        return total

    def gather_pieces(piece):
        return [piece] + [to_replica(piece, k) for k in range(1, groups)]

    piece = reduce_pieces(sketch_rows(me, e_list, y_list, activations, groups, scale))
    stacked = jnp.stack([piece] + [to_chip(piece, k) for k in steps])
    other = to_sibling(stacked)
    stacked = jnp.stack([stacked, other], axis=1).reshape(n_t, RANK, part // groups)
    basis_t = make_basis(me, src, gather_pieces(stacked), n_dp, part, din)

    xts = [x_t, to_sibling(x_t)]
    for a in x_far:
        xts += [a, to_sibling(a)]
    piece = reduce_pieces(
        right_factor(me, src, error, basis_t, out_grad, xts, groups, scale)
    )
    new_error, q_t = update_error(
        me, src, error, basis_t, out_grad, xts, gather_pieces(piece), n_dp, scale
    )

    grad = near_input_grad(t, out_grad, g_sib, weight, w_sib)
    for i in range(n_chunk):
        gs = []
        for a in g_far[i]:
            gs += [a, to_sibling(a)]
        grad = far_input_grad(grad, w_far, gs, i * rows)
    return (grad, new_error[None], q_t.T)


def solution(mesh):
    placed = (
        P("dp", "tensor"),
        P("dp", "tensor"),
        P(None, "tensor"),
        P("dp", None, "tensor"),
        P("tensor", None),
    )
    return jax.shard_map(
        per_device,
        mesh=mesh,
        in_specs=placed,
        out_specs=(P("dp", "tensor"), P("dp", None, "tensor"), P("tensor", None)),
        check_vma=False,
    )
```

time: 470 us -> 255 us (0.54)
  waiting for transfers between devices: 352 us -> 92.9 us
  matrix products: 90.1 us -> 0 us
  Pallas kernels: 0 us -> 68.9 us
  starting transfers between devices: 0.56 us -> 52.1 us
  local copies, waits for them, and re-layouts: 5.43 us -> 24.9 us
  other arithmetic: 7.6 us -> 0.98 us
    psum x2 -> x0, waiting for transfers between devices: 182 us -> none  [the longest x1 128 us: per_device(): sketch = lax.psum(local_sketch, ('dp', 'tensor')) / replicas]
    reduce_scatter x1 -> x0, waiting for transfers between devices: 107 us -> none  [per_device(): lax.psum_scatter(lax.dot_general(weight, out_grad, (((1,), (1,)), ((), ()...]
    ppermute x0 -> x45, waiting for transfers between devices: none -> 92.9 us  [the longest x28 42.2 us: to_replica(): return lax.ppermute(a, 'dp', [(i, i ^ k) for i in range(n_dp)])]
    dot_general x6 -> x0, matrix products: 88.4 us -> none  [the longest x1 19.9 us: per_device(): approx = jnp.dot(basis, q_factor.T, precision=lax.Precision.HIGHEST)]
    pallas_call x0 -> x8, Pallas kernels: none -> 68.9 us  [the longest x1 22.9 us: update_error(): pl.pallas_call(functools.partial(update_kernel, n_t=n_t, groups=groups, w...]
    all_gather x1, waiting for transfers between devices: 62.6 us -> 0.01 us  [per_device(): lax.all_gather(jnp.concatenate(w_parts, axis=1), 'dp', axis=0, tiled=True)]
    ppermute x0 -> x45, starting transfers between devices: none -> 52 us  [the longest x28 40.4 us: to_replica(): return lax.ppermute(a, 'dp', [(i, i ^ k) for i in range(n_dp)])]
    unnamed x7 -> x29, local copies, waits for them, and re-layouts: 5.36 us -> 19.1 us
  transfers between devices with their start and end apart: 4 -> 46, of which waited for: 4 -> 27; matrix products, arithmetic and copies ran while one was open for 8% -> 4% of each run, Pallas kernels for 0% -> 25%
where the time goes in v1:
time: 255 us; the launch traced here: 254 us
  waiting for transfers between devices  92.9 us (36%)
  Pallas kernels  68.9 us (27%)
  starting transfers between devices  52.1 us (20%)
  local copies, waits for them, and re-layouts  24.9 us (10%)
  between operations  14.3 us (6%)
    ppermute x28, waiting for transfers between devices, to_replica(): return lax.ppermute(a, 'dp', [(i, i ^ k) for i in range(n_dp)])  42.2 us
    ppermute x28, starting transfers between devices, to_replica(): return lax.ppermute(a, 'dp', [(i, i ^ k) for i in range(n_dp)])  40.4 us
    ppermute x6, waiting for transfers between devices, to_chip(): lax.ppermute(a, 'tensor', [(i, (i // 2 + k) % chips * 2 + i % 2) for i in...  37.4 us
    pallas_call x1, Pallas kernels, update_error(): pl.pallas_call(functools.partial(update_kernel, n_t=n_t, groups=groups, w...  22.9 us
    unnamed x29, local copies, waits for them, and re-layouts  19.1 us
    pallas_call x1, Pallas kernels, right_factor(): pl.pallas_call(functools.partial(right_kernel, n_t=n_t, per=per, n_out=n_...  14.4 us
    ppermute x2, waiting for transfers between devices, per_device(): lax.ppermute(piece, 'tensor', [(i, (i // 2 + k) % chips * 2 + (i % 2 ^ e)...  11.2 us
    pallas_call x2, Pallas kernels, far_input_grad(): pl.pallas_call(far_kernel, grid=(rows // blk,), in_specs=[to, pl.BlockSpe...  9.7 us
  transfers between devices with their start and end apart: 46, of which 27 were waited for; matrix products, arithmetic and copies ran while one was open for 4% of the time, Pallas kernels for 25%

profile of v1, /device:TPU:0, one launch (start us, length us, event | category | flops | bytes accessed | tf_op | source)
XLA Modules:
  0.0 254.0 jit_solution(2371173385622509857)
XLA Ops:
  8.3 3.0 %collective-permute-start.2 = (bf16[128,1024]{1,0:T(8,128)(2,1)S(1)}, bf16[128,1024]{1,0:T(8,128)(2,1)S(1)}, u32[]{:S(2)}, u32[]{:S(2)}) collective-permute-start(bf16[128,1024]{1,0:T(8,128)(2,1)S(1)} %get-tuple-element.45), channel_id=1, source_target_pairs={{0,2},{1,3},{2,0},{3,1},{4,6},{5,7},{6,4},{7,5},{8,10},{9,11},{10,... | collective-permute-start | bytes 786440 | tf_op jit(solution)/shard_map/ppermute | solution.py:414
  11.4 7.1 %collective-permute-done.2 = bf16[128,1024]{1,0:T(8,128)(2,1)S(1)} collective-permute-done((bf16[128,1024]{1,0:T(8,128)(2,1)S(1)}, bf16[128,1024]{1,0:T(8,128)(2,1)S(1)}, u32[]{:S(2)}, u32[]{:S(2)}) %collective-permute-start.2) | collective-permute-done | bytes 262176 | tf_op jit(solution)/shard_map/ppermute | solution.py:414
  18.5 4.0 %collective-permute-done.3 = bf16[128,1024]{1,0:T(8,128)(2,1)S(1)} collective-permute-done((bf16[128,1024]{1,0:T(8,128)(2,1)S(1)}, bf16[128,1024]{1,0:T(8,128)(2,1)S(1)}, u32[]{:S(2)}, u32[]{:S(2)}) %collective-permute-start.3) | collective-permute-done | bytes 262176 | tf_op jit(solution)/shard_map/ppermute | solution.py:414
  23.4 4.1 %copy.11 = bf16[1024,1024]{0,1:T(8,128)(2,1)} copy(bf16[1024,1024]{1,0:T(8,128)(2,1)} %refs_5_.1) | data formatting | bytes 4194304 | tf_op args[0]
  28.9 6.3 %copy-done.7 = f32[1,4096,1024]{2,1,0:T(8,128)S(1)} copy-done((f32[1,4096,1024]{2,1,0:T(8,128)S(1)}, f32[1,4096,1024]{2,1,0:T(8,128)}, u32[]{:S(2)}) %copy-start.7) | copy-done | bytes 16777240
  35.2 8.1 %error_sketch.1 = (f32[2,32,1024]{2,1,0:T(8,128)S(1)}, f32[2,32,1024]{2,1,0:T(8,128)S(1)}, f32[32,1024]{1,0:T(8,128)S(1)}) custom-call(s32[1]{0:T(128)} %bitcast.7.ids, f32[4096,1024]{1,0:T(8,128)S(1)} %bitcast.34, f32[32,1024]{1,0:T(8,128)S(1)} %bitcast.35, bf16[1024,1024]{1,0:T(8,128)(2,1)S(1)} %copy-done.1), custom_call_target="tpu_custom_call" | custom-call | flops 6000000000 | bytes 16777216 | tf_op jit(solution)/shard_map/error_sketch/pallas_call | solution.py:79
  45.7 30.6 %collective-permute-done.29.refs_7_ = bf16[1024,1024]{1,0:T(8,128)(2,1)} collective-permute-done((bf16[1024,1024]{1,0:T(8,128)(2,1)}, bf16[1024,1024]{1,0:T(8,128)(2,1)}, u32[]{:S(2)}, u32[]{:S(2)}) %collective-permute-start.29) | collective-permute-done | bytes 2097184 | tf_op jit(solution)/shard_map/ppermute | solution.py:394
  78.6 3.6 %collective-permute-done.9.refs_2_ = f32[32,1024]{1,0:T(8,128)S(1)} collective-permute-done((f32[32,1024]{1,0:T(8,128)S(1)}, f32[32,1024]{1,0:T(8,128)S(1)}, u32[]{:S(2)}, u32[]{:S(2)}) %collective-permute-start.9) | collective-permute-done | bytes 131104 | tf_op jit(solution)/shard_map/ppermute | solution.py:394
  95.8 3.3 %collective-permute-start.18 = (f32[32,128]{1,0:T(8,128)S(1)}, f32[32,128]{1,0:T(8,128)S(1)}, u32[]{:S(2)}, u32[]{:S(2)}) collective-permute-start(f32[32,128]{1,0:T(8,128)S(1)} %get-tuple-element.34), channel_id=1, source_target_pairs={{0,28},{4,24},{8,20},{12,16},{16,12},{20,8},{24,4},{28,0},{1,29},{... | collective-permute-start | bytes 49160 | tf_op jit(solution)/shard_map/ppermute | solution.py:399
  99.1 3.1 %collective-permute-done.18 = f32[32,128]{1,0:T(8,128)S(1)} collective-permute-done((f32[32,128]{1,0:T(8,128)S(1)}, f32[32,128]{1,0:T(8,128)S(1)}, u32[]{:S(2)}, u32[]{:S(2)}) %collective-permute-start.18) | collective-permute-done | bytes 16416 | tf_op jit(solution)/shard_map/ppermute | solution.py:399
  107.3 3.4 %collective-permute-start.27 = (f32[4,32,128]{2,1,0:T(8,128)S(1)}, f32[4,32,128]{2,1,0:T(8,128)S(1)}, u32[]{:S(2)}, u32[]{:S(2)}) collective-permute-start(f32[4,32,128]{2,1,0:T(8,128)S(1)} %bitcast.24), channel_id=1, source_target_pairs={{0,28},{4,24},{8,20},{12,16},{16,12},{20,8},{24,4},{28,0},{1,29},{... | collective-permute-start | bytes 196616 | tf_op jit(solution)/shard_map/ppermute | solution.py:399
  118.7 3.1 %constant_dynamic-slice_fusion.2 = bf16[1024,1024]{1,0:T(8,128)(2,1)} fusion(bf16[4096,1024]{1,0:T(8,128)(2,1)} %w_ref.1, s32[]{:T(128)S(6)} %select_n.47), kind=kLoop, calls=%fused_computation.9 | loop fusion | bytes 4194308 | tf_op jit(solution)/shard_map/dynamic_slice | solution.py:421
  133.4 5.1 %basis.1.refs_3_ = f32[32,4096]{1,0:T(8,128)S(1)} custom-call(s32[1]{0:T(128)} %bitcast.1.refs_0_, s32[4]{0:T(128)S(1)} %pad_add_fusion.refs_1_, f32[4,32,128]{2,1,0:T(8,128)S(1)} %bitcast.31, f32[4,32,128]{2,1,0:T(8,128)S(1)} %collective-permute-done.21.refs_3_, f32[4,32,128]{2,1,0:T(8,128)S(1)} %copy-done.10, ...), custom_call_target="tpu_custom_call" | custom-call | flops 6000000000 | bytes 2000000 | tf_op jit(solution)/shard_map/basis/pallas_call | solution.py:171
  139.9 14.4 %right_factor.1 = (f32[32,128]{1,0:T(8,128)S(1)}, f32[32,128]{1,0:T(8,128)S(1)}, f32[32,128]{1,0:T(8,128)S(1)}, f32[32,128]{1,0:T(8,128)S(1)}, f32[32,128]{1,0:T...) custom-call(s32[1]{0:T(128)} %bitcast.1.refs_0_, s32[4]{0:T(128)S(1)} %pad_add_fusion.refs_1_, ...), custom_call_target="tpu_custom_call" | custom-call | flops 8999999488 | bytes 25165824 | tf_op jit(solution)/shard_map/right_factor/pallas_call | solution.py:232
  158.3 3.7 %collective-permute-done.32 = f32[32,128]{1,0:T(8,128)S(1)} collective-permute-done((f32[32,128]{1,0:T(8,128)S(1)}, f32[32,128]{1,0:T(8,128)S(1)}, u32[]{:S(2)}, u32[]{:S(2)}) %collective-permute-start.32) | collective-permute-done | bytes 16416 | tf_op jit(solution)/shard_map/ppermute | solution.py:399
  163.0 3.6 %collective-permute-done.33 = f32[32,128]{1,0:T(8,128)S(1)} collective-permute-done((f32[32,128]{1,0:T(8,128)S(1)}, f32[32,128]{1,0:T(8,128)S(1)}, u32[]{:S(2)}, u32[]{:S(2)}) %collective-permute-start.33) | collective-permute-done | bytes 16416 | tf_op jit(solution)/shard_map/ppermute | solution.py:399
  167.1 4.1 %collective-permute-done.34 = f32[32,128]{1,0:T(8,128)S(1)} collective-permute-done((f32[32,128]{1,0:T(8,128)S(1)}, f32[32,128]{1,0:T(8,128)S(1)}, u32[]{:S(2)}, u32[]{:S(2)}) %collective-permute-start.34) | collective-permute-done | bytes 16416 | tf_op jit(solution)/shard_map/ppermute | solution.py:399
  172.6 4.2 %collective-permute-done.35 = f32[32,128]{1,0:T(8,128)S(1)} collective-permute-done((f32[32,128]{1,0:T(8,128)S(1)}, f32[32,128]{1,0:T(8,128)S(1)}, u32[]{:S(2)}, u32[]{:S(2)}) %collective-permute-start.35) | collective-permute-done | bytes 16416 | tf_op jit(solution)/shard_map/ppermute | solution.py:399
  178.4 3.9 %collective-permute-done.36 = f32[32,128]{1,0:T(8,128)S(1)} collective-permute-done((f32[32,128]{1,0:T(8,128)S(1)}, f32[32,128]{1,0:T(8,128)S(1)}, u32[]{:S(2)}, u32[]{:S(2)}) %collective-permute-start.36) | collective-permute-done | bytes 16416 | tf_op jit(solution)/shard_map/ppermute | solution.py:399
  185.2 3.6 %collective-permute-done.37 = f32[32,128]{1,0:T(8,128)S(1)} collective-permute-done((f32[32,128]{1,0:T(8,128)S(1)}, f32[32,128]{1,0:T(8,128)S(1)}, u32[]{:S(2)}, u32[]{:S(2)}) %collective-permute-start.37) | collective-permute-done | bytes 16416 | tf_op jit(solution)/shard_map/ppermute | solution.py:399
  200.7 8.1 %input_grad_near.1.refs_0_ = f32[1024,1024]{1,0:T(8,128)} custom-call(s32[1]{0:T(128)} %bitcast.ids, bf16[1024,1024]{1,0:T(8,128)(2,1)S(1)} %copy-done.1, bf16[1024,1024]{1,0:T(8,128)(2,1)} %collective-permute-done.gs_ref, bf16[4096,1024]{1,0:T(8,128)(2,1)S(1)} %bitcast.23, bf16[1024,1024]{1,0:T(8,128)(2,1)} %collective-permute-done.1.ws_ref), custom_call_target="tpu_custom_call" | custom-call | flops 4294967296 | bytes 12000000 | tf_op jit(solution)/shard_map/input_grad_near/pallas_call | solution.py:328
  208.8 22.9 %update_error.1 = (f32[4096,1024]{1,0:T(8,128)}, f32[32,1024]{1,0:T(8,128)}) custom-call(s32[1]{0:T(128)} %bitcast.1.refs_0_, s32[4]{0:T(128)S(1)} %pad_add_fusion.refs_1_, f32[4096,1024]{1,0:T(8,128)} %bitcast.33, f32[32,4096]{1,0:T(8,128)S(1)} %basis.1.refs_3_, bf16[1024,1024]{1,0:T(8,128)(2,1)S(1)} %copy-done.1, bf16[1024,1024]{1,0:T(8,128)(2,1)} %bitcast.16.refs_5_, ...), custom_call_target="tpu_custom_call" | custom-call | flops 8999999488 | bytes 41943040 | tf_op jit(solution)/shard_map/update_error/pallas_call | solution.py:289
  237.4 4.8 %input_grad_far.2.refs_0_ = f32[1024,1024]{1,0:T(8,128)} custom-call(f32[1024,1024]{1,0:T(8,128)} %input_grad_near.1.refs_0_, bf16[1024,2048]{1,0:T(8,128)(2,1)S(1)} %copy-done, bf16[512,1024]{1,0:T(8,128)(2,1)S(1)} %copy-done.4, bf16[512,1024]{1,0:T(8,128)(2,1)S(1)} %copy-done.6), custom_call_target="tpu_custom_call", output_to_operand_aliasing={{}: (0, {})} | custom-call | flops 2147483648 | bytes 10000000 | tf_op jit(solution)/shard_map/input_grad_far/pallas_call | solution.py:364
  242.2 4.9 %input_grad_far.3 = f32[1024,1024]{1,0:T(8,128)} custom-call(f32[1024,1024]{1,0:T(8,128)} %input_grad_far.2.refs_0_, bf16[1024,2048]{1,0:T(8,128)(2,1)S(1)} %copy-done, bf16[512,1024]{1,0:T(8,128)(2,1)S(1)} %collective-permute-done.6.refs_2_, bf16[512,1024]{1,0:T(8,128)(2,1)} %collective-permute-done.7.refs_3_), custom_call_target="tpu_custom_call", output_to_operand_aliasing={{}: (0, {})} | custom-call | flops 2147483648 | bytes 10000000 | tf_op jit(solution)/shard_map/input_grad_far/pallas_call | solution.py:364
  (120 shorter events, 76.6 us)
Async XLA Ops:
  7.2 225.6 %all-gather.2.cloned.1.call-start = ((), (), s32[]{:S(2)}) async-start(), calls=%async_computation | async-start | bytes 4718592 | tf_op jit(solution)/shard_map/all_gather | solution.py:420
  8.3 10.2 %collective-permute-start.2 = (bf16[128,1024]{1,0:T(8,128)(2,1)S(1)}, bf16[128,1024]{1,0:T(8,128)(2,1)S(1)}, u32[]{:S(2)}, u32[]{:S(2)}) collective-permute-start(bf16[128,1024]{1,0:T(8,128)(2,1)S(1)} %get-tuple-element.45), channel_id=1, source_target_pairs={{0,2},{1,3},{2,0},{3,1},{4,6},{5,7},{6,4},{7,5},{8,10},{9,11},{10,... | collective-permute-start | bytes 786440 | tf_op jit(solution)/shard_map/ppermute | solution.py:414
  11.4 11.2 %collective-permute-start.3 = (bf16[128,1024]{1,0:T(8,128)(2,1)S(1)}, bf16[128,1024]{1,0:T(8,128)(2,1)S(1)}, u32[]{:S(2)}, u32[]{:S(2)}) collective-permute-start(bf16[128,1024]{1,0:T(8,128)(2,1)S(1)} %get-tuple-element.46), channel_id=1, source_target_pairs={{0,3},{1,2},{2,1},{3,0},{4,7},{5,6},{6,5},{7,4},{8,11},{9,10},{10,... | collective-permute-start | bytes 786440 | tf_op jit(solution)/shard_map/ppermute | solution.py:414
  27.5 48.7 %collective-permute-start.29 = (bf16[1024,1024]{1,0:T(8,128)(2,1)}, bf16[1024,1024]{1,0:T(8,128)(2,1)}, u32[]{:S(2)}, u32[]{:S(2)}) collective-permute-start(bf16[1024,1024]{1,0:T(8,128)(2,1)} %bitcast.16.refs_5_), channel_id=1, source_target_pairs={{0,2},{1,3},{2,0},{3,1},{4,6},{5,7},{6,4},{7,5},{8,10},{9,11},{10,... | collective-permute-start | bytes 6291464 | tf_op jit(solution)/shard_map/ppermute | solution.py:394
  44.1 94.4 %collective-permute-start.28 = (bf16[1024,1024]{1,0:T(8,128)(2,1)}, bf16[1024,1024]{1,0:T(8,128)(2,1)}, u32[]{:S(2)}, u32[]{:S(2)}) collective-permute-start(bf16[1024,1024]{1,0:T(8,128)(2,1)} %bitcast.16.refs_5_), channel_id=1, source_target_pairs={{0,1},{1,0},{2,3},{3,2},{4,5},{5,4},{6,7},{7,6},{8,9},{9,8},{10,11... | collective-permute-start | bytes 6291464 | tf_op jit(solution)/shard_map/ppermute | solution.py:391
  45.4 33.2 %collective-permute-start.11 = (f32[32,1024]{1,0:T(8,128)S(1)}, f32[32,1024]{1,0:T(8,128)S(1)}, u32[]{:S(2)}, u32[]{:S(2)}) collective-permute-start(f32[32,1024]{1,0:T(8,128)S(1)} %add.131.refs_3_), channel_id=1, source_target_pairs={{0,2},{1,3},{2,0},{3,1},{4,6},{5,7},{6,4},{7,5},{8,10},{9,11},{10,... | collective-permute-start | bytes 393224 | tf_op jit(solution)/shard_map/ppermute | solution.py:394
  76.3 63.7 %collective-permute-start.30 = (bf16[1024,1024]{1,0:T(8,128)(2,1)}, bf16[1024,1024]{1,0:T(8,128)(2,1)}, u32[]{:S(2)}, u32[]{:S(2)}) collective-permute-start(bf16[1024,1024]{1,0:T(8,128)(2,1)} %collective-permute-done.29.refs_7_), channel_id=1, source_target_pairs={{0,1},{1,0},{2,3},{3,2},{4,5},{5,4},{6,7},{7,6},{8,9},{9,8},{10,11... | collective-permute-start | bytes 6291464 | tf_op jit(solution)/shard_map/ppermute | solution.py:391
  88.2 7.6 %collective-permute-start.15 = (f32[32,128]{1,0:T(8,128)S(1)}, f32[32,128]{1,0:T(8,128)S(1)}, u32[]{:S(2)}, u32[]{:S(2)}) collective-permute-start(f32[32,128]{1,0:T(8,128)S(1)} %get-tuple-element.31), channel_id=1, source_target_pairs={{0,16},{4,20},{8,24},{12,28},{16,0},{20,4},{24,8},{28,12},{1,17},{... | collective-permute-start | bytes 49160 | tf_op jit(solution)/shard_map/ppermute | solution.py:399
  91.2 7.9 %collective-permute-start.16 = (f32[32,128]{1,0:T(8,128)S(1)}, f32[32,128]{1,0:T(8,128)S(1)}, u32[]{:S(2)}, u32[]{:S(2)}) collective-permute-start(f32[32,128]{1,0:T(8,128)S(1)} %get-tuple-element.32), channel_id=1, source_target_pairs={{0,20},{4,16},{8,28},{12,24},{16,4},{20,0},{24,12},{28,8},{1,21},{... | collective-permute-start | bytes 49160 | tf_op jit(solution)/shard_map/ppermute | solution.py:399
  95.8 6.4 %collective-permute-start.18 = (f32[32,128]{1,0:T(8,128)S(1)}, f32[32,128]{1,0:T(8,128)S(1)}, u32[]{:S(2)}, u32[]{:S(2)}) collective-permute-start(f32[32,128]{1,0:T(8,128)S(1)} %get-tuple-element.34), channel_id=1, source_target_pairs={{0,28},{4,24},{8,20},{12,16},{16,12},{20,8},{24,4},{28,0},{1,29},{... | collective-permute-start | bytes 49160 | tf_op jit(solution)/shard_map/ppermute | solution.py:399
  107.3 7.0 %collective-permute-start.27 = (f32[4,32,128]{2,1,0:T(8,128)S(1)}, f32[4,32,128]{2,1,0:T(8,128)S(1)}, u32[]{:S(2)}, u32[]{:S(2)}) collective-permute-start(f32[4,32,128]{2,1,0:T(8,128)S(1)} %bitcast.24), channel_id=1, source_target_pairs={{0,28},{4,24},{8,20},{12,16},{16,12},{20,8},{24,4},{28,0},{1,29},{... | collective-permute-start | bytes 196616 | tf_op jit(solution)/shard_map/ppermute | solution.py:399
  110.6 6.9 %collective-permute-start.26 = (f32[4,32,128]{2,1,0:T(8,128)S(1)}, f32[4,32,128]{2,1,0:T(8,128)S(1)}, u32[]{:S(2)}, u32[]{:S(2)}) collective-permute-start(f32[4,32,128]{2,1,0:T(8,128)S(1)} %bitcast.25), channel_id=1, source_target_pairs={{0,24},{4,28},{8,16},{12,20},{16,8},{20,12},{24,0},{28,4},{1,25},{... | collective-permute-start | bytes 196616 | tf_op jit(solution)/shard_map/ppermute | solution.py:399
  111.9 9.9 %collective-permute-start.25 = (f32[4,32,128]{2,1,0:T(8,128)S(1)}, f32[4,32,128]{2,1,0:T(8,128)S(1)}, u32[]{:S(2)}, u32[]{:S(2)}) collective-permute-start(f32[4,32,128]{2,1,0:T(8,128)S(1)} %bitcast.26), channel_id=1, source_target_pairs={{0,20},{4,16},{8,28},{12,24},{16,4},{20,0},{24,12},{28,8},{1,21},{... | collective-permute-start | bytes 196616 | tf_op jit(solution)/shard_map/ppermute | solution.py:399
  114.3 7.7 %collective-permute-start.24 = (f32[4,32,128]{2,1,0:T(8,128)S(1)}, f32[4,32,128]{2,1,0:T(8,128)S(1)}, u32[]{:S(2)}, u32[]{:S(2)}) collective-permute-start(f32[4,32,128]{2,1,0:T(8,128)S(1)} %bitcast.27), channel_id=1, source_target_pairs={{0,16},{4,20},{8,24},{12,28},{16,0},{20,4},{24,8},{28,12},{1,17},{... | collective-permute-start | bytes 196616 | tf_op jit(solution)/shard_map/ppermute | solution.py:399
  121.8 74.7 %collective-permute-start = (bf16[1024,1024]{1,0:T(8,128)(2,1)S(1)}, bf16[1024,1024]{1,0:T(8,128)(2,1)}, u32[]{:S(2)}, u32[]{:S(2)}) collective-permute-start(bf16[1024,1024]{1,0:T(8,128)(2,1)S(1)} %copy-done.1), channel_id=1, source_target_pairs={{0,1},{1,0},{2,3},{3,2},{4,5},{5,4},{6,7},{7,6},{8,9},{9,8},{10,11... | collective-permute-start | bytes 6291464 | tf_op jit(solution)/shard_map/ppermute | solution.py:391
  122.0 71.6 %collective-permute-start.1 = (bf16[1024,1024]{1,0:T(8,128)(2,1)}, bf16[1024,1024]{1,0:T(8,128)(2,1)}, u32[]{:S(2)}, u32[]{:S(2)}) collective-permute-start(bf16[1024,1024]{1,0:T(8,128)(2,1)} %constant_dynamic-slice_fusion.2), channel_id=1, source_target_pairs={{0,1},{1,0},{2,3},{3,2},{4,5},{5,4},{6,7},{7,6},{8,9},{9,8},{10,11... | collective-permute-start | bytes 6291464 | tf_op jit(solution)/shard_map/ppermute | solution.py:391
  131.8 59.9 %collective-permute-start.6 = (bf16[512,1024]{1,0:T(8,128)(2,1)}, bf16[512,1024]{1,0:T(8,128)(2,1)S(1)}, u32[]{:S(2)}, u32[]{:S(2)}) collective-permute-start(bf16[512,1024]{1,0:T(8,128)(2,1)} %get-tuple-element.47), channel_id=1, source_target_pairs={{0,2},{1,3},{2,0},{3,1},{4,6},{5,7},{6,4},{7,5},{8,10},{9,11},{10,... | collective-permute-start | bytes 3145736 | tf_op jit(solution)/shard_map/ppermute | solution.py:394
  138.6 55.0 %collective-permute-start.4 = (bf16[512,1024]{1,0:T(8,128)(2,1)S(1)}, bf16[512,1024]{1,0:T(8,128)(2,1)S(1)}, u32[]{:S(2)}, u32[]{:S(2)}) collective-permute-start(bf16[512,1024]{1,0:T(8,128)(2,1)S(1)} %copy-done.11), channel_id=1, source_target_pairs={{0,2},{1,3},{2,0},{3,1},{4,6},{5,7},{6,4},{7,5},{8,10},{9,11},{10,... | collective-permute-start | bytes 3145736 | tf_op jit(solution)/shard_map/ppermute | solution.py:394
  188.8 7.7 %collective-permute-start.44 = (f32[32,128]{1,0:T(8,128)S(1)}, f32[32,128]{1,0:T(8,128)S(1)}, u32[]{:S(2)}, u32[]{:S(2)}) collective-permute-start(f32[32,128]{1,0:T(8,128)S(1)} %add_add_fusion.refs_9_), channel_id=1, source_target_pairs={{0,28},{4,24},{8,20},{12,16},{16,12},{20,8},{24,4},{28,0},{1,29},{... | collective-permute-start | bytes 49160 | tf_op jit(solution)/shard_map/ppermute | solution.py:399
  196.5 45.7 %collective-permute-start.7 = (bf16[512,1024]{1,0:T(8,128)(2,1)S(1)}, bf16[512,1024]{1,0:T(8,128)(2,1)}, u32[]{:S(2)}, u32[]{:S(2)}) collective-permute-start(bf16[512,1024]{1,0:T(8,128)(2,1)S(1)} %collective-permute-done.6.refs_2_), channel_id=1, source_target_pairs={{0,1},{1,0},{2,3},{3,2},{4,5},{5,4},{6,7},{7,6},{8,9},{9,8},{10,11... | collective-permute-start | bytes 3145736 | tf_op jit(solution)/shard_map/ppermute | solution.py:391
  196.5 35.3 %collective-permute-start.5 = (bf16[512,1024]{1,0:T(8,128)(2,1)S(1)}, bf16[512,1024]{1,0:T(8,128)(2,1)S(1)}, u32[]{:S(2)}, u32[]{:S(2)}) collective-permute-start(bf16[512,1024]{1,0:T(8,128)(2,1)S(1)} %collective-permute-done.4.refs_2_), channel_id=1, source_target_pairs={{0,1},{1,0},{2,3},{3,2},{4,5},{5,4},{6,7},{7,6},{8,9},{9,8},{10,11... | collective-permute-start | bytes 3145736 | tf_op jit(solution)/shard_map/ppermute | solution.py:391
  197.2 11.6 %collective-permute-start.40 = (f32[32,128]{1,0:T(8,128)S(1)}, f32[32,128]{1,0:T(8,128)S(1)}, u32[]{:S(2)}, u32[]{:S(2)}) collective-permute-start(f32[32,128]{1,0:T(8,128)S(1)} %add_add_fusion.refs_9_), channel_id=1, source_target_pairs={{0,12},{4,8},{8,4},{12,0},{16,28},{20,24},{24,20},{28,16},{1,13},{... | collective-permute-start | bytes 49160 | tf_op jit(solution)/shard_map/ppermute | solution.py:399
  199.1 9.7 %collective-permute-start.39 = (f32[32,128]{1,0:T(8,128)S(1)}, f32[32,128]{1,0:T(8,128)S(1)}, u32[]{:S(2)}, u32[]{:S(2)}) collective-permute-start(f32[32,128]{1,0:T(8,128)S(1)} %add_add_fusion.refs_9_), channel_id=1, source_target_pairs={{0,8},{4,12},{8,0},{12,4},{16,24},{20,28},{24,16},{28,20},{1,9},{5... | collective-permute-start | bytes 49160 | tf_op jit(solution)/shard_map/ppermute | solution.py:399
  200.0 8.9 %collective-permute-start.38 = (f32[32,128]{1,0:T(8,128)S(1)}, f32[32,128]{1,0:T(8,128)S(1)}, u32[]{:S(2)}, u32[]{:S(2)}) collective-permute-start(f32[32,128]{1,0:T(8,128)S(1)} %add_add_fusion.refs_9_), channel_id=1, source_target_pairs={{0,4},{4,0},{8,12},{12,8},{16,20},{20,16},{24,28},{28,24},{1,5},{5... | collective-permute-start | bytes 49160 | tf_op jit(solution)/shard_map/ppermute | solution.py:399
  (36 other events, 271.3 us)
Sparse Core Ops, SparseCore 0:
  23.5 77.8 all-gather.1

commit v2 on v1

v2 whole, which is shorter than its diff:
```python
import functools
import math

import jax
import jax.numpy as jnp
from jax import lax
from jax.experimental import pallas as pl
from jax.experimental.pallas import tpu as pltpu
from jax.sharding import PartitionSpec as P

TOK_DEV = 1024
RANK = 32
MIB = 1 << 20
F32 = jnp.float32
BF16 = jnp.bfloat16


def dot(a, b, ca, cb, precision=None):
    return lax.dot_general(
        a, b, (((ca,), (cb,)), ((), ())), precision=precision, preferred_element_type=F32
    )


def split(a):
    high = a.astype(BF16)
    return high, (a - high.astype(F32)).astype(BF16)


def params(mib):
    return pltpu.CompilerParams(vmem_limit_bytes=mib * MIB)


def cost(flops, nbytes):
    return pl.CostEstimate(flops=int(flops / 16), bytes_accessed=int(nbytes / 16), transcendentals=0)


def project_kernel(g_ref, qt_ref, y_ref):
    both = dot(jnp.concatenate(split(qt_ref[...]), axis=0), g_ref[...], 1, 1)
    y_ref[...] = both[0:RANK, :] + both[RANK:, :]


def project(out_grad, q_t):
    vm = pl.BlockSpec(memory_space=pltpu.VMEM)
    return pl.pallas_call(
        project_kernel,
        in_specs=[vm, vm],
        out_specs=vm,
        out_shape=jax.ShapeDtypeStruct((RANK, out_grad.shape[0]), F32),
        compiler_params=params(24),
        cost_estimate=cost(1e9, 2e6),
        name="project",
    )(out_grad, q_t)


def sketch_kernel(e_ref, qt_ref, s_ref, qs_ref, *, width):
    @pl.when((pl.program_id(0) == 0) & (pl.program_id(1) == 0))
    def _():
        high, low = split(qt_ref[...])
        qs_ref[0:RANK, :] = high
        qs_ref[RANK : 2 * RANK, :] = low

    high, low = split(e_ref[...])
    main = dot(high, qs_ref[...], 1, 1)
    rest = dot(low, qs_ref[0:RANK, :], 1, 1)
    rows = (main[:, 0:RANK] + main[:, RANK : 2 * RANK] + rest).T
    for k in range(s_ref.shape[0]):
        s_ref[k, 0] = rows[:, k * width : (k + 1) * width]


def local_sketch(error, q_t, n_dp, n_t, part):
    blk = min(512, part)
    per = part // blk
    width = part // n_dp
    outs = error.shape[1]
    return pl.pallas_call(
        functools.partial(sketch_kernel, width=width),
        grid=(n_t, per),
        in_specs=[
            pl.BlockSpec((blk, outs), lambda s, j: (s * per + j, 0)),
            pl.BlockSpec((RANK, outs), lambda s, j: (0, 0)),
        ],
        out_specs=pl.BlockSpec((n_dp // per, 1, RANK, width), lambda s, j: (j, s, 0, 0)),
        out_shape=jax.ShapeDtypeStruct((n_dp, n_t, RANK, width), F32),
        scratch_shapes=[pltpu.VMEM((2 * RANK, outs), BF16)],
        compiler_params=params(48),
        cost_estimate=cost(6e9, error.size * 4),
        name="error_sketch",
    )(error, q_t)


def sketch_rows_kernel(*refs, scale, width):
    s_ref, x_ref = refs[1], refs[2]
    y_refs, out = refs[3:-1], refs[-1]
    y = y_refs[0][...]
    for r in y_refs[1:]:
        y = y + r[...]
    both = dot(jnp.concatenate(split(y), axis=0), x_ref[...], 1, 0)
    total = (both[0:RANK, :] + both[RANK:, :]) * scale
    for k in range(out.shape[0]):
        out[k, 0] = s_ref[k, 0] + total[:, k * width : (k + 1) * width]


def sketch_rows(t, blocks, acts, y_list, scale):
    tok, part = acts.shape
    n_dp, n_t, _, width = blocks.shape
    own = pl.BlockSpec((n_dp, 1, RANK, width), lambda i, ids: (0, ids[0], 0, 0))
    whole = lambda i, ids: (0, 0)
    return pl.pallas_call(
        functools.partial(sketch_rows_kernel, scale=scale, width=width),
        grid_spec=pltpu.PrefetchScalarGridSpec(
            num_scalar_prefetch=1,
            grid=(1,),
            in_specs=[own, pl.BlockSpec((tok, part), whole)]
            + [pl.BlockSpec((RANK, tok), whole)] * len(y_list),
            out_specs=own,
        ),
        out_shape=jax.ShapeDtypeStruct(blocks.shape, F32),
        input_output_aliases={1: 0},
        compiler_params=params(24),
        cost_estimate=cost(1e9, 3e6),
        name="sketch_rows",
    )(jnp.reshape(t, (1,)), blocks, acts, *y_list)


def basis_kernel(pieces, out, sk, *, n_dp, n_t, width, part):
    for s in range(n_t):
        for k in range(n_dp):
            at = s * part + k * width
            sk[:, at : at + width] = pieces[k * n_t + s] * (1.0 / n_dp)
    s = sk[...]
    gram = dot(s, s, 1, 1, lax.Precision.HIGHEST)
    row = lax.broadcasted_iota(jnp.int32, (RANK, RANK), 0)
    col = lax.broadcasted_iota(jnp.int32, (RANK, RANK), 1)
    eye = (row == col).astype(F32)
    m = jnp.concatenate([gram, eye, jnp.zeros((RANK, 2 * RANK), F32)], axis=1)
    index = lax.broadcasted_iota(jnp.int32, (RANK, 1), 0)
    for j in range(RANK - 1):
        factor = jnp.where(index > j, m[:, j : j + 1] / m[j : j + 1, j : j + 1], 0.0)
        m = m - factor * m[j : j + 1, :]
    diag = jnp.sum(jnp.where(row == col, m[:, 0:RANK], 0.0), axis=1, keepdims=True)
    inverse = m[:, RANK : 2 * RANK] / jnp.sqrt(diag)
    out[...] = dot(inverse, s, 1, 0, lax.Precision.HIGHEST)


def make_basis(pieces, n_dp, n_t, part, din):
    width = pieces.shape[2]
    vm = pl.BlockSpec(memory_space=pltpu.VMEM)
    return pl.pallas_call(
        functools.partial(basis_kernel, n_dp=n_dp, n_t=n_t, width=width, part=part),
        in_specs=[vm],
        out_specs=vm,
        out_shape=jax.ShapeDtypeStruct((RANK, din), F32),
        scratch_shapes=[pltpu.VMEM((RANK, din), F32)],
        compiler_params=params(24),
        cost_estimate=cost(6e9, 2e6),
        name="basis",
    )(pieces)


def right_error_kernel(e_ref, b_ref, acc):
    @pl.when(pl.program_id(0) == 0)
    def _():
        acc[...] = jnp.zeros_like(acc)

    bh, bl = split(b_ref[...])
    eh, el = split(e_ref[...])
    main = dot(jnp.concatenate([bh, bl], axis=0), eh, 1, 0)
    acc[...] += main[0:RANK, :] + main[RANK:, :] + dot(bh, el, 1, 0)


def right_error(error, basis_t):
    din, outs = error.shape
    blk = 512
    return pl.pallas_call(
        right_error_kernel,
        grid=(din // blk,),
        in_specs=[
            pl.BlockSpec((blk, outs), lambda i: (i, 0)),
            pl.BlockSpec((RANK, blk), lambda i: (0, i)),
        ],
        out_specs=pl.BlockSpec((RANK, outs), lambda i: (0, 0)),
        out_shape=jax.ShapeDtypeStruct((RANK, outs), F32),
        compiler_params=params(48),
        cost_estimate=cost(8e9, error.size * 4),
        name="right_error",
    )(error, basis_t)


def right_grad_kernel(*refs, n_t, n_out, scale):
    src, b_ref, r_ref, g_ref = refs[0:4]
    x_refs = refs[4 : 4 + n_t]
    out, vacc = refs[4 + n_t :]
    r = pl.program_id(0)

    @pl.when(r == 0)
    def _():
        vacc[...] = jnp.zeros_like(vacc)

    both = jnp.concatenate(split(b_ref[...]), axis=0)
    for n in range(n_t):

        @pl.when(r == n)
        def _(n=n):
            v = dot(both, x_refs[n][...], 1, 0)
            vacc[...] += v[0:RANK, :] + v[RANK:, :]

    @pl.when(r == n_t - 1)
    def _():
        w = dot(jnp.concatenate(split(vacc[...]), axis=0), g_ref[...], 1, 0)
        total = r_ref[...] + (w[0:RANK, :] + w[RANK:, :]) * scale
        width = total.shape[1] // n_out
        for k in range(n_out):
            out[k] = total[:, k * width : (k + 1) * width]


def right_grad(src, basis_t, right_e, out_grad, xts, n_out, scale):
    part, tok = xts[0].shape
    outs = out_grad.shape[1]
    n_t = len(xts)
    same = lambda r, src: (0, 0)
    return pl.pallas_call(
        functools.partial(right_grad_kernel, n_t=n_t, n_out=n_out, scale=scale),
        grid_spec=pltpu.PrefetchScalarGridSpec(
            num_scalar_prefetch=1,
            grid=(n_t,),
            in_specs=[
                pl.BlockSpec((RANK, part), lambda r, src: (0, src[r])),
                pl.BlockSpec((RANK, outs), same),
                pl.BlockSpec((tok, outs), same),
            ]
            + [pl.BlockSpec((part, tok), same)] * n_t,
            out_specs=pl.BlockSpec((n_out, RANK, outs // n_out), lambda r, src: (0, 0, 0)),
            scratch_shapes=[pltpu.VMEM((RANK, tok), F32)],
        ),
        out_shape=jax.ShapeDtypeStruct((n_out, RANK, outs // n_out), F32),
        compiler_params=params(40),
        cost_estimate=cost(4e9, n_t * part * tok * 2),
        name="right_grad",
    )(src, basis_t, right_e, out_grad, *xts)


def x_map(n, per, r, j, *_):
    return (jnp.clip((r - n) * per + j, 0, per - 1), 0)


def right_factor(me, src, error, basis_t, out_grad, xts, n_out, scale):
    part = xts[0].shape[0]
    tok, outs = out_grad.shape
    n_t = len(xts)
    blk = min(512, part)
    per = part // blk
    return pl.pallas_call(
        functools.partial(right_kernel, n_t=n_t, per=per, n_out=n_out, scale=scale),
        grid_spec=pltpu.PrefetchScalarGridSpec(
            num_scalar_prefetch=2,
            grid=(n_t, per),
            in_specs=[
                pl.BlockSpec((blk, outs), lambda r, j, ids, src: (src[r] * per + j, 0)),
                pl.BlockSpec((RANK, blk), lambda r, j, ids, src: (0, src[r] * per + j)),
                pl.BlockSpec((tok, outs), lambda r, j, ids, src: (0, 0)),
            ]
            + [pl.BlockSpec((blk, tok), functools.partial(x_map, n, per)) for n in range(n_t)],
            out_specs=[pl.BlockSpec((RANK, outs // n_out), lambda r, j, ids, src: (0, 0))] * n_out,
            scratch_shapes=[pltpu.VMEM((RANK, outs), F32), pltpu.VMEM((RANK, tok), F32)],
        ),
        out_shape=[jax.ShapeDtypeStruct((RANK, outs // n_out), F32)] * n_out,
        compiler_params=params(40),
        cost_estimate=cost(9e9, error.size * 4 + n_t * part * tok * 2),
        name="right_factor",
    )(jnp.reshape(me, (1,)), src, error, basis_t, out_grad, *xts)


def update_kernel(*refs, n_t, n_dp, scale):
    e_ref, b_ref, g_ref, q_ref = refs[1:5]
    x_refs = refs[5 : 5 + n_t]
    out, qt_out, qs = refs[5 + n_t :]
    r, j = pl.program_id(0), pl.program_id(1)

    @pl.when((r == 0) & (j == 0))
    def _():
        q_t = jnp.concatenate([q_ref[k] for k in range(n_dp)], axis=1) * (1.0 / n_dp)
        qt_out[...] = q_t
        high, low = split(q_t)
        qs[0:RANK, :] = high
        qs[RANK : 2 * RANK, :] = low
        qs[2 * RANK : 3 * RANK, :] = high

    bh, bl = split(b_ref[...].T)
    both = jnp.concatenate([bh, bh, bl], axis=1)
    for n in range(n_t):

        @pl.when(r == n)
        def _(n=n):
            out[...] = (
                e_ref[...]
                + dot(x_refs[n][...], g_ref[...], 1, 0) * scale
                - dot(both, qs[...], 1, 0)
            )


def update_error(src, error, basis_t, out_grad, xts, q_pieces, n_dp, scale):
    part = xts[0].shape[0]
    tok, outs = out_grad.shape
    n_t = len(xts)
    blk = min(512, part)
    per = part // blk
    return pl.pallas_call(
        functools.partial(update_kernel, n_t=n_t, n_dp=n_dp, scale=scale),
        grid_spec=pltpu.PrefetchScalarGridSpec(
            num_scalar_prefetch=1,
            grid=(n_t, per),
            in_specs=[
                pl.BlockSpec((blk, outs), lambda r, j, src: (src[r] * per + j, 0)),
                pl.BlockSpec((RANK, blk), lambda r, j, src: (0, src[r] * per + j)),
                pl.BlockSpec((tok, outs), lambda r, j, src: (0, 0)),
                pl.BlockSpec(q_pieces.shape, lambda r, j, src: (0, 0, 0)),
            ]
            + [pl.BlockSpec((blk, tok), functools.partial(x_map, n, per)) for n in range(n_t)],
            out_specs=[
                pl.BlockSpec((blk, outs), lambda r, j, src: (src[r] * per + j, 0)),
                pl.BlockSpec((RANK, outs), lambda r, j, src: (0, 0)),
            ],
            scratch_shapes=[pltpu.VMEM((3 * RANK, outs), BF16)],
        ),
        out_shape=[
            jax.ShapeDtypeStruct(error.shape, F32),
            jax.ShapeDtypeStruct((RANK, outs), F32),
        ],
        compiler_params=params(48),
        cost_estimate=cost(9e9, error.size * 8 + n_t * part * tok * 2),
        name="update_error",
    )(src, error, basis_t, out_grad, q_pieces, *xts)


def near_kernel(ids, g_ref, gs_ref, w_ref, ws_ref, out):
    out[...] = dot(g_ref[...], w_ref[...], 1, 1) + dot(gs_ref[...], ws_ref[...], 1, 1)


def near_input_grad(me_t, g_own, g_sib, weight, w_sib):
    tok, outs = g_own.shape
    part = w_sib.shape[0]
    blk = 256
    row = pl.BlockSpec((blk, outs), lambda i, ids: (i, 0))
    return pl.pallas_call(
        near_kernel,
        grid_spec=pltpu.PrefetchScalarGridSpec(
            num_scalar_prefetch=1,
            grid=(tok // blk,),
            in_specs=[
                row,
                row,
                pl.BlockSpec((part, outs), lambda i, ids: (ids[0], 0)),
                pl.BlockSpec((part, outs), lambda i, ids: (0, 0)),
            ],
            out_specs=pl.BlockSpec((blk, part), lambda i, ids: (i, 0)),
        ),
        out_shape=jax.ShapeDtypeStruct((tok, part), F32),
        compiler_params=params(58),
        cost_estimate=cost(4 * tok * outs * part, 12e6),
        name="input_grad_near",
    )(jnp.reshape(me_t, (1,)), g_own, g_sib, weight, w_sib)


def far_kernel(*refs):
    prev, w_ref = refs[0], refs[1]
    g_refs, out = refs[2:-1], refs[-1]
    width = g_refs[0].shape[1]
    total = prev[...]
    for n, g in enumerate(g_refs):
        total = total + dot(g[...], w_ref[:, n * width : (n + 1) * width], 1, 1)
    out[...] = total


def far_input_grad(prev, w_far, gs, start):
    rows, outs = gs[0].shape
    tok, part = prev.shape
    blk = 256
    row = pl.BlockSpec((blk, outs), lambda i: (i, 0))
    to = pl.BlockSpec((blk, part), lambda i: (i + start // blk, 0))
    return pl.pallas_call(
        far_kernel,
        grid=(rows // blk,),
        in_specs=[to, pl.BlockSpec(w_far.shape, lambda i: (0, 0))] + [row] * len(gs),
        out_specs=to,
        out_shape=jax.ShapeDtypeStruct((tok, part), F32),
        input_output_aliases={0: 0},
        compiler_params=params(40),
        cost_estimate=cost(2 * len(gs) * rows * outs * part, 10e6),
        name="input_grad_far",
    )(prev, w_far, *gs)


def after(value, *others):
    return lax.optimization_barrier((value, others))[0]


def per_device(activations, out_grad, weight, error, q_start):
    scale = 1.0 / math.sqrt(TOK_DEV)
    n_t = lax.axis_size("tensor")
    n_dp = lax.axis_size("dp")
    chips = n_t // 2
    t = lax.axis_index("tensor").astype(jnp.int32)
    d = lax.axis_index("dp").astype(jnp.int32)
    y, c = t // 2, t % 2
    tok, part = activations.shape
    outs = out_grad.shape[1]
    din = weight.shape[0]
    error = error[0]
    q_t = q_start.T

    def to_sibling(a):
        return lax.ppermute(a, "tensor", [(i, i ^ 1) for i in range(n_t)])

    def to_chip(a, k, flip=0):
        pairs = [(i, ((i // 2 + k) % chips) * 2 + ((i % 2) ^ flip)) for i in range(n_t)]
        return lax.ppermute(a, "tensor", pairs)

    def exchange(a, axes):
        return lax.all_to_all(a, axes, 0, 0, tiled=True)

    def everywhere(a, axes, n):
        return exchange(jnp.broadcast_to(a, (n, *a.shape)), axes)

    src = jnp.stack([((y - k) % chips) * 2 + (c ^ e) for k in range(chips) for e in range(2)])
    src = src.astype(jnp.int32)
    steps = range(1, chips)

    share = part // n_dp
    pieces = []
    for k in steps:
        for e in range(2):
            dest = ((y + k) % chips) * 2 + (c ^ e)
            piece = lax.dynamic_slice(weight, (dest * part + d * share, 0), (share, outs))
            pieces.append(piece)
    x_t = after(activations, *pieces).T
    w_parts = [to_chip(p, k, e) for p, (k, e) in zip(pieces, [(k, e) for k in steps for e in range(2)])]
    x_far = [to_chip(x_t, k) for k in steps]
    n_chunk = 4
    rows = tok // n_chunk
    g_rows = after(out_grad, x_t)
    g_rows = [g_rows[i * rows : (i + 1) * rows] for i in range(n_chunk)]
    g_far = [[to_chip(a, k) for k in steps] for a in g_rows]
    w_far = lax.all_gather(jnp.concatenate(w_parts, axis=1), "dp", axis=0, tiled=True)
    w_sib = to_sibling(lax.dynamic_slice(weight, ((t ^ 1) * part, 0), (part, outs)))
    g_sib = to_sibling(out_grad)
    x_sib = to_sibling(x_t)

    y_t = project(out_grad, after(q_t, *g_rows))
    y_t = y_t + to_sibling(y_t)
    y_list = [y_t] + [to_chip(y_t, k) for k in steps]
    blocks = local_sketch(error, q_t, n_dp, n_t, part)
    blocks = sketch_rows(t, blocks, activations, y_list, scale)
    axes = ("dp", "tensor")
    n = n_dp * n_t
    blocks = exchange(blocks.reshape(n, RANK, part // n_dp), axes)
    pieces = everywhere(jnp.sum(blocks, axis=0), axes, n)
    basis_t = make_basis(pieces, n_dp, n_t, part, din)
    right_e = right_error(error, basis_t)
    grad = near_input_grad(t, out_grad, g_sib, weight, after(w_sib, right_e))

    xts = [x_t, x_sib]
    for a in x_far:
        a = after(a, grad)
        xts += [a, to_sibling(a)]
    right = right_grad(src, basis_t, right_e, out_grad, xts, n_dp, scale)
    right = jnp.sum(exchange(right, "dp"), axis=0)
    new_error, q_t = update_error(
        src, error, basis_t, out_grad, xts, everywhere(right, "dp", n_dp), n_dp, scale
    )

    for i in range(n_chunk):
        gs = []
        for a in g_far[i]:
            a = after(a, q_t)
            gs += [a, to_sibling(a)]
        grad = far_input_grad(grad, w_far, gs, i * rows)
    return (grad, new_error[None], q_t.T)


def solution(mesh):
    placed = (
        P("dp", "tensor"),
        P("dp", "tensor"),
        P(None, "tensor"),
        P("dp", None, "tensor"),
        P("tensor", None),
    )
    return jax.shard_map(
        per_device,
        mesh=mesh,
        in_specs=placed,
        out_specs=(P("dp", "tensor"), P("dp", None, "tensor"), P("tensor", None)),
        check_vma=False,
    )
```

time: 255 us -> 220 us (0.86)
  waiting for transfers between devices: 92.9 us -> 68.2 us
  starting transfers between devices: 52.1 us -> 29 us
  Pallas kernels: 68.9 us -> 83.3 us
  local copies, waits for them, and re-layouts: 24.9 us -> 13 us
  blocking collectives: 0 us -> 9.79 us
    ppermute x36 -> x8, waiting for transfers between devices: 90.8 us -> 11.2 us  [to_chip(): return lax.ppermute(a, 'tensor', pairs)]
    all_to_all x0 -> x3, waiting for transfers between devices: none -> 52.9 us  [exchange(): return lax.all_to_all(a, axes, 0, 0, tiled=True)]
    ppermute x36 -> x8, starting transfers between devices: 50 us -> 10.7 us  [to_chip(): return lax.ppermute(a, 'tensor', pairs)]
    unnamed x29 -> x6, local copies, waits for them, and re-layouts: 19.1 us -> 2.2 us
    all_to_all x0 -> x3, starting transfers between devices: none -> 15.5 us  [exchange(): return lax.all_to_all(a, axes, 0, 0, tiled=True)]
    all_to_all x0 -> x1, blocking collectives: none -> 9.79 us  [exchange(): return lax.all_to_all(a, axes, 0, 0, tiled=True)]
    pallas_call x4 -> x6, Pallas kernels: 46 us -> 55.4 us  [the longest x1 22.3 us: update_error(): pl.pallas_call(functools.partial(update_kernel, n_t=n_t, n_dp=n_dp, scale...]
    pallas_call x2 -> x4, Pallas kernels: 9.7 us -> 14.3 us  [far_input_grad(): pl.pallas_call(far_kernel, grid=(rows // blk,), in_specs=[to, pl.BlockSpe...]
  transfers between devices with their start and end apart: 46 -> 21, of which waited for: 27 -> 8; matrix products, arithmetic and copies ran while one was open for 4% -> 5% of each run, Pallas kernels for 25% -> 36%
where the time goes in v2:
time: 220 us; the launch traced here: 219 us
  Pallas kernels  83.3 us (38%)
  waiting for transfers between devices  68.2 us (31%)
  starting transfers between devices  29 us (13%)
  between operations  14.2 us (6%)
  local copies, waits for them, and re-layouts  13 us (6%)
  blocking collectives  9.79 us (4%)
    all_to_all x3, waiting for transfers between devices, exchange(): return lax.all_to_all(a, axes, 0, 0, tiled=True)  52.9 us
    pallas_call x1, Pallas kernels, update_error(): pl.pallas_call(functools.partial(update_kernel, n_t=n_t, n_dp=n_dp, scale...  22.3 us
    all_to_all x3, starting transfers between devices, exchange(): return lax.all_to_all(a, axes, 0, 0, tiled=True)  15.5 us
    pallas_call x4, Pallas kernels, far_input_grad(): pl.pallas_call(far_kernel, grid=(rows // blk,), in_specs=[to, pl.BlockSpe...  14.3 us
    pallas_call x1, Pallas kernels, local_sketch(): pl.pallas_call(functools.partial(sketch_kernel, width=width), grid=(n_t,...  12.1 us
    ppermute x8, waiting for transfers between devices, to_chip(): return lax.ppermute(a, 'tensor', pairs)  11.2 us
    ppermute x8, starting transfers between devices, to_chip(): return lax.ppermute(a, 'tensor', pairs)  10.7 us
    all_to_all x1, blocking collectives, exchange(): return lax.all_to_all(a, axes, 0, 0, tiled=True)  9.79 us
  transfers between devices with their start and end apart: 21, of which 8 were waited for; matrix products, arithmetic and copies ran while one was open for 5% of the time, Pallas kernels for 36%

profile of v2, /device:TPU:0, one launch (start us, length us, event | category | flops | bytes accessed | tf_op | source)
XLA Modules:
  0.0 218.6 jit_solution(1445151052393624653)
XLA Ops:
  8.3 3.0 %collective-permute-start.4 = (bf16[128,1024]{1,0:T(8,128)(2,1)S(1)}, bf16[128,1024]{1,0:T(8,128)(2,1)S(1)}, u32[]{:S(2)}, u32[]{:S(2)}) collective-permute-start(bf16[128,1024]{1,0:T(8,128)(2,1)S(1)} %get-tuple-element.26), channel_id=1, source_target_pairs={{0,2},{1,3},{2,0},{3,1},{4,6},{5,7},{6,4},{7,5},{8,10},{9,11},{10,... | collective-permute-start | bytes 786440 | tf_op jit(solution)/shard_map/ppermute | solution.py:416
  11.4 7.1 %collective-permute-done.4 = bf16[128,1024]{1,0:T(8,128)(2,1)S(1)} collective-permute-done((bf16[128,1024]{1,0:T(8,128)(2,1)S(1)}, bf16[128,1024]{1,0:T(8,128)(2,1)S(1)}, u32[]{:S(2)}, u32[]{:S(2)}) %collective-permute-start.4) | collective-permute-done | bytes 262176 | tf_op jit(solution)/shard_map/ppermute | solution.py:416
  18.5 4.0 %collective-permute-done.5 = bf16[128,1024]{1,0:T(8,128)(2,1)S(1)} collective-permute-done((bf16[128,1024]{1,0:T(8,128)(2,1)S(1)}, bf16[128,1024]{1,0:T(8,128)(2,1)S(1)}, u32[]{:S(2)}, u32[]{:S(2)}) %collective-permute-start.5) | collective-permute-done | bytes 262176 | tf_op jit(solution)/shard_map/ppermute | solution.py:416
  23.5 2.9 %copy.13 = bf16[1024,1024]{0,1:T(8,128)(2,1)S(1)} copy(bf16[1024,1024]{1,0:T(8,128)(2,1)} %refs_2_.1) | data formatting | bytes 4194304 | tf_op jit(solution)/shard_map/optimization_barrier | solution.py:394
  26.4 2.8 %fusion = (bf16[256,1024]{1,0:T(8,128)(2,1)}, bf16[256,1024]{1,0:T(8,128)(2,1)}, bf16[256,1024]{1,0:T(8,128)(2,1)}, bf16[256,1024]{1,0:T(8,128)(2,1)}) fusion(bf16[1024,1024]{1,0:T(8,128)(2,1)} %refs_3_.3), kind=kLoop, calls=%fused_computation.5 | loop fusion | bytes 4194304 | tf_op jit(solution)/shard_map/slice | solution.py:441
  29.2 2.3 %project.1 = f32[32,1024]{1,0:T(8,128)S(1)} custom-call(bf16[1024,1024]{1,0:T(8,128)(2,1)} %refs_3_.3, f32[32,1024]{1,0:T(8,128)S(1)} %bitcast.15), custom_call_target="tpu_custom_call" | custom-call | flops 62500000 | bytes 125000 | tf_op jit(solution)/shard_map/project/pallas_call | solution.py:44
  34.9 12.1 %error_sketch.1.refs_1_ = f32[8,4,32,128]{3,2,1,0:T(8,128)} custom-call(f32[4096,1024]{1,0:T(8,128)} %bitcast.17, f32[32,1024]{1,0:T(8,128)S(1)} %bitcast.16), custom_call_target="tpu_custom_call" | custom-call | flops 375000000 | bytes 1048576 | tf_op jit(solution)/shard_map/error_sketch/pallas_call | solution.py:75
  49.1 4.9 %all-to-all-start = ((f32[32,32,128]{2,1,0:T(8,128)}), f32[32,32,128]{2,1,0:T(8,128)S(1)}, u32[]{:S(2)}, u32[]{:S(2)}) async-start(f32[32,32,128]{2,1,0:T(8,128)} %bitcast.4), calls=%async_computation | async-start | bytes 1048576 | tf_op jit(solution)/shard_map/all_to_all | solution.py:419
  54.1 3.1 %constant_dynamic-slice_fusion.2 = bf16[1024,1024]{1,0:T(8,128)(2,1)} fusion(bf16[4096,1024]{1,0:T(8,128)(2,1)} %w_ref.1, s32[]{:T(128)S(6)} %select_n.38), kind=kLoop, calls=%fused_computation.3 | loop fusion | bytes 4194308 | tf_op jit(solution)/shard_map/dynamic_slice | solution.py:444
  59.4 19.1 %all-to-all-done = f32[32,32,128]{2,1,0:T(8,128)S(1)} async-done(((f32[32,32,128]{2,1,0:T(8,128)}), f32[32,32,128]{2,1,0:T(8,128)S(1)}, u32[]{:S(2)}, u32[]{:S(2)}) %all-to-all-start) | async-done | bytes 524320 | tf_op jit(solution)/shard_map/all_to_all | solution.py:419
  79.4 5.6 %all-to-all-start.1 = ((f32[32,32,128]{2,1,0:T(8,128)}), f32[32,32,128]{2,1,0:T(8,128)S(1)}, u32[]{:S(2)}, u32[]{:S(2)}) async-start(f32[32,32,128]{2,1,0:T(8,128)} %broadcast_in_dim.9), calls=%async_computation.1 | async-start | bytes 1048576 | tf_op jit(solution)/shard_map/all_to_all | solution.py:419
  85.4 28.5 %all-to-all-done.1.pieces = f32[32,32,128]{2,1,0:T(8,128)S(1)} async-done(((f32[32,32,128]{2,1,0:T(8,128)}), f32[32,32,128]{2,1,0:T(8,128)S(1)}, u32[]{:S(2)}, u32[]{:S(2)}) %all-to-all-start.1) | async-done | bytes 524320 | tf_op jit(solution)/shard_map/all_to_all | solution.py:419
  113.9 4.5 %basis.1.b_ref.refs_1_.refs_2_ = f32[32,4096]{1,0:T(8,128)S(1)} custom-call(f32[32,32,128]{2,1,0:T(8,128)S(1)} %all-to-all-done.1.pieces), custom_call_target="tpu_custom_call" | custom-call | flops 375000000 | bytes 125000 | tf_op jit(solution)/shard_map/basis/pallas_call | solution.py:148
  118.4 9.5 %right_error.1.refs_2_ = f32[32,1024]{1,0:T(8,128)S(1)} custom-call(f32[4096,1024]{1,0:T(8,128)} %bitcast.18, f32[32,4096]{1,0:T(8,128)S(1)} %basis.1.b_ref.refs_1_.refs_2_), custom_call_target="tpu_custom_call" | custom-call | flops 500000000 | bytes 1048576 | tf_op jit(solution)/shard_map/right_error/pallas_call | solution.py:174
  127.9 9.1 %input_grad_near.1.refs_0_ = f32[1024,1024]{1,0:T(8,128)} custom-call(s32[1]{0:T(128)} %bitcast.refs_0_.ids, bf16[1024,1024]{1,0:T(8,128)(2,1)} %refs_3_.3, bf16[1024,1024]{1,0:T(8,128)(2,1)} %collective-permute-done.gs_ref, bf16[4096,1024]{1,0:T(8,128)(2,1)} %w_ref.1, bf16[1024,1024]{1,0:T(8,128)(2,1)} %collective-permute-done.1.ws_ref), custom_call_target="tpu_custom_call" | custom-call | flops 268435456 | bytes 750000 | tf_op jit(solution)/shard_map/input_grad_near/pallas_call | solution.py:344
  141.5 7.1 %right_grad.1 = f32[8,32,128]{2,1,0:T(8,128)} custom-call(s32[4]{0:T(128)S(1)} %pad_add_fusion.refs_0_, f32[32,4096]{1,0:T(8,128)S(1)} %basis.1.b_ref.refs_1_.refs_2_, f32[32,1024]{1,0:T(8,128)S(1)} %right_error.1.refs_2_, bf16[1024,1024]{1,0:T(8,128)(2,1)} %refs_3_.3, bf16[1024,1024]{1,0:T(8,128)(2,1)S(1)} %bitcast.13, ...), custom_call_target="tpu_custom_call" | custom-call | flops 250000000 | bytes 524288 | tf_op jit(solution)/shard_map/right_grad/pallas_call | solution.py:221
  148.7 4.9 %all-to-all-start.2 = ((f32[8,32,128]{2,1,0:T(8,128)}), f32[8,32,128]{2,1,0:T(8,128)S(1)}, u32[]{:S(2)}, u32[]{:S(2)}) async-start(f32[8,32,128]{2,1,0:T(8,128)} %right_grad.1), calls=%async_computation.2 | async-start | bytes 262144 | tf_op jit(solution)/shard_map/all_to_all | solution.py:419
  155.6 5.3 %all-to-all-done.2 = f32[8,32,128]{2,1,0:T(8,128)S(1)} async-done(((f32[8,32,128]{2,1,0:T(8,128)}), f32[8,32,128]{2,1,0:T(8,128)S(1)}, u32[]{:S(2)}, u32[]{:S(2)}) %all-to-all-start.2) | async-done | bytes 131104 | tf_op jit(solution)/shard_map/all_to_all | solution.py:419
  160.9 9.8 %all_to_all.20.refs_4_ = f32[8,32,128]{2,1,0:T(8,128)S(1)} all-to-all(f32[8,32,128]{2,1,0:T(8,128)S(1)} %broadcast_in_dim.10), channel_id=1, replica_groups=mesh['dp'=8,'tensor'=4] {'dp'}, dimensions={0} | all-to-all | bytes 262144 | tf_op jit(solution)/shard_map/all_to_all | solution.py:419
  170.7 22.3 %update_error.1 = (f32[4096,1024]{1,0:T(8,128)}, f32[32,1024]{1,0:T(8,128)}) custom-call(s32[4]{0:T(128)S(1)} %pad_add_fusion.refs_0_, f32[4096,1024]{1,0:T(8,128)} %bitcast.19, f32[32,4096]{1,0:T(8,128)S(1)} %basis.1.b_ref.refs_1_.refs_2_, bf16[1024,1024]{1,0:T(8,128)(2,1)} %refs_3_.3, f32[8,32,128]{2,1,0:T(8,128)S(1)} %all_to_all.20.refs_4_, ...), custom_call_target="tpu_custom_call" | custom-call | flops 562499968 | bytes 2621440 | tf_op jit(solution)/shard_map/update_error/pallas_call | solution.py:307
  197.4 3.6 %input_grad_far.4.refs_0_ = f32[1024,1024]{1,0:T(8,128)} custom-call(f32[1024,1024]{1,0:T(8,128)} %input_grad_near.1.refs_0_, bf16[1024,2048]{1,0:T(8,128)(2,1)S(1)} %copy-done, bf16[256,1024]{1,0:T(8,128)(2,1)} %collective-permute-done.6.refs_2_, bf16[256,1024]{1,0:T(8,128)(2,1)S(1)} %collective-permute-done.10.refs_3_), custom_call_target="tpu_custom_call", output_to_operand_aliasing={{}: (0, {})} | custom-call | flops 67108864 | bytes 625000 | tf_op jit(solution)/shard_map/input_grad_far/pallas_call | solution.py:380
  201.0 3.5 %input_grad_far.5.refs_0_ = f32[1024,1024]{1,0:T(8,128)} custom-call(f32[1024,1024]{1,0:T(8,128)} %input_grad_far.4.refs_0_, bf16[1024,2048]{1,0:T(8,128)(2,1)S(1)} %copy-done, bf16[256,1024]{1,0:T(8,128)(2,1)S(1)} %collective-permute-done.11.refs_2_, bf16[256,1024]{1,0:T(8,128)(2,1)S(1)} %collective-permute-done.12.refs_3_), custom_call_target="tpu_custom_call", output_to_operand_aliasing={{}: (0, {})} | custom-call | flops 67108864 | bytes 625000 | tf_op jit(solution)/shard_map/input_grad_far/pallas_call | solution.py:380
  204.5 3.6 %input_grad_far.6.refs_0_ = f32[1024,1024]{1,0:T(8,128)} custom-call(f32[1024,1024]{1,0:T(8,128)} %input_grad_far.5.refs_0_, bf16[1024,2048]{1,0:T(8,128)(2,1)S(1)} %copy-done, bf16[256,1024]{1,0:T(8,128)(2,1)} %collective-permute-done.13.refs_2_, bf16[256,1024]{1,0:T(8,128)(2,1)S(1)} %collective-permute-done.14.refs_3_), custom_call_target="tpu_custom_call", output_to_operand_aliasing={{}: (0, {})} | custom-call | flops 67108864 | bytes 625000 | tf_op jit(solution)/shard_map/input_grad_far/pallas_call | solution.py:380
  208.1 3.6 %input_grad_far.7 = f32[1024,1024]{1,0:T(8,128)} custom-call(f32[1024,1024]{1,0:T(8,128)} %input_grad_far.6.refs_0_, bf16[1024,2048]{1,0:T(8,128)(2,1)S(1)} %copy-done, bf16[256,1024]{1,0:T(8,128)(2,1)} %collective-permute-done.15.refs_2_, bf16[256,1024]{1,0:T(8,128)(2,1)S(1)} %collective-permute-done.16.refs_3_), custom_call_target="tpu_custom_call", output_to_operand_aliasing={{}: (0, {})} | custom-call | flops 67108864 | bytes 625000 | tf_op jit(solution)/shard_map/input_grad_far/pallas_call | solution.py:380
  (49 shorter events, 21.9 us)
Async XLA Ops:
  7.2 188.0 %all-gather.2.cloned.1.call-start = ((), (), s32[]{:S(2)}) async-start(), calls=%async_computation.4 | async-start | bytes 4718592 | tf_op jit(solution)/shard_map/all_gather | solution.py:443
  8.3 10.2 %collective-permute-start.4 = (bf16[128,1024]{1,0:T(8,128)(2,1)S(1)}, bf16[128,1024]{1,0:T(8,128)(2,1)S(1)}, u32[]{:S(2)}, u32[]{:S(2)}) collective-permute-start(bf16[128,1024]{1,0:T(8,128)(2,1)S(1)} %get-tuple-element.26), channel_id=1, source_target_pairs={{0,2},{1,3},{2,0},{3,1},{4,6},{5,7},{6,4},{7,5},{8,10},{9,11},{10,... | collective-permute-start | bytes 786440 | tf_op jit(solution)/shard_map/ppermute | solution.py:416
  11.4 11.2 %collective-permute-start.5 = (bf16[128,1024]{1,0:T(8,128)(2,1)S(1)}, bf16[128,1024]{1,0:T(8,128)(2,1)S(1)}, u32[]{:S(2)}, u32[]{:S(2)}) collective-permute-start(bf16[128,1024]{1,0:T(8,128)(2,1)S(1)} %get-tuple-element.25), channel_id=1, source_target_pairs={{0,3},{1,2},{2,1},{3,0},{4,7},{5,6},{6,5},{7,4},{8,11},{9,10},{10,... | collective-permute-start | bytes 786440 | tf_op jit(solution)/shard_map/ppermute | solution.py:416
  23.5 5.8 %copy-start.2 = (f32[1024,32]{0,1:T(8,128)S(1)}, f32[1024,32]{0,1:T(8,128)}, u32[]{:S(2)}) copy-start(f32[1024,32]{0,1:T(8,128)} %param.9) | copy-start | bytes 393220
  31.6 1.5 collective-permute-start.2
  33.1 13.9 %collective-permute-start.3 = (f32[32,1024]{1,0:T(8,128)S(1)}, f32[32,1024]{1,0:T(8,128)S(1)}, u32[]{:S(2)}, u32[]{:S(2)}) collective-permute-start(f32[32,1024]{1,0:T(8,128)S(1)} %add.68.refs_3_), channel_id=1, source_target_pairs={{0,2},{1,3},{2,0},{3,1},{4,6},{5,7},{6,4},{7,5},{8,10},{9,11},{10,... | collective-permute-start | bytes 393224 | tf_op jit(solution)/shard_map/ppermute | solution.py:416
  34.9 12.1 %copy-start.1 = (bf16[1024,1024]{1,0:T(8,128)(2,1)S(1)}, bf16[1024,1024]{1,0:T(8,128)(2,1)}, u32[]{:S(2)}) copy-start(bf16[1024,1024]{1,0:T(8,128)(2,1)} %refs_2_.1) | copy-start | bytes 6291460
  49.1 29.4 %all-to-all-start = ((f32[32,32,128]{2,1,0:T(8,128)}), f32[32,32,128]{2,1,0:T(8,128)S(1)}, u32[]{:S(2)}, u32[]{:S(2)}) async-start(f32[32,32,128]{2,1,0:T(8,128)} %bitcast.4), calls=%async_computation | async-start | bytes 1048576 | tf_op jit(solution)/shard_map/all_to_all | solution.py:419
  57.1 70.8 %collective-permute-start.1 = (bf16[1024,1024]{1,0:T(8,128)(2,1)}, bf16[1024,1024]{1,0:T(8,128)(2,1)}, u32[]{:S(2)}, u32[]{:S(2)}) collective-permute-start(bf16[1024,1024]{1,0:T(8,128)(2,1)} %constant_dynamic-slice_fusion.2), channel_id=1, source_target_pairs={{0,1},{1,0},{2,3},{3,2},{4,5},{5,4},{6,7},{7,6},{8,9},{9,8},{10,11... | collective-permute-start | bytes 6291464 | tf_op jit(solution)/shard_map/ppermute | solution.py:412
  57.4 70.5 %collective-permute-start = (bf16[1024,1024]{1,0:T(8,128)(2,1)}, bf16[1024,1024]{1,0:T(8,128)(2,1)}, u32[]{:S(2)}, u32[]{:S(2)}) collective-permute-start(bf16[1024,1024]{1,0:T(8,128)(2,1)} %refs_3_.3), channel_id=1, source_target_pairs={{0,1},{1,0},{2,3},{3,2},{4,5},{5,4},{6,7},{7,6},{8,9},{9,8},{10,11... | collective-permute-start | bytes 6291464 | tf_op jit(solution)/shard_map/ppermute | solution.py:412
  57.7 79.4 %collective-permute-start.8 = (bf16[1024,1024]{1,0:T(8,128)(2,1)S(1)}, bf16[1024,1024]{1,0:T(8,128)(2,1)}, u32[]{:S(2)}, u32[]{:S(2)}) collective-permute-start(bf16[1024,1024]{1,0:T(8,128)(2,1)S(1)} %bitcast.11), channel_id=1, source_target_pairs={{0,2},{1,3},{2,0},{3,1},{4,6},{5,7},{6,4},{7,5},{8,10},{9,11},{10,... | collective-permute-start | bytes 6291464 | tf_op jit(solution)/shard_map/ppermute | solution.py:416
  79.4 34.5 %all-to-all-start.1 = ((f32[32,32,128]{2,1,0:T(8,128)}), f32[32,32,128]{2,1,0:T(8,128)S(1)}, u32[]{:S(2)}, u32[]{:S(2)}) async-start(f32[32,32,128]{2,1,0:T(8,128)} %broadcast_in_dim.9), calls=%async_computation.1 | async-start | bytes 1048576 | tf_op jit(solution)/shard_map/all_to_all | solution.py:419
  85.1 54.5 %collective-permute-start.7 = (bf16[1024,1024]{1,0:T(8,128)(2,1)S(1)}, bf16[1024,1024]{1,0:T(8,128)(2,1)}, u32[]{:S(2)}, u32[]{:S(2)}) collective-permute-start(bf16[1024,1024]{1,0:T(8,128)(2,1)S(1)} %bitcast.12), channel_id=1, source_target_pairs={{0,1},{1,0},{2,3},{3,2},{4,5},{5,4},{6,7},{7,6},{8,9},{9,8},{10,11... | collective-permute-start | bytes 6291464 | tf_op jit(solution)/shard_map/ppermute | solution.py:412
  137.0 4.5 %collective-permute-start.9 = (bf16[1024,1024]{1,0:T(8,128)(2,1)}, bf16[1024,1024]{1,0:T(8,128)(2,1)}, u32[]{:S(2)}, u32[]{:S(2)}) collective-permute-start(bf16[1024,1024]{1,0:T(8,128)(2,1)} %collective-permute-done.8.refs_6_.refs_7_), channel_id=1, source_target_pairs={{0,1},{1,0},{2,3},{3,2},{4,5},{5,4},{6,7},{7,6},{8,9},{9,8},{10,11... | collective-permute-start | bytes 6291464 | tf_op jit(solution)/shard_map/ppermute | solution.py:412
  137.4 55.7 %collective-permute-start.11 = (bf16[256,1024]{1,0:T(8,128)(2,1)}, bf16[256,1024]{1,0:T(8,128)(2,1)S(1)}, u32[]{:S(2)}, u32[]{:S(2)}) collective-permute-start(bf16[256,1024]{1,0:T(8,128)(2,1)} %get-tuple-element.29), channel_id=1, source_target_pairs={{0,2},{1,3},{2,0},{3,1},{4,6},{5,7},{6,4},{7,5},{8,10},{9,11},{10,... | collective-permute-start | bytes 1572872 | tf_op jit(solution)/shard_map/ppermute | solution.py:416
  138.3 54.7 %collective-permute-start.6 = (bf16[256,1024]{1,0:T(8,128)(2,1)}, bf16[256,1024]{1,0:T(8,128)(2,1)}, u32[]{:S(2)}, u32[]{:S(2)}) collective-permute-start(bf16[256,1024]{1,0:T(8,128)(2,1)} %get-tuple-element.30), channel_id=1, source_target_pairs={{0,2},{1,3},{2,0},{3,1},{4,6},{5,7},{6,4},{7,5},{8,10},{9,11},{10,... | collective-permute-start | bytes 1572872 | tf_op jit(solution)/shard_map/ppermute | solution.py:416
  148.7 12.2 %all-to-all-start.2 = ((f32[8,32,128]{2,1,0:T(8,128)}), f32[8,32,128]{2,1,0:T(8,128)S(1)}, u32[]{:S(2)}, u32[]{:S(2)}) async-start(f32[8,32,128]{2,1,0:T(8,128)} %right_grad.1), calls=%async_computation.2 | async-start | bytes 262144 | tf_op jit(solution)/shard_map/all_to_all | solution.py:419
  153.6 40.1 %collective-permute-start.13 = (bf16[256,1024]{1,0:T(8,128)(2,1)}, bf16[256,1024]{1,0:T(8,128)(2,1)}, u32[]{:S(2)}, u32[]{:S(2)}) collective-permute-start(bf16[256,1024]{1,0:T(8,128)(2,1)} %get-tuple-element.28), channel_id=1, source_target_pairs={{0,2},{1,3},{2,0},{3,1},{4,6},{5,7},{6,4},{7,5},{8,10},{9,11},{10,... | collective-permute-start | bytes 1572872 | tf_op jit(solution)/shard_map/ppermute | solution.py:416
  154.5 39.2 %collective-permute-start.15 = (bf16[256,1024]{1,0:T(8,128)(2,1)}, bf16[256,1024]{1,0:T(8,128)(2,1)}, u32[]{:S(2)}, u32[]{:S(2)}) collective-permute-start(bf16[256,1024]{1,0:T(8,128)(2,1)} %get-tuple-element.27), channel_id=1, source_target_pairs={{0,2},{1,3},{2,0},{3,1},{4,6},{5,7},{6,4},{7,5},{8,10},{9,11},{10,... | collective-permute-start | bytes 1572872 | tf_op jit(solution)/shard_map/ppermute | solution.py:416
  193.0 2.2 collective-permute-start.10
  193.1 7.9 %collective-permute-start.12 = (bf16[256,1024]{1,0:T(8,128)(2,1)S(1)}, bf16[256,1024]{1,0:T(8,128)(2,1)S(1)}, u32[]{:S(2)}, u32[]{:S(2)}) collective-permute-start(bf16[256,1024]{1,0:T(8,128)(2,1)S(1)} %collective-permute-done.11.refs_2_), channel_id=1, source_target_pairs={{0,1},{1,0},{2,3},{3,2},{4,5},{5,4},{6,7},{7,6},{8,9},{9,8},{10,11... | collective-permute-start | bytes 1572872 | tf_op jit(solution)/shard_map/ppermute | solution.py:412
  193.6 10.9 %collective-permute-start.14 = (bf16[256,1024]{1,0:T(8,128)(2,1)}, bf16[256,1024]{1,0:T(8,128)(2,1)S(1)}, u32[]{:S(2)}, u32[]{:S(2)}) collective-permute-start(bf16[256,1024]{1,0:T(8,128)(2,1)} %collective-permute-done.13.refs_2_), channel_id=1, source_target_pairs={{0,1},{1,0},{2,3},{3,2},{4,5},{5,4},{6,7},{7,6},{8,9},{9,8},{10,11... | collective-permute-start | bytes 1572872 | tf_op jit(solution)/shard_map/ppermute | solution.py:412
  193.7 14.4 %collective-permute-start.16 = (bf16[256,1024]{1,0:T(8,128)(2,1)}, bf16[256,1024]{1,0:T(8,128)(2,1)S(1)}, u32[]{:S(2)}, u32[]{:S(2)}) collective-permute-start(bf16[256,1024]{1,0:T(8,128)(2,1)} %collective-permute-done.15.refs_2_), channel_id=1, source_target_pairs={{0,1},{1,0},{2,3},{3,2},{4,5},{5,4},{6,7},{7,6},{8,9},{9,8},{10,11... | collective-permute-start | bytes 1572872 | tf_op jit(solution)/shard_map/ppermute | solution.py:412
  195.2 2.2 %copy-start = (bf16[1024,2048]{1,0:T(8,128)(2,1)S(1)}, bf16[1024,2048]{1,0:T(8,128)(2,1)}, u32[]{:S(2)}) copy-start(bf16[1024,2048]{1,0:T(8,128)(2,1)} %all-gather.2.cloned.1.call-done.refs_1_) | copy-start | bytes 12582916
Sparse Core Ops, SparseCore 0:
  23.6 90.8 all-gather.1

commit v3 on v2

v3 whole, which is shorter than its diff:
```python
import functools
import math

import jax
import jax.numpy as jnp
from jax import lax
from jax.experimental import pallas as pl
from jax.experimental.pallas import tpu as pltpu
from jax.sharding import PartitionSpec as P

TOK_DEV = 1024
RANK = 32
MIB = 1 << 20
F32 = jnp.float32
BF16 = jnp.bfloat16


def dot(a, b, ca, cb, precision=None):
    return lax.dot_general(
        a, b, (((ca,), (cb,)), ((), ())), precision=precision, preferred_element_type=F32
    )


def split(a):
    high = a.astype(BF16)
    return high, (a - high.astype(F32)).astype(BF16)


def params(mib):
    return pltpu.CompilerParams(vmem_limit_bytes=mib * MIB)


def cost(flops, nbytes):
    return pl.CostEstimate(flops=int(flops / 1000), bytes_accessed=int(nbytes / 1000), transcendentals=0)


def project_kernel(g_ref, qt_ref, y_ref):
    both = dot(jnp.concatenate(split(qt_ref[...]), axis=0), g_ref[...], 1, 1)
    y_ref[...] = both[0:RANK, :] + both[RANK:, :]


def project(out_grad, q_t):
    vm = pl.BlockSpec(memory_space=pltpu.VMEM)
    return pl.pallas_call(
        project_kernel,
        in_specs=[vm, vm],
        out_specs=vm,
        out_shape=jax.ShapeDtypeStruct((RANK, out_grad.shape[0]), F32),
        compiler_params=params(24),
        cost_estimate=cost(1e9, 2e6),
        name="project",
    )(out_grad, q_t)


def sketch_kernel(ids, e_ref, qt_ref, send_ref, keep_ref, qs_ref, *, width):
    phase = pl.program_id(0)

    @pl.when((phase == 0) & (pl.program_id(1) == 0) & (pl.program_id(2) == 0))
    def _():
        high, low = split(qt_ref[...])
        qs_ref[0:RANK, :] = high
        qs_ref[RANK : 2 * RANK, :] = low

    high, low = split(e_ref[...])
    main = dot(high, qs_ref[...], 1, 1)
    rest = dot(low, qs_ref[0:RANK, :], 1, 1)
    rows = (main[:, 0:RANK] + main[:, RANK : 2 * RANK] + rest).T

    @pl.when(phase == 0)
    def _():
        for k in range(send_ref.shape[0]):
            send_ref[k, 0] = rows[:, k * width : (k + 1) * width]

    @pl.when(phase == 1)
    def _():
        for k in range(keep_ref.shape[0]):
            keep_ref[k, 0] = rows[:, k * width : (k + 1) * width]


def local_sketch(core, error, q_t, n_dp, chips, part):
    blk = min(512, part)
    per = part // blk
    width = part // n_dp
    outs = error.shape[1]

    def e_map(p, y, j, ids):
        return ((2 * y + jnp.where(p == 0, 1 - ids[0], ids[0])) * per + j, 0)

    def send_map(p, y, j, ids):
        return (jnp.where(p == 0, j, per - 1), jnp.where(p == 0, y, chips - 1), 0, 0)

    def keep_map(p, y, j, ids):
        return (jnp.where(p == 1, j, 0), jnp.where(p == 1, y, 0), 0, 0)

    half = jax.ShapeDtypeStruct((n_dp, chips, RANK, width), F32)
    return pl.pallas_call(
        functools.partial(sketch_kernel, width=width),
        grid_spec=pltpu.PrefetchScalarGridSpec(
            num_scalar_prefetch=1,
            grid=(2, chips, per),
            in_specs=[
                pl.BlockSpec((blk, outs), e_map),
                pl.BlockSpec((RANK, outs), lambda p, y, j, ids: (0, 0)),
            ],
            out_specs=[
                pl.BlockSpec((n_dp // per, 1, RANK, width), send_map),
                pl.BlockSpec((n_dp // per, 1, RANK, width), keep_map),
            ],
            scratch_shapes=[pltpu.VMEM((2 * RANK, outs), BF16)],
        ),
        out_shape=[half, half],
        compiler_params=params(48),
        cost_estimate=cost(6e9, error.size * 4),
        name="error_sketch",
    )(jnp.reshape(core, (1,)), error, q_t)


def sketch_rows_kernel(*refs, scale, width):
    chip, keep, got, x_ref = refs[0:4]
    y_refs, out = refs[4:-1], refs[-1]
    y = y_refs[0][...]
    for r in y_refs[1:]:
        y = y + r[...]
    both = dot(jnp.concatenate(split(y), axis=0), x_ref[...], 1, 0)
    total = (both[0:RANK, :] + both[RANK:, :]) * scale
    out[...] = keep[...] + got[...]
    for k in range(out.shape[0]):
        out[k, chip[0]] += total[:, k * width : (k + 1) * width]


def sketch_rows(chip, keep, got, acts, y_list, scale):
    vm = pl.BlockSpec(memory_space=pltpu.VMEM)
    return pl.pallas_call(
        functools.partial(sketch_rows_kernel, scale=scale, width=keep.shape[3]),
        in_specs=[pl.BlockSpec(memory_space=pltpu.SMEM)] + [vm] * (3 + len(y_list)),
        out_specs=vm,
        out_shape=jax.ShapeDtypeStruct(keep.shape, F32),
        compiler_params=params(24),
        cost_estimate=cost(1e9, 3e6),
        name="sketch_rows",
    )(jnp.reshape(chip, (1,)), keep, got, acts, *y_list)


def basis_kernel(core, mine, other, out, sk, *, n_dp, chips, width, part):
    first = core[0] == 0
    for k in range(n_dp):
        for y in range(chips):
            a, b = mine[k * chips + y], other[k * chips + y]
            for e in range(2):
                at = (2 * y + e) * part + k * width
                block = jnp.where(first, a, b) if e == 0 else jnp.where(first, b, a)
                sk[:, at : at + width] = block * (1.0 / n_dp)
    s = sk[...]
    gram = dot(s, s, 1, 1, lax.Precision.HIGHEST)
    row = lax.broadcasted_iota(jnp.int32, (RANK, RANK), 0)
    col = lax.broadcasted_iota(jnp.int32, (RANK, RANK), 1)
    eye = (row == col).astype(F32)
    m = jnp.concatenate([gram, eye, jnp.zeros((RANK, 2 * RANK), F32)], axis=1)
    index = lax.broadcasted_iota(jnp.int32, (RANK, 1), 0)
    for j in range(RANK - 1):
        factor = jnp.where(index > j, m[:, j : j + 1] / m[j : j + 1, j : j + 1], 0.0)
        m = m - factor * m[j : j + 1, :]
    diag = jnp.sum(jnp.where(row == col, m[:, 0:RANK], 0.0), axis=1, keepdims=True)
    inverse = m[:, RANK : 2 * RANK] / jnp.sqrt(diag)
    out[...] = dot(inverse, s, 1, 0, lax.Precision.HIGHEST)


def make_basis(core, mine, other, n_dp, chips, part, din):
    width = mine.shape[2]
    vm = pl.BlockSpec(memory_space=pltpu.VMEM)
    return pl.pallas_call(
        functools.partial(basis_kernel, n_dp=n_dp, chips=chips, width=width, part=part),
        in_specs=[pl.BlockSpec(memory_space=pltpu.SMEM), vm, vm],
        out_specs=vm,
        out_shape=jax.ShapeDtypeStruct((RANK, din), F32),
        scratch_shapes=[pltpu.VMEM((RANK, din), F32)],
        compiler_params=params(24),
        cost_estimate=cost(6e9, 2e6),
        name="basis",
    )(jnp.reshape(core, (1,)), mine, other)


def right_error_kernel(e_ref, b_ref, acc):
    @pl.when(pl.program_id(0) == 0)
    def _():
        acc[...] = jnp.zeros_like(acc)

    bh, bl = split(b_ref[...])
    eh, el = split(e_ref[...])
    main = dot(jnp.concatenate([bh, bl], axis=0), eh, 1, 0)
    acc[...] += main[0:RANK, :] + main[RANK:, :] + dot(bh, el, 1, 0)


def right_error(error, basis_t):
    din, outs = error.shape
    blk = 512
    return pl.pallas_call(
        right_error_kernel,
        grid=(din // blk,),
        in_specs=[
            pl.BlockSpec((blk, outs), lambda i: (i, 0)),
            pl.BlockSpec((RANK, blk), lambda i: (0, i)),
        ],
        out_specs=pl.BlockSpec((RANK, outs), lambda i: (0, 0)),
        out_shape=jax.ShapeDtypeStruct((RANK, outs), F32),
        compiler_params=params(48),
        cost_estimate=cost(8e9, error.size * 4),
        name="right_error",
    )(error, basis_t)


def piece_specs(pieces, blk):
    specs, ranges, first = [], [], 0
    for p in pieces:
        count = p.shape[0] // blk

        def at(i, rows, first=first, count=count):
            return (jnp.clip(i - first, 0, count - 1), 0)

        specs.append(pl.BlockSpec((blk, p.shape[1]), at))
        ranges.append((first, first + count))
        first += count
    return specs, ranges


def right_grad_kernel(*refs, ranges, n_out, scale):
    b_ref, r_ref, g_ref = refs[1:4]
    x_refs = refs[4 : 4 + len(ranges)]
    out, vacc = refs[4 + len(ranges) :]
    i = pl.program_id(0)

    @pl.when(i == 0)
    def _():
        vacc[...] = jnp.zeros_like(vacc)

    both = jnp.concatenate(split(b_ref[...]), axis=0)
    for x_ref, (lo, hi) in zip(x_refs, ranges):

        @pl.when((i >= lo) & (i < hi))
        def _(x_ref=x_ref):
            v = dot(both, x_ref[...], 1, 0)
            vacc[...] += v[0:RANK, :] + v[RANK:, :]

    @pl.when(i == ranges[-1][1] - 1)
    def _():
        w = dot(jnp.concatenate(split(vacc[...]), axis=0), g_ref[...], 1, 0)
        total = r_ref[...] + (w[0:RANK, :] + w[RANK:, :]) * scale
        width = total.shape[1] // n_out
        for k in range(n_out):
            out[k] = total[:, k * width : (k + 1) * width]


def right_grad(rows, basis_t, right_e, out_grad, pieces, blk, n_out, scale):
    tok, outs = out_grad.shape
    same = lambda i, rows: (0, 0)
    specs, ranges = piece_specs(pieces, blk)
    return pl.pallas_call(
        functools.partial(right_grad_kernel, ranges=ranges, n_out=n_out, scale=scale),
        grid_spec=pltpu.PrefetchScalarGridSpec(
            num_scalar_prefetch=1,
            grid=(ranges[-1][1],),
            in_specs=[
                pl.BlockSpec((RANK, blk), lambda i, rows: (0, rows[i])),
                pl.BlockSpec((RANK, outs), same),
                pl.BlockSpec((tok, outs), same),
            ]
            + specs,
            out_specs=pl.BlockSpec((n_out, RANK, outs // n_out), lambda i, rows: (0, 0, 0)),
            scratch_shapes=[pltpu.VMEM((RANK, tok), F32)],
        ),
        out_shape=jax.ShapeDtypeStruct((n_out, RANK, outs // n_out), F32),
        compiler_params=params(48),
        cost_estimate=cost(4e9, basis_t.shape[1] * tok * 2),
        name="right_grad",
    )(rows, basis_t, right_e, out_grad, *pieces)


def update_kernel(*refs, ranges, n_dp, scale):
    e_ref, b_ref, g_ref, q_ref = refs[1:5]
    x_refs = refs[5 : 5 + len(ranges)]
    out, qt_out, qs = refs[5 + len(ranges) :]
    i = pl.program_id(0)

    @pl.when(i == 0)
    def _():
        q_t = jnp.concatenate([q_ref[k] for k in range(n_dp)], axis=1) * (1.0 / n_dp)
        qt_out[...] = q_t
        high, low = split(q_t)
        qs[0:RANK, :] = high
        qs[RANK : 2 * RANK, :] = low
        qs[2 * RANK : 3 * RANK, :] = high

    bh, bl = split(b_ref[...].T)
    both = jnp.concatenate([bh, bh, bl], axis=1)
    for x_ref, (lo, hi) in zip(x_refs, ranges):

        @pl.when((i >= lo) & (i < hi))
        def _(x_ref=x_ref):
            out[...] = (
                e_ref[...]
                + dot(x_ref[...], g_ref[...], 1, 0) * scale
                - dot(both, qs[...], 1, 0)
            )


def update_error(rows, error, basis_t, out_grad, pieces, blk, q_pieces, n_dp, scale):
    tok, outs = out_grad.shape
    specs, ranges = piece_specs(pieces, blk)
    return pl.pallas_call(
        functools.partial(update_kernel, ranges=ranges, n_dp=n_dp, scale=scale),
        grid_spec=pltpu.PrefetchScalarGridSpec(
            num_scalar_prefetch=1,
            grid=(ranges[-1][1],),
            in_specs=[
                pl.BlockSpec((blk, outs), lambda i, rows: (rows[i], 0)),
                pl.BlockSpec((RANK, blk), lambda i, rows: (0, rows[i])),
                pl.BlockSpec((tok, outs), lambda i, rows: (0, 0)),
                pl.BlockSpec(q_pieces.shape, lambda i, rows: (0, 0, 0)),
            ]
            + specs,
            out_specs=[
                pl.BlockSpec((blk, outs), lambda i, rows: (rows[i], 0)),
                pl.BlockSpec((RANK, outs), lambda i, rows: (0, 0)),
            ],
            scratch_shapes=[pltpu.VMEM((3 * RANK, outs), BF16)],
        ),
        out_shape=[
            jax.ShapeDtypeStruct(error.shape, F32),
            jax.ShapeDtypeStruct((RANK, outs), F32),
        ],
        compiler_params=params(48),
        cost_estimate=cost(9e9, error.size * 8 + basis_t.shape[1] * tok * 2),
        name="update_error",
    )(rows, error, basis_t, out_grad, q_pieces, *pieces)


def near_kernel(ids, g_ref, gs_ref, w_ref, ws_ref, out):
    out[...] = dot(g_ref[...], w_ref[...], 1, 1) + dot(gs_ref[...], ws_ref[...], 1, 1)


def near_input_grad(me_t, g_own, g_sib, weight, w_sib):
    tok, outs = g_own.shape
    part = w_sib.shape[0]
    blk = min(256, part)
    per = part // blk
    whole = pl.BlockSpec((tok, outs), lambda i, ids: (0, 0))
    return pl.pallas_call(
        near_kernel,
        grid_spec=pltpu.PrefetchScalarGridSpec(
            num_scalar_prefetch=1,
            grid=(per,),
            in_specs=[
                whole,
                whole,
                pl.BlockSpec((blk, outs), lambda i, ids: (ids[0] * per + i, 0)),
                pl.BlockSpec((blk, outs), lambda i, ids: (i, 0)),
            ],
            out_specs=pl.BlockSpec((tok, blk), lambda i, ids: (0, i)),
        ),
        out_shape=jax.ShapeDtypeStruct((tok, part), F32),
        compiler_params=params(48),
        cost_estimate=cost(4 * tok * outs * part, 12e6),
        name="input_grad_near",
    )(jnp.reshape(me_t, (1,)), g_own, g_sib, weight, w_sib)


def far_kernel(*refs):
    prev, w_ref = refs[0], refs[1]
    g_refs, out = refs[2:-1], refs[-1]
    width = g_refs[0].shape[1]
    total = prev[...]
    for n, g in enumerate(g_refs):
        total = total + dot(g[...], w_ref[:, n * width : (n + 1) * width], 1, 1)
    out[...] = total


def far_input_grad(prev, w_far, gs, start):
    rows, outs = gs[0].shape
    tok, part = prev.shape
    blk = min(256, part)
    to = pl.BlockSpec((rows, blk), lambda i: (start // rows, i))
    return pl.pallas_call(
        far_kernel,
        grid=(part // blk,),
        in_specs=[to, pl.BlockSpec((blk, w_far.shape[1]), lambda i: (i, 0))]
        + [pl.BlockSpec((rows, outs), lambda i: (0, 0))] * len(gs),
        out_specs=to,
        out_shape=jax.ShapeDtypeStruct((tok, part), F32),
        input_output_aliases={0: 0},
        compiler_params=params(48),
        cost_estimate=cost(2 * len(gs) * rows * outs * part, 10e6),
        name="input_grad_far",
    )(prev, w_far, *gs)


def after(value, *others):
    return lax.optimization_barrier((value, others))[0]


def per_device(activations, out_grad, weight, error, q_start):
    scale = 1.0 / math.sqrt(TOK_DEV)
    n_dp = lax.axis_size("dp")
    chips = lax.axis_size("chip")
    n_t = 2 * chips
    d = lax.axis_index("dp").astype(jnp.int32)
    y = lax.axis_index("chip").astype(jnp.int32)
    c = lax.axis_index("core").astype(jnp.int32)
    t = 2 * y + c
    tok, part = activations.shape
    outs = out_grad.shape[1]
    din = weight.shape[0]
    error = error[0]
    q_t = q_start.T
    steps = range(1, chips)
    share = part // n_dp
    spread = ("dp", "chip")
    n = n_dp * chips

    def to_sibling(a):
        return lax.ppermute(a, "core", [(0, 1), (1, 0)])

    def to_chip(a, k, flip=0):
        pairs = [(i, ((i // 2 + k) % chips) * 2 + ((i % 2) ^ flip)) for i in range(n_t)]
        return lax.ppermute(a, ("chip", "core"), pairs)

    def exchange(a, axes):
        return lax.all_to_all(a, axes, 0, 0, tiled=True)

    def everywhere(a, axes, n):
        return exchange(jnp.broadcast_to(a, (n, *a.shape)), axes)

    moves = [(k, e) for k in steps for e in range(2)]
    w_parts = []
    for k, e in moves:
        dest = ((y + k) % chips) * 2 + (c ^ e)
        w_parts.append(lax.dynamic_slice(weight, (dest * part + d * share, 0), (share, outs)))
    x_t = after(activations, *w_parts).T
    w_parts = [to_chip(a, k, e) for a, (k, e) in zip(w_parts, moves)]
    blk = min(512, part)
    per = part // blk
    x_far = [[to_chip(x_t[j * blk : (j + 1) * blk], k) for k in steps] for j in range(per)]

    y_t = project(out_grad, after(q_t, x_t))
    y_t = y_t + to_sibling(y_t)
    y_list = [y_t] + [to_chip(y_t, k) for k in steps]
    send, keep = local_sketch(c, error, after(q_t, y_t), n_dp, chips, part)
    w_parts = jnp.concatenate([after(a, send) for a in w_parts], axis=1)
    blocks = sketch_rows(y, keep, to_sibling(send), activations, after(y_list, w_parts), scale)
    w_far = lax.all_gather(w_parts, "dp", axis=0, tiled=True)

    g_sib = to_sibling(out_grad)
    w_sib = to_sibling(lax.dynamic_slice(after(weight, send), ((t ^ 1) * part, 0), (part, outs)))
    grad = near_input_grad(t, out_grad, g_sib, weight, after(w_sib, blocks))

    blocks = exchange(blocks.reshape(n, RANK, share), spread)
    x_far[0] = after(x_far[0], grad)
    mine = everywhere(after(jnp.sum(blocks, axis=0), x_far[0]), spread, n)
    basis_t = make_basis(c, mine, to_sibling(mine), n_dp, chips, part, din)
    right_e = right_error(error, basis_t)

    pieces = [x_t, to_sibling(x_t)]
    rows = [(2 * y + (c ^ e)) * per + j for e in range(2) for j in range(per)]
    for j in range(per):
        if j > 0:
            x_far[j] = after(x_far[j], right_e)
        for k, a in zip(steps, x_far[j]):
            for e in range(2):
                pieces.append(to_sibling(a) if e else a)
                rows.append((2 * ((y - k) % chips) + (c ^ e)) * per + j)
    rows = jnp.stack(rows).astype(jnp.int32)

    n_chunk = 2
    span = tok // n_chunk
    g_far = []
    for i in range(n_chunk):
        g = after(out_grad, mine if i == 0 else right_e)[i * span : (i + 1) * span]
        g_far.append([to_chip(g, k) for k in steps])

    def far(grad, i):
        gs = []
        for a in g_far[i]:
            gs += [a, to_sibling(a)]
        return far_input_grad(grad, w_far, gs, i * span)

    right = right_grad(rows, basis_t, right_e, out_grad, pieces, blk, n_dp, scale)
    right = jnp.sum(exchange(right, "dp"), axis=0)
    g_far[0] = after(g_far[0], right)
    q_pieces = everywhere(after(right, g_far[0]), "dp", n_dp)
    new_error, q_t = update_error(
        rows, error, basis_t, out_grad, pieces, blk, q_pieces, n_dp, scale
    )
    for i in range(n_chunk):
        if i > 0:
            g_far[i] = after(g_far[i], q_t)
        grad = far(grad, i)
    return (grad, new_error[None], q_t.T)


def solution(mesh):
    n_dp, n_t = mesh.devices.shape
    mesh = jax.sharding.Mesh(mesh.devices.reshape(n_dp, n_t // 2, 2), ("dp", "chip", "core"))
    tensor = ("chip", "core")
    placed = (
        P("dp", tensor),
        P("dp", tensor),
        P(None, tensor),
        P("dp", None, tensor),
        P(tensor, None),
    )
    return jax.shard_map(
        per_device,
        mesh=mesh,
        in_specs=placed,
        out_specs=(P("dp", tensor), P("dp", None, tensor), P(tensor, None)),
        check_vma=False,
    )
```

time: 220 us -> 217 us (0.986)
  blocking collectives: 9.79 us -> 30.1 us
  waiting for transfers between devices: 68.2 us -> 52.6 us
  starting transfers between devices: 29 us -> 21.3 us
  local copies, waits for them, and re-layouts: 13 us -> 17 us
  Pallas kernels: 83.3 us -> 80.2 us
    all_to_all x3 -> x2, waiting for transfers between devices: 52.9 us -> 19.4 us  [exchange(): return lax.all_to_all(a, axes, 0, 0, tiled=True)]
    all_to_all x1 -> x2, blocking collectives: 9.79 us -> 30.1 us  [exchange(): return lax.all_to_all(a, axes, 0, 0, tiled=True)]
    ppermute x17, waiting for transfers between devices: 15.3 us -> 33.2 us  [the longest x7 30.6 us: to_chip(): return lax.ppermute(a, ('chip', 'core'), pairs)]
    all_to_all x3 -> x2, starting transfers between devices: 15.5 us -> 10.6 us  [exchange(): return lax.all_to_all(a, axes, 0, 0, tiled=True)]
    ppermute x17, starting transfers between devices: 13.5 us -> 10.6 us  [the longest x7 9.01 us: to_chip(): return lax.ppermute(a, ('chip', 'core'), pairs)]
    pallas_call x9 -> x7, Pallas kernels: 62.4 us -> 61.5 us  [the longest x1 22.7 us: update_error(): pl.pallas_call(functools.partial(update_kernel, ranges=ranges, n_dp=n_dp,...]
  transfers between devices with their start and end apart: 21 -> 20, of which waited for: 8 -> 6; matrix products, arithmetic and copies ran while one was open for 5% -> 6% of each run, Pallas kernels for 36% -> 34%
where the time goes in v3:
time: 217 us; the launch traced here: 216 us
  Pallas kernels  80.2 us (37%)
  waiting for transfers between devices  52.6 us (24%)
  blocking collectives  30.1 us (14%)
  starting transfers between devices  21.3 us (10%)
  local copies, waits for them, and re-layouts  17 us (8%)
  between operations  14.3 us (7%)
    ppermute x7, waiting for transfers between devices, to_chip(): return lax.ppermute(a, ('chip', 'core'), pairs)  30.6 us
    all_to_all x2, blocking collectives, exchange(): return lax.all_to_all(a, axes, 0, 0, tiled=True)  30.1 us
    pallas_call x1, Pallas kernels, update_error(): pl.pallas_call(functools.partial(update_kernel, ranges=ranges, n_dp=n_dp,...  22.7 us
    all_to_all x2, waiting for transfers between devices, exchange(): return lax.all_to_all(a, axes, 0, 0, tiled=True)  19.4 us
    pallas_call x2, Pallas kernels, far_input_grad(): pl.pallas_call(far_kernel, grid=(part // blk,), in_specs=[to, pl.BlockSpe...  13.3 us
    pallas_call x1, Pallas kernels, local_sketch(): pl.pallas_call(functools.partial(sketch_kernel, width=width), grid_spec=p...  11.4 us
    all_to_all x2, starting transfers between devices, exchange(): return lax.all_to_all(a, axes, 0, 0, tiled=True)  10.6 us
    pallas_call x1, Pallas kernels, right_error(): pl.pallas_call(right_error_kernel, grid=(din // blk,), in_specs=[pl.Block...  9.5 us
  transfers between devices with their start and end apart: 20, of which 6 were waited for; matrix products, arithmetic and copies ran while one was open for 6% of the time, Pallas kernels for 34%

profile of v3, /device:TPU:0, one launch (start us, length us, event | category | flops | bytes accessed | tf_op | source)
XLA Modules:
  0.0 215.5 jit_solution(10360505987704398447)
XLA Ops:
  7.3 1.9 constant_dynamic-slice_fusion.1
  9.2 3.0 %collective-permute-start.5 = (bf16[128,1024]{1,0:T(8,128)(2,1)S(1)}, bf16[128,1024]{1,0:T(8,128)(2,1)S(1)}, u32[]{:S(2)}, u32[]{:S(2)}) collective-permute-start(bf16[128,1024]{1,0:T(8,128)(2,1)S(1)} %get-tuple-element.46), channel_id=1, source_target_pairs={{0,2},{1,3},{2,0},{3,1},{4,6},{5,7},{6,4},{7,5},{8,10},{9,11},{10,... | collective-permute-start | bytes 786440 | tf_op jit(solution)/shard_map/ppermute | solution.py:424
  12.1 4.0 %copy.10 = bf16[1024,1024]{0,1:T(8,128)(2,1)} copy(bf16[1024,1024]{1,0:T(8,128)(2,1)} %refs_3_.3) | data formatting | bytes 4194304 | tf_op jit(solution)/shard_map/optimization_barrier | solution.py:397
  18.2 11.4 %error_sketch.1 = (f32[8,2,32,128]{3,2,1,0:T(8,128)S(1)}, f32[8,2,32,128]{3,2,1,0:T(8,128)S(1)}) custom-call(s32[1]{0:T(128)} %bitcast.1.ids.core, f32[4096,1024]{1,0:T(8,128)} %bitcast.19, f32[32,1024]{1,0:T(8,128)S(1)} %bitcast.18), custom_call_target="tpu_custom_call" | custom-call | flops 6000000 | bytes 16777 | tf_op jit(solution)/shard_map/error_sketch/pallas_call | solution.py:96
  33.2 3.2 %constant_dynamic-slice_fusion = bf16[1024,1024]{1,0:T(8,128)(2,1)} fusion(bf16[4096,1024]{1,0:T(8,128)(2,1)} %w_ref.1, s32[]{:T(128)S(6)} %select_n.31), kind=kLoop, calls=%fused_computation.2 | loop fusion | bytes 4194308 | tf_op jit(solution)/shard_map/dynamic_slice | solution.py:452
  37.0 1.5 fusion
  38.5 1.8 collective-permute-start.7
  40.6 26.3 %collective-permute-done.4.refs_5_ = f32[32,1024]{1,0:T(8,128)S(1)} collective-permute-done((f32[32,1024]{1,0:T(8,128)S(1)}, f32[32,1024]{1,0:T(8,128)S(1)}, u32[]{:S(2)}, u32[]{:S(2)}) %collective-permute-start.4) | collective-permute-done | bytes 131104 | tf_op jit(solution)/shard_map/ppermute | solution.py:424
  68.2 7.1 %all-to-all-start = ((f32[16,32,128]{2,1,0:T(8,128)}), f32[16,32,128]{2,1,0:T(8,128)S(1)}, u32[]{:S(2)}, u32[]{:S(2)}) async-start(f32[16,32,128]{2,1,0:T(8,128)} %bitcast.6), calls=%async_computation | async-start | bytes 524288 | tf_op jit(solution)/shard_map/all_to_all | solution.py:427
  75.3 1.9 collective-permute-start.12
  77.2 12.3 %all-to-all-done = f32[16,32,128]{2,1,0:T(8,128)S(1)} async-done(((f32[16,32,128]{2,1,0:T(8,128)}), f32[16,32,128]{2,1,0:T(8,128)S(1)}, u32[]{:S(2)}, u32[]{:S(2)}) %all-to-all-start) | async-done | bytes 262176 | tf_op jit(solution)/shard_map/all_to_all | solution.py:427
  89.6 8.5 %input_grad_near.1.refs_0_ = f32[1024,1024]{1,0:T(8,128)} custom-call(s32[1]{0:T(128)} %bitcast.ids, bf16[1024,1024]{1,0:T(8,128)(2,1)S(1)} %copy-done, bf16[1024,1024]{1,0:T(8,128)(2,1)} %collective-permute-done.gs_ref, bf16[4096,1024]{1,0:T(8,128)(2,1)} %w_ref.1, bf16[1024,1024]{1,0:T(8,128)(2,1)} %collective-permute-done.2.ws_ref), custom_call_target="tpu_custom_call" | custom-call | flops 4294967 | bytes 12000 | tf_op jit(solution)/shard_map/input_grad_near/pallas_call | solution.py:347
  98.1 19.6 %all_to_all.20.mine = f32[16,32,128]{2,1,0:T(8,128)S(1)} all-to-all(f32[16,32,128]{2,1,0:T(8,128)S(1)} %broadcast_in_dim.9), channel_id=1, replica_groups=mesh['dp'=8,'chip'=2,'core'=2] {'dp','chip'}, dimensions={0} | all-to-all | bytes 524288 | tf_op jit(solution)/shard_map/all_to_all | solution.py:427
  119.5 4.5 %basis.1.b_ref.refs_1_.refs_2_ = f32[32,4096]{1,0:T(8,128)S(1)} custom-call(s32[1]{0:T(128)} %bitcast.1.ids.core, f32[16,32,128]{2,1,0:T(8,128)S(1)} %all_to_all.20.mine, f32[16,32,128]{2,1,0:T(8,128)S(1)} %collective-permute-done.9.other), custom_call_target="tpu_custom_call" | custom-call | flops 6000000 | bytes 2000 | tf_op jit(solution)/shard_map/basis/pallas_call | solution.py:171
  124.0 9.5 %right_error.1.refs_2_ = f32[32,1024]{1,0:T(8,128)S(1)} custom-call(f32[4096,1024]{1,0:T(8,128)} %bitcast.20, f32[32,4096]{1,0:T(8,128)S(1)} %basis.1.b_ref.refs_1_.refs_2_), custom_call_target="tpu_custom_call" | custom-call | flops 8000000 | bytes 16777 | tf_op jit(solution)/shard_map/right_error/pallas_call | solution.py:197
  136.4 1.5 collective-permute-start.15
  138.0 8.2 %right_grad.1 = f32[8,32,128]{2,1,0:T(8,128)S(1)} custom-call(s32[8]{0:T(128)S(1)} %stack.35.refs_0_, f32[32,4096]{1,0:T(8,128)S(1)} %basis.1.b_ref.refs_1_.refs_2_, f32[32,1024]{1,0:T(8,128)S(1)} %right_error.1.refs_2_, bf16[1024,1024]{1,0:T(8,128)(2,1)} %refs_3_.5, bf16[1024,1024]{1,0:T(8,128)(2,1)} %bitcast.23, ...), custom_call_target="tpu_custom_call" | custom-call | flops 4000000 | bytes 8388 | tf_op jit(solution)/shard_map/right_grad/pallas_call | solution.py:257
  146.3 10.6 %all_to_all.21 = f32[8,32,128]{2,1,0:T(8,128)S(1)} all-to-all(f32[8,32,128]{2,1,0:T(8,128)S(1)} %right_grad.1), channel_id=1, replica_groups=mesh['dp'=8,'chip'=2,'core'=2] {'dp'}, dimensions={0} | all-to-all | bytes 262144 | tf_op jit(solution)/shard_map/all_to_all | solution.py:427
  156.8 4.3 %collective-permute-done.8.refs_2_ = bf16[512,1024]{1,0:T(8,128)(2,1)} collective-permute-done((bf16[512,1024]{1,0:T(8,128)(2,1)}, bf16[512,1024]{1,0:T(8,128)(2,1)}, u32[]{:S(2)}, u32[]{:S(2)}) %collective-permute-start.8) | collective-permute-done | bytes 1048608 | tf_op jit(solution)/shard_map/ppermute | solution.py:424
  161.8 3.6 %all-to-all-start.3 = ((f32[8,32,128]{2,1,0:T(8,128)}), f32[8,32,128]{2,1,0:T(8,128)S(1)}, u32[]{:S(2)}, u32[]{:S(2)}) async-start(f32[8,32,128]{2,1,0:T(8,128)} %broadcast_in_dim.10), calls=%async_computation.3 | async-start | bytes 262144 | tf_op jit(solution)/shard_map/all_to_all | solution.py:427
  165.4 7.1 %all-to-all-done.3.refs_4_ = f32[8,32,128]{2,1,0:T(8,128)S(1)} async-done(((f32[8,32,128]{2,1,0:T(8,128)}), f32[8,32,128]{2,1,0:T(8,128)S(1)}, u32[]{:S(2)}, u32[]{:S(2)}) %all-to-all-start.3) | async-done | bytes 131104 | tf_op jit(solution)/shard_map/all_to_all | solution.py:427
  172.6 22.7 %update_error.1 = (f32[4096,1024]{1,0:T(8,128)}, f32[32,1024]{1,0:T(8,128)}) custom-call(s32[8]{0:T(128)S(1)} %stack.35.refs_0_, f32[4096,1024]{1,0:T(8,128)} %bitcast.21, f32[32,4096]{1,0:T(8,128)S(1)} %basis.1.b_ref.refs_1_.refs_2_, bf16[1024,1024]{1,0:T(8,128)(2,1)} %refs_3_.5, f32[8,32,128]{2,1,0:T(8,128)S(1)} %all-to-all-done.3.refs_4_, ...), custom_call_target="tpu_custom_call" | custom-call | flops 9000000 | bytes 41943 | tf_op jit(solution)/shard_map/update_error/pallas_call | solution.py:309
  195.4 6.8 %input_grad_far.2.refs_0_ = f32[1024,1024]{1,0:T(8,128)} custom-call(f32[1024,1024]{1,0:T(8,128)} %input_grad_near.1.refs_0_, bf16[1024,2048]{1,0:T(8,128)(2,1)} %all-gather.2.cloned.1.call-done.refs_1_, bf16[512,1024]{1,0:T(8,128)(2,1)} %collective-permute-done.8.refs_2_, ...), custom_call_target="tpu_custom_call", output_to_operand_aliasing={{}: (0, {})} | custom-call | flops 2147483 | bytes 10000 | tf_op jit(solution)/shard_map/input_grad_far/pallas_call | solution.py:382
  202.2 6.5 %input_grad_far.3 = f32[1024,1024]{1,0:T(8,128)} custom-call(f32[1024,1024]{1,0:T(8,128)} %input_grad_far.2.refs_0_, bf16[1024,2048]{1,0:T(8,128)(2,1)} %all-gather.2.cloned.1.call-done.refs_1_, bf16[512,1024]{1,0:T(8,128)(2,1)} %collective-permute-done.15.refs_2_, bf16[512,1024]{1,0:T(8,128)(2,1)S(1)} %collective-permute-done.16.refs_3_), custom_call_target="tpu_custom_call", output_to_operand_aliasing={{}: (0, {})} | custom-call | flops 2147483 | bytes 10000 | tf_op jit(solution)/shard_map/input_grad_far/pallas_call | solution.py:382
  (55 shorter events, 13.4 us)
Async XLA Ops:
  7.2 8.9 %copy-start.2 = (f32[1024,32]{0,1:T(8,128)S(1)}, f32[1024,32]{0,1:T(8,128)}, u32[]{:S(2)}) copy-start(f32[1024,32]{0,1:T(8,128)} %param.9) | copy-start | bytes 393220
  7.2 8.9 %copy-start = (bf16[1024,1024]{1,0:T(8,128)(2,1)S(1)}, bf16[1024,1024]{1,0:T(8,128)(2,1)}, u32[]{:S(2)}) copy-start(bf16[1024,1024]{1,0:T(8,128)(2,1)} %refs_3_.5) | copy-start | bytes 6291460
  7.2 188.2 %all-gather.2.cloned.1.call-start = ((), (), s32[]{:S(2)}) async-start(), calls=%async_computation.4 | async-start | bytes 4718592 | tf_op jit(solution)/shard_map/all_gather | solution.py:449
  9.2 20.5 %collective-permute-start.5 = (bf16[128,1024]{1,0:T(8,128)(2,1)S(1)}, bf16[128,1024]{1,0:T(8,128)(2,1)S(1)}, u32[]{:S(2)}, u32[]{:S(2)}) collective-permute-start(bf16[128,1024]{1,0:T(8,128)(2,1)S(1)} %get-tuple-element.46), channel_id=1, source_target_pairs={{0,2},{1,3},{2,0},{3,1},{4,6},{5,7},{6,4},{7,5},{8,10},{9,11},{10,... | collective-permute-start | bytes 786440 | tf_op jit(solution)/shard_map/ppermute | solution.py:424
  12.1 19.2 %collective-permute-start.6 = (bf16[128,1024]{1,0:T(8,128)(2,1)}, bf16[128,1024]{1,0:T(8,128)(2,1)}, u32[]{:S(2)}, u32[]{:S(2)}) collective-permute-start(bf16[128,1024]{1,0:T(8,128)(2,1)} %get-tuple-element.45), channel_id=1, source_target_pairs={{0,3},{1,2},{2,1},{3,0},{4,7},{5,6},{6,5},{7,4},{8,11},{9,10},{10,... | collective-permute-start | bytes 786440 | tf_op jit(solution)/shard_map/ppermute | solution.py:424
  16.8 1.4 collective-permute-start.1
  33.2 3.8 %copy-start.3 = (bf16[1024,1024]{0,1:T(8,128)(2,1)S(1)}, bf16[1024,1024]{0,1:T(8,128)(2,1)}, u32[]{:S(2)}) copy-start(bf16[1024,1024]{0,1:T(8,128)(2,1)} %copy.10) | copy-start | bytes 6291460
  33.2 33.8 %copy-start.1 = (bf16[1024,1024]{1,0:T(8,128)(2,1)S(1)}, bf16[1024,1024]{1,0:T(8,128)(2,1)}, u32[]{:S(2)}) copy-start(bf16[1024,1024]{1,0:T(8,128)(2,1)} %refs_3_.3) | copy-start | bytes 6291460
  36.5 53.1 %collective-permute-start.2 = (bf16[1024,1024]{1,0:T(8,128)(2,1)}, bf16[1024,1024]{1,0:T(8,128)(2,1)}, u32[]{:S(2)}, u32[]{:S(2)}) collective-permute-start(bf16[1024,1024]{1,0:T(8,128)(2,1)} %constant_dynamic-slice_fusion), channel_id=1, source_target_pairs={{0,1},{1,0},{2,3},{3,2},{4,5},{5,4},{6,7},{7,6},{8,9},{9,8},{10,11... | collective-permute-start | bytes 6291464 | tf_op jit(solution)/shard_map/ppermute | solution.py:420
  36.6 52.9 %collective-permute-start = (bf16[1024,1024]{1,0:T(8,128)(2,1)S(1)}, bf16[1024,1024]{1,0:T(8,128)(2,1)}, u32[]{:S(2)}, u32[]{:S(2)}) collective-permute-start(bf16[1024,1024]{1,0:T(8,128)(2,1)S(1)} %copy-done), channel_id=1, source_target_pairs={{0,1},{1,0},{2,3},{3,2},{4,5},{5,4},{6,7},{7,6},{8,9},{9,8},{10,11... | collective-permute-start | bytes 6291464 | tf_op jit(solution)/shard_map/ppermute | solution.py:420
  38.5 59.5 %collective-permute-start.7 = (bf16[512,1024]{1,0:T(8,128)(2,1)}, bf16[512,1024]{1,0:T(8,128)(2,1)}, u32[]{:S(2)}, u32[]{:S(2)}) collective-permute-start(bf16[512,1024]{1,0:T(8,128)(2,1)} %get-tuple-element.48), channel_id=1, source_target_pairs={{0,2},{1,3},{2,0},{3,1},{4,6},{5,7},{6,4},{7,5},{8,10},{9,11},{10,... | collective-permute-start | bytes 3145736 | tf_op jit(solution)/shard_map/ppermute | solution.py:424
  40.3 26.7 %collective-permute-start.3 = (f32[8,2,32,128]{3,2,1,0:T(8,128)S(1)}, f32[8,2,32,128]{3,2,1,0:T(8,128)S(1)}, u32[]{:S(2)}, u32[]{:S(2)}) collective-permute-start(f32[8,2,32,128]{3,2,1,0:T(8,128)S(1)} %get-tuple-element.27), channel_id=1, source_target_pairs={{0,1},{1,0},{2,3},{3,2},{4,5},{5,4},{6,7},{7,6},{8,9},{9,8},{10,11... | collective-permute-start | bytes 786440 | tf_op jit(solution)/shard_map/ppermute | solution.py:420
  40.4 26.6 %collective-permute-start.4 = (f32[32,1024]{1,0:T(8,128)S(1)}, f32[32,1024]{1,0:T(8,128)S(1)}, u32[]{:S(2)}, u32[]{:S(2)}) collective-permute-start(f32[32,1024]{1,0:T(8,128)S(1)} %add.78.refs_4_), channel_id=1, source_target_pairs={{0,2},{1,3},{2,0},{3,1},{4,6},{5,7},{6,4},{7,5},{8,10},{9,11},{10,... | collective-permute-start | bytes 393224 | tf_op jit(solution)/shard_map/ppermute | solution.py:424
  68.2 21.3 %all-to-all-start = ((f32[16,32,128]{2,1,0:T(8,128)}), f32[16,32,128]{2,1,0:T(8,128)S(1)}, u32[]{:S(2)}, u32[]{:S(2)}) async-start(f32[16,32,128]{2,1,0:T(8,128)} %bitcast.6), calls=%async_computation | async-start | bytes 524288 | tf_op jit(solution)/shard_map/all_to_all | solution.py:427
  75.3 58.2 %collective-permute-start.12 = (bf16[512,1024]{1,0:T(8,128)(2,1)}, bf16[512,1024]{1,0:T(8,128)(2,1)}, u32[]{:S(2)}, u32[]{:S(2)}) collective-permute-start(bf16[512,1024]{1,0:T(8,128)(2,1)} %get-tuple-element.47), channel_id=1, source_target_pairs={{0,2},{1,3},{2,0},{3,1},{4,6},{5,7},{6,4},{7,5},{8,10},{9,11},{10,... | collective-permute-start | bytes 3145736 | tf_op jit(solution)/shard_map/ppermute | solution.py:424
  77.2 60.8 %collective-permute-start.10 = (bf16[1024,1024]{1,0:T(8,128)(2,1)}, bf16[1024,1024]{1,0:T(8,128)(2,1)}, u32[]{:S(2)}, u32[]{:S(2)}) collective-permute-start(bf16[1024,1024]{1,0:T(8,128)(2,1)} %bitcast.22), channel_id=1, source_target_pairs={{0,1},{1,0},{2,3},{3,2},{4,5},{5,4},{6,7},{7,6},{8,9},{9,8},{10,11... | collective-permute-start | bytes 6291464 | tf_op jit(solution)/shard_map/ppermute | solution.py:420
  117.6 1.9 collective-permute-start.9
  117.6 20.4 %collective-permute-start.11 = (bf16[512,1024]{1,0:T(8,128)(2,1)}, bf16[512,1024]{1,0:T(8,128)(2,1)}, u32[]{:S(2)}, u32[]{:S(2)}) collective-permute-start(bf16[512,1024]{1,0:T(8,128)(2,1)} %collective-permute-done.7.refs_6_.refs_7_), channel_id=1, source_target_pairs={{0,1},{1,0},{2,3},{3,2},{4,5},{5,4},{6,7},{7,6},{8,9},{9,8},{10,11... | collective-permute-start | bytes 3145736 | tf_op jit(solution)/shard_map/ppermute | solution.py:420
  133.6 4.5 %collective-permute-start.13 = (bf16[512,1024]{1,0:T(8,128)(2,1)}, bf16[512,1024]{1,0:T(8,128)(2,1)}, u32[]{:S(2)}, u32[]{:S(2)}) collective-permute-start(bf16[512,1024]{1,0:T(8,128)(2,1)} %collective-permute-done.12.refs_8_.refs_9_), channel_id=1, source_target_pairs={{0,1},{1,0},{2,3},{3,2},{4,5},{5,4},{6,7},{7,6},{8,9},{9,8},{10,11... | collective-permute-start | bytes 3145736 | tf_op jit(solution)/shard_map/ppermute | solution.py:420
  134.8 26.3 %collective-permute-start.8 = (bf16[512,1024]{1,0:T(8,128)(2,1)}, bf16[512,1024]{1,0:T(8,128)(2,1)}, u32[]{:S(2)}, u32[]{:S(2)}) collective-permute-start(bf16[512,1024]{1,0:T(8,128)(2,1)} %slice.13), channel_id=1, source_target_pairs={{0,2},{1,3},{2,0},{3,1},{4,6},{5,7},{6,4},{7,5},{8,10},{9,11},{10,... | collective-permute-start | bytes 3145736 | tf_op jit(solution)/shard_map/ppermute | solution.py:424
  136.4 58.9 %collective-permute-start.15 = (bf16[512,1024]{1,0:T(8,128)(2,1)}, bf16[512,1024]{1,0:T(8,128)(2,1)}, u32[]{:S(2)}, u32[]{:S(2)}) collective-permute-start(bf16[512,1024]{1,0:T(8,128)(2,1)} %slice.15), channel_id=1, source_target_pairs={{0,2},{1,3},{2,0},{3,1},{4,6},{5,7},{6,4},{7,5},{8,10},{9,11},{10,... | collective-permute-start | bytes 3145736 | tf_op jit(solution)/shard_map/ppermute | solution.py:424
  161.8 10.8 %all-to-all-start.3 = ((f32[8,32,128]{2,1,0:T(8,128)}), f32[8,32,128]{2,1,0:T(8,128)S(1)}, u32[]{:S(2)}, u32[]{:S(2)}) async-start(f32[8,32,128]{2,1,0:T(8,128)} %broadcast_in_dim.10), calls=%async_computation.3 | async-start | bytes 262144 | tf_op jit(solution)/shard_map/all_to_all | solution.py:427
  165.3 30.0 %collective-permute-start.14 = (bf16[512,1024]{1,0:T(8,128)(2,1)}, bf16[512,1024]{1,0:T(8,128)(2,1)}, u32[]{:S(2)}, u32[]{:S(2)}) collective-permute-start(bf16[512,1024]{1,0:T(8,128)(2,1)} %collective-permute-done.8.refs_2_), channel_id=1, source_target_pairs={{0,1},{1,0},{2,3},{3,2},{4,5},{5,4},{6,7},{7,6},{8,9},{9,8},{10,11... | collective-permute-start | bytes 3145736 | tf_op jit(solution)/shard_map/ppermute | solution.py:420
  195.3 6.9 %collective-permute-start.16 = (bf16[512,1024]{1,0:T(8,128)(2,1)}, bf16[512,1024]{1,0:T(8,128)(2,1)S(1)}, u32[]{:S(2)}, u32[]{:S(2)}) collective-permute-start(bf16[512,1024]{1,0:T(8,128)(2,1)} %collective-permute-done.15.refs_2_), channel_id=1, source_target_pairs={{0,1},{1,0},{2,3},{3,2},{4,5},{5,4},{6,7},{7,6},{8,9},{9,8},{10,11... | collective-permute-start | bytes 3145736 | tf_op jit(solution)/shard_map/ppermute | solution.py:420
  (2 other events, 1.5 us)
Sparse Core Ops, SparseCore 0:
  33.3 83.3 all-gather.1

commit v4 on v3

--- a/solution.py
+++ b/solution.py
@@ -30,8 +30,10 @@
     return pltpu.CompilerParams(vmem_limit_bytes=mib * MIB)
 
 
-def cost(flops, nbytes):
-    return pl.CostEstimate(flops=int(flops / 1000), bytes_accessed=int(nbytes / 1000), transcendentals=0)
+def cost(flops, nbytes, weight=0.001):
+    return pl.CostEstimate(
+        flops=int(flops * weight), bytes_accessed=int(nbytes * weight), transcendentals=0
+    )
 
 
 def project_kernel(g_ref, qt_ref, y_ref):
@@ -110,7 +112,7 @@
         ),
         out_shape=[half, half],
         compiler_params=params(48),
-        cost_estimate=cost(6e9, error.size * 4),
+        cost_estimate=cost(6e9, error.size * 4, 2),
         name="error_sketch",
     )(jnp.reshape(core, (1,)), error, q_t)
 
@@ -180,33 +182,49 @@
     )(jnp.reshape(core, (1,)), mine, other)
 
 
-def right_error_kernel(e_ref, b_ref, acc):
-    @pl.when(pl.program_id(0) == 0)
+def right_rows_kernel(rows, m_ref, e_ref, b_ref, acc, *, near):
+    i = pl.program_id(0)
+
+    @pl.when(i == 0)
     def _():
         acc[...] = jnp.zeros_like(acc)
 
     bh, bl = split(b_ref[...])
-    eh, el = split(e_ref[...])
-    main = dot(jnp.concatenate([bh, bl], axis=0), eh, 1, 0)
-    acc[...] += main[0:RANK, :] + main[RANK:, :] + dot(bh, el, 1, 0)
-
-
-def right_error(error, basis_t):
+    both = jnp.concatenate([bh, bl], axis=0)
+
+    def add(ref):
+        high, low = split(ref[...])
+        main = dot(both, high, 1, 0)
+        acc[...] += main[0:RANK, :] + main[RANK:, :] + dot(bh, low, 1, 0)
+
+    @pl.when(i < near)
+    def _():
+        add(m_ref)
+
+    @pl.when(i >= near)
+    def _():
+        add(e_ref)
+
+
+def right_rows(rows, near, merged, error, basis_t, blk):
     din, outs = error.shape
-    blk = 512
-    return pl.pallas_call(
-        right_error_kernel,
-        grid=(din // blk,),
-        in_specs=[
-            pl.BlockSpec((blk, outs), lambda i: (i, 0)),
-            pl.BlockSpec((RANK, blk), lambda i: (0, i)),
-        ],
-        out_specs=pl.BlockSpec((RANK, outs), lambda i: (0, 0)),
+    return pl.pallas_call(
+        functools.partial(right_rows_kernel, near=near),
+        grid_spec=pltpu.PrefetchScalarGridSpec(
+            num_scalar_prefetch=1,
+            grid=(din // blk,),
+            in_specs=[
+                pl.BlockSpec((blk, outs), lambda i, rows: (rows[jnp.minimum(i, near - 1)], 0)),
+                pl.BlockSpec((blk, outs), lambda i, rows: (rows[jnp.maximum(i, near)], 0)),
+                pl.BlockSpec((RANK, blk), lambda i, rows: (0, rows[i])),
+            ],
+            out_specs=pl.BlockSpec((RANK, outs), lambda i, rows: (0, 0)),
+        ),
         out_shape=jax.ShapeDtypeStruct((RANK, outs), F32),
         compiler_params=params(48),
         cost_estimate=cost(8e9, error.size * 4),
-        name="right_error",
-    )(error, basis_t)
+        name="right_rows",
+    )(rows, merged, error, basis_t)
 
 
 def piece_specs(pieces, blk):
@@ -275,13 +293,41 @@
     )(rows, basis_t, right_e, out_grad, *pieces)
 
 
-def update_kernel(*refs, ranges, n_dp, scale):
-    e_ref, b_ref, g_ref, q_ref = refs[1:5]
-    x_refs = refs[5 : 5 + len(ranges)]
-    out, qt_out, qs = refs[5 + len(ranges) :]
+def merge_kernel(*refs, ranges, scale, kept):
+    e_ref, g_ref = refs[1 + kept : 3 + kept]
+    x_refs, out = refs[3 + kept : -1], refs[-1]
     i = pl.program_id(0)
-
-    @pl.when(i == 0)
+    for x_ref, (lo, hi) in zip(x_refs, ranges):
+
+        @pl.when((i >= lo) & (i < hi))
+        def _(x_ref=x_ref):
+            out[...] = e_ref[...] + dot(x_ref[...], g_ref[...], 1, 0) * scale
+
+
+def merge(rows, kept, error, out_grad, pieces, blk, scale):
+    tok, outs = out_grad.shape
+    specs, ranges = piece_specs(pieces, blk)
+    block = pl.BlockSpec((blk, outs), lambda i, rows: (rows[i], 0))
+    return pl.pallas_call(
+        functools.partial(merge_kernel, ranges=ranges, scale=scale, kept=len(kept)),
+        grid_spec=pltpu.PrefetchScalarGridSpec(
+            num_scalar_prefetch=1,
+            grid=(ranges[-1][1],),
+            in_specs=[pl.BlockSpec(memory_space=pl.ANY)] * len(kept)
+            + [block, pl.BlockSpec((tok, outs), lambda i, rows: (0, 0))]
+            + specs,
+            out_specs=block,
+        ),
+        out_shape=jax.ShapeDtypeStruct(error.shape, F32),
+        input_output_aliases={1: 0} if kept else {},
+        compiler_params=params(48),
+        cost_estimate=cost(5e9, error.size * 4, 2),
+        name="merge",
+    )(rows, *kept, error, out_grad, *pieces)
+
+
+def update_kernel(m_ref, b_ref, q_ref, out, qt_out, qs, *, n_dp):
+    @pl.when(pl.program_id(0) == 0)
     def _():
         q_t = jnp.concatenate([q_ref[k] for k in range(n_dp)], axis=1) * (1.0 / n_dp)
         qt_out[...] = q_t
@@ -291,47 +337,32 @@
         qs[2 * RANK : 3 * RANK, :] = high
 
     bh, bl = split(b_ref[...].T)
-    both = jnp.concatenate([bh, bh, bl], axis=1)
-    for x_ref, (lo, hi) in zip(x_refs, ranges):
-
-        @pl.when((i >= lo) & (i < hi))
-        def _(x_ref=x_ref):
-            out[...] = (
-                e_ref[...]
-                + dot(x_ref[...], g_ref[...], 1, 0) * scale
-                - dot(both, qs[...], 1, 0)
-            )
-
-
-def update_error(rows, error, basis_t, out_grad, pieces, blk, q_pieces, n_dp, scale):
-    tok, outs = out_grad.shape
-    specs, ranges = piece_specs(pieces, blk)
-    return pl.pallas_call(
-        functools.partial(update_kernel, ranges=ranges, n_dp=n_dp, scale=scale),
-        grid_spec=pltpu.PrefetchScalarGridSpec(
-            num_scalar_prefetch=1,
-            grid=(ranges[-1][1],),
-            in_specs=[
-                pl.BlockSpec((blk, outs), lambda i, rows: (rows[i], 0)),
-                pl.BlockSpec((RANK, blk), lambda i, rows: (0, rows[i])),
-                pl.BlockSpec((tok, outs), lambda i, rows: (0, 0)),
-                pl.BlockSpec(q_pieces.shape, lambda i, rows: (0, 0, 0)),
-            ]
-            + specs,
-            out_specs=[
-                pl.BlockSpec((blk, outs), lambda i, rows: (rows[i], 0)),
-                pl.BlockSpec((RANK, outs), lambda i, rows: (0, 0)),
-            ],
-            scratch_shapes=[pltpu.VMEM((3 * RANK, outs), BF16)],
-        ),
+    out[...] = m_ref[...] - dot(jnp.concatenate([bh, bh, bl], axis=1), qs[...], 1, 0)
+
+
+def update_error(merged, basis_t, q_pieces, n_dp):
+    din, outs = merged.shape
+    blk = 512
+    block = pl.BlockSpec((blk, outs), lambda i: (i, 0))
+    return pl.pallas_call(
+        functools.partial(update_kernel, n_dp=n_dp),
+        grid=(din // blk,),
+        in_specs=[
+            block,
+            pl.BlockSpec((RANK, blk), lambda i: (0, i)),
+            pl.BlockSpec(q_pieces.shape, lambda i: (0, 0, 0)),
+        ],
+        out_specs=[block, pl.BlockSpec((RANK, outs), lambda i: (0, 0))],
         out_shape=[
-            jax.ShapeDtypeStruct(error.shape, F32),
+            jax.ShapeDtypeStruct(merged.shape, F32),
             jax.ShapeDtypeStruct((RANK, outs), F32),
         ],
-        compiler_params=params(48),
-        cost_estimate=cost(9e9, error.size * 8 + basis_t.shape[1] * tok * 2),
+        scratch_shapes=[pltpu.VMEM((3 * RANK, outs), BF16)],
+        input_output_aliases={0: 0},
+        compiler_params=params(48),
+        cost_estimate=cost(2e9, merged.size * 8),
         name="update_error",
-    )(rows, error, basis_t, out_grad, q_pieces, *pieces)
+    )(merged, basis_t, q_pieces)
 
 
 def near_kernel(ids, g_ref, gs_ref, w_ref, ws_ref, out):
@@ -359,7 +390,7 @@
         ),
         out_shape=jax.ShapeDtypeStruct((tok, part), F32),
         compiler_params=params(48),
-        cost_estimate=cost(4 * tok * outs * part, 12e6),
+        cost_estimate=cost(4 * tok * outs * part, 12e6, 2),
         name="input_grad_near",
     )(jnp.reshape(me_t, (1,)), g_own, g_sib, weight, w_sib)
 
@@ -429,44 +460,59 @@
     def everywhere(a, axes, n):
         return exchange(jnp.broadcast_to(a, (n, *a.shape)), axes)
 
+    y_t = project(out_grad, q_t)
+    y_t = y_t + to_sibling(y_t)
+    y_list = [y_t] + [to_chip(y_t, k) for k in steps]
+
     moves = [(k, e) for k in steps for e in range(2)]
     w_parts = []
     for k, e in moves:
         dest = ((y + k) % chips) * 2 + (c ^ e)
         w_parts.append(lax.dynamic_slice(weight, (dest * part + d * share, 0), (share, outs)))
+    w_parts = after(w_parts, y_t)
     x_t = after(activations, *w_parts).T
     w_parts = [to_chip(a, k, e) for a, (k, e) in zip(w_parts, moves)]
-    blk = min(512, part)
-    per = part // blk
-    x_far = [[to_chip(x_t[j * blk : (j + 1) * blk], k) for k in steps] for j in range(per)]
-
-    y_t = project(out_grad, after(q_t, x_t))
-    y_t = y_t + to_sibling(y_t)
-    y_list = [y_t] + [to_chip(y_t, k) for k in steps]
-    send, keep = local_sketch(c, error, after(q_t, y_t), n_dp, chips, part)
+    tall = min(512, part)
+    short = part // 4
+    starts = [0, short, 3 * short, part]
+    x_rows = [x_t[lo:hi] for lo, hi in zip(starts[:-1], starts[1:])]
+    x_far = [[to_chip(a, k) for k in steps] for a in x_rows]
+
+    send, keep = local_sketch(c, error, after(q_t, *x_rows), n_dp, chips, part)
     w_parts = jnp.concatenate([after(a, send) for a in w_parts], axis=1)
-    blocks = sketch_rows(y, keep, to_sibling(send), activations, after(y_list, w_parts), scale)
+    y_list, x_far[0] = after((y_list, x_far[0]), w_parts)
+    blocks = sketch_rows(y, keep, to_sibling(send), activations, y_list, scale)
     w_far = lax.all_gather(w_parts, "dp", axis=0, tiled=True)
 
     g_sib = to_sibling(out_grad)
     w_sib = to_sibling(lax.dynamic_slice(after(weight, send), ((t ^ 1) * part, 0), (part, outs)))
     grad = near_input_grad(t, out_grad, g_sib, weight, after(w_sib, blocks))
-
-    blocks = exchange(blocks.reshape(n, RANK, share), spread)
-    x_far[0] = after(x_far[0], grad)
-    mine = everywhere(after(jnp.sum(blocks, axis=0), x_far[0]), spread, n)
-    basis_t = make_basis(c, mine, to_sibling(mine), n_dp, chips, part, din)
-    right_e = right_error(error, basis_t)
-
-    pieces = [x_t, to_sibling(x_t)]
-    rows = [(2 * y + (c ^ e)) * per + j for e in range(2) for j in range(per)]
-    for j in range(per):
-        if j > 0:
-            x_far[j] = after(x_far[j], right_e)
-        for k, a in zip(steps, x_far[j]):
+    blocks = after(blocks, x_far[0])
+    blocks = after(exchange(blocks.reshape(n, RANK, share), spread), grad)
+    piece = jnp.sum(blocks, axis=0)
+
+    per = part // tall
+    rows_near = [(2 * y + (c ^ e)) * per + j for e in range(2) for j in range(per)]
+    rows_all = list(rows_near)
+    for k in steps:
+        rows_all += [(2 * ((y - k) % chips) + e) * per + j for e in range(2) for j in range(per)]
+    rows_near = jnp.stack(rows_near).astype(jnp.int32)
+    rows_all = jnp.stack(rows_all).astype(jnp.int32)
+    x_near = [x_t, to_sibling(x_t)]
+    merged = merge(rows_near, [], error, out_grad, after(x_near, piece), tall, scale)
+
+    mine = everywhere(after(piece, x_far[1]), spread, n)
+    basis_t = make_basis(c, after(mine, merged), to_sibling(mine), n_dp, chips, part, din)
+    right_e = right_rows(rows_all, 2 * per, merged, error, basis_t, tall)
+
+    pieces, rows = [], []
+    for j in range(3):
+        a = after(x_far[j], right_e if j == 2 else mine)
+        for k, a in zip(steps, a):
             for e in range(2):
                 pieces.append(to_sibling(a) if e else a)
-                rows.append((2 * ((y - k) % chips) + (c ^ e)) * per + j)
+                base = (2 * ((y - k) % chips) + (c ^ e)) * 4 + starts[j] // short
+                rows += [base + i for i in range((starts[j + 1] - starts[j]) // short)]
     rows = jnp.stack(rows).astype(jnp.int32)
 
     n_chunk = 2
@@ -476,23 +522,16 @@
         g = after(out_grad, mine if i == 0 else right_e)[i * span : (i + 1) * span]
         g_far.append([to_chip(g, k) for k in steps])
 
-    def far(grad, i):
+    right = right_grad(rows, basis_t, right_e, out_grad, pieces, short, n_dp, scale)
+    merged = merge(rows, [merged], error, after(out_grad, right), pieces, short, scale)
+    right = jnp.sum(after(exchange(right, "dp"), merged), axis=0)
+    q_pieces = everywhere(right, "dp", n_dp)
+    new_error, q_t = update_error(merged, basis_t, q_pieces, n_dp)
+    for i in range(n_chunk):
         gs = []
-        for a in g_far[i]:
+        for a in after(g_far[i], right if i == 0 else q_t):
             gs += [a, to_sibling(a)]
-        return far_input_grad(grad, w_far, gs, i * span)
-
-    right = right_grad(rows, basis_t, right_e, out_grad, pieces, blk, n_dp, scale)
-    right = jnp.sum(exchange(right, "dp"), axis=0)
-    g_far[0] = after(g_far[0], right)
-    q_pieces = everywhere(after(right, g_far[0]), "dp", n_dp)
-    new_error, q_t = update_error(
-        rows, error, basis_t, out_grad, pieces, blk, q_pieces, n_dp, scale
-    )
-    for i in range(n_chunk):
-        if i > 0:
-            g_far[i] = after(g_far[i], q_t)
-        grad = far(grad, i)
+        grad = far_input_grad(after(grad, q_t), w_far, gs, i * span)
     return (grad, new_error[None], q_t.T)
 
 

time: 217 us -> 216 us (level)
  blocking collectives: 30.1 us -> 0 us
  Pallas kernels: 80.2 us -> 97.3 us
  starting transfers between devices: 21.3 us -> 38.1 us
  waiting for transfers between devices: 52.6 us -> 46.6 us
    all_to_all x2 -> x0, blocking collectives: 30.1 us -> none  [exchange(): return lax.all_to_all(a, axes, 0, 0, tiled=True)]
    pallas_call x2 -> x4, Pallas kernels: 32.2 us -> 50.4 us  [the longest x2 24.1 us: merge(): pl.pallas_call(functools.partial(merge_kernel, ranges=ranges, scale=scale...]
    ppermute x7 -> x8, waiting for transfers between devices: 30.6 us -> 15.4 us  [to_chip(): return lax.ppermute(a, ('chip', 'core'), pairs)]
    all_to_all x2 -> x4, starting transfers between devices: 10.6 us -> 25.5 us  [exchange(): return lax.all_to_all(a, axes, 0, 0, tiled=True)]
    all_to_all x2 -> x4, waiting for transfers between devices: 19.4 us -> 31 us  [exchange(): return lax.all_to_all(a, axes, 0, 0, tiled=True)]
    slice x1 -> x2, local copies, waits for them, and re-layouts: 1.53 us -> 4.53 us  [per_device(): x_rows = [x_t[lo:hi] for lo, hi in zip(starts[:-1], starts[1:])]]
    ppermute x10 -> x11, waiting for transfers between devices: 2.58 us -> 0.13 us  [to_sibling(): return lax.ppermute(a, 'core', [(0, 1), (1, 0)])]
    ppermute x7 -> x8, starting transfers between devices: 9.01 us -> 10.2 us  [to_chip(): return lax.ppermute(a, ('chip', 'core'), pairs)]
  transfers between devices with their start and end apart: 20 -> 24, of which waited for: 6 -> 6; matrix products, arithmetic and copies ran while one was open for 6% -> 4% of each run, Pallas kernels for 34% -> 42%
where the time goes in v4:
time: 216 us; the launch traced here: 215 us
  Pallas kernels  97.3 us (45%)
  waiting for transfers between devices  46.6 us (22%)
  starting transfers between devices  38.1 us (18%)
  local copies, waits for them, and re-layouts  18.5 us (9%)
  between operations  14.3 us (7%)
    all_to_all x4, waiting for transfers between devices, exchange(): return lax.all_to_all(a, axes, 0, 0, tiled=True)  31 us
    all_to_all x4, starting transfers between devices, exchange(): return lax.all_to_all(a, axes, 0, 0, tiled=True)  25.5 us
    pallas_call x2, Pallas kernels, merge(): pl.pallas_call(functools.partial(merge_kernel, ranges=ranges, scale=scale...  24.1 us
    pallas_call x1, Pallas kernels, update_error(): pl.pallas_call(functools.partial(update_kernel, n_dp=n_dp), grid=(din //...  15.8 us
    ppermute x8, waiting for transfers between devices, to_chip(): return lax.ppermute(a, ('chip', 'core'), pairs)  15.4 us
    pallas_call x2, Pallas kernels, far_input_grad(): pl.pallas_call(far_kernel, grid=(part // blk,), in_specs=[to, pl.BlockSpe...  12.6 us
    pallas_call x1, Pallas kernels, local_sketch(): pl.pallas_call(functools.partial(sketch_kernel, width=width), grid_spec=p...  11.4 us
    pallas_call x1, Pallas kernels, right_rows(): pl.pallas_call(functools.partial(right_rows_kernel, near=near), grid_spec...  10.5 us
  transfers between devices with their start and end apart: 24, of which 6 were waited for; matrix products, arithmetic and copies ran while one was open for 4% of the time, Pallas kernels for 42%

profile of v4, /device:TPU:0, one launch (start us, length us, event | category | flops | bytes accessed | tf_op | source)
XLA Modules:
  0.0 214.8 jit_solution(11083785184987675370)
XLA Ops:
  12.1 2.6 %copy.12 = bf16[1024,1024]{0,1:T(8,128)(2,1)} copy(bf16[1024,1024]{1,0:T(8,128)(2,1)S(1)} %copy-done.2) | data formatting | bytes 4194304 | tf_op jit(solution)/shard_map/optimization_barrier | solution.py:428
  14.7 2.3 %fusion = (bf16[256,1024]{1,0:T(8,128)(2,1)}, bf16[256,1024]{1,0:T(8,128)(2,1)}) fusion(bf16[1024,1024]{1,0:T(8,128)(2,1)} %bitcast.4.refs_3_), kind=kLoop, calls=%fused_computation.6 | loop fusion | bytes 2097152 | tf_op jit(solution)/shard_map/slice | solution.py:478
  16.9 2.3 %slice.21 = bf16[512,1024]{1,0:T(8,128)(2,1)} slice(bf16[1024,1024]{1,0:T(8,128)(2,1)} %bitcast.4.refs_3_), slice={[256:768], [0:1024]} | slice | bytes 2097152 | tf_op jit(solution)/shard_map/slice | solution.py:478
  19.2 2.8 %collective-permute-start.6 = (bf16[128,1024]{1,0:T(8,128)(2,1)S(1)}, bf16[128,1024]{1,0:T(8,128)(2,1)S(1)}, u32[]{:S(2)}, u32[]{:S(2)}) collective-permute-start(bf16[128,1024]{1,0:T(8,128)(2,1)S(1)} %get-tuple-element.35), channel_id=1, source_target_pairs={{0,2},{1,3},{2,0},{3,1},{4,6},{5,7},{6,4},{7,5},{8,10},{9,11},{10,... | collective-permute-start | bytes 786440 | tf_op jit(solution)/shard_map/ppermute | solution.py:455
  22.0 11.4 %error_sketch.1 = (f32[8,2,32,128]{3,2,1,0:T(8,128)S(1)}, f32[8,2,32,128]{3,2,1,0:T(8,128)S(1)}) custom-call(s32[1]{0:T(128)} %bitcast.1.ids.core, f32[4096,1024]{1,0:T(8,128)} %bitcast.28, f32[32,1024]{1,0:T(8,128)S(1)} %bitcast.26), custom_call_target="tpu_custom_call" | custom-call | flops 12000000000 | bytes 33554432 | tf_op jit(solution)/shard_map/error_sketch/pallas_call | solution.py:98
  34.8 3.2 %constant_dynamic-slice_fusion = bf16[1024,1024]{1,0:T(8,128)(2,1)} fusion(bf16[4096,1024]{1,0:T(8,128)(2,1)} %w_ref.1, s32[]{:T(128)S(6)} %select_n.43), kind=kLoop, calls=%fused_computation.2 | loop fusion | bytes 4194308 | tf_op jit(solution)/shard_map/dynamic_slice | solution.py:488
  40.8 14.9 %collective-permute-done.4.refs_5_ = f32[32,1024]{1,0:T(8,128)S(1)} collective-permute-done((f32[32,1024]{1,0:T(8,128)S(1)}, f32[32,1024]{1,0:T(8,128)S(1)}, u32[]{:S(2)}, u32[]{:S(2)}) %collective-permute-start.4) | collective-permute-done | bytes 131104 | tf_op jit(solution)/shard_map/ppermute | solution.py:455
  58.4 6.8 %all-to-all-start = ((f32[16,32,128]{2,1,0:T(8,128)}), f32[16,32,128]{2,1,0:T(8,128)S(1)}, u32[]{:S(2)}, u32[]{:S(2)}) async-start(f32[16,32,128]{2,1,0:T(8,128)} %bitcast.18), calls=%async_computation | async-start | bytes 524288 | tf_op jit(solution)/shard_map/all_to_all | solution.py:458
  65.2 8.5 %input_grad_near.1.refs_0_ = f32[1024,1024]{1,0:T(8,128)} custom-call(s32[1]{0:T(128)} %bitcast.ids, bf16[1024,1024]{1,0:T(8,128)(2,1)S(1)} %copy-done.1, bf16[1024,1024]{1,0:T(8,128)(2,1)} %collective-permute-done.gs_ref, bf16[4096,1024]{1,0:T(8,128)(2,1)} %w_ref.1, bf16[1024,1024]{1,0:T(8,128)(2,1)} %collective-permute-done.2.ws_ref), custom_call_target="tpu_custom_call" | custom-call | flops 8589934592 | bytes 24000000 | tf_op jit(solution)/shard_map/input_grad_near/pallas_call | solution.py:378
  73.8 10.5 %all-to-all-done = f32[16,32,128]{2,1,0:T(8,128)S(1)} async-done(((f32[16,32,128]{2,1,0:T(8,128)}), f32[16,32,128]{2,1,0:T(8,128)S(1)}, u32[]{:S(2)}, u32[]{:S(2)}) %all-to-all-start) | async-done | bytes 262176 | tf_op jit(solution)/shard_map/all_to_all | solution.py:458
  85.1 6.8 %all-to-all-start.1 = ((f32[16,32,128]{2,1,0:T(8,128)}), f32[16,32,128]{2,1,0:T(8,128)S(1)}, u32[]{:S(2)}, u32[]{:S(2)}) async-start(f32[16,32,128]{2,1,0:T(8,128)} %broadcast_in_dim.9), calls=%async_computation.1 | async-start | bytes 524288 | tf_op jit(solution)/shard_map/all_to_all | solution.py:458
  92.0 1.9 collective-permute-start.13
  93.9 13.2 %all-to-all-done.1.mine = f32[16,32,128]{2,1,0:T(8,128)S(1)} async-done(((f32[16,32,128]{2,1,0:T(8,128)}), f32[16,32,128]{2,1,0:T(8,128)S(1)}, u32[]{:S(2)}, u32[]{:S(2)}) %all-to-all-start.1) | async-done | bytes 262176 | tf_op jit(solution)/shard_map/all_to_all | solution.py:458
  107.6 10.7 %merge.2.m_ref.refs_1_ = f32[4096,1024]{1,0:T(8,128)} custom-call(s32[4]{0:T(128)S(1)} %pad_add_fusion.refs_0_, f32[4096,1024]{1,0:T(8,128)} %bitcast.29, bf16[1024,1024]{1,0:T(8,128)(2,1)S(1)} %copy-done.1, bf16[1024,1024]{1,0:T(8,128)(2,1)} %bitcast.4.refs_3_, bf16[1024,1024]{1,0:T(8,128)(2,1)} %collective-permute-done.8.refs_4_), custom_call_target="tpu_custom_call" | custom-call | flops 10000000000 | bytes 33554432 | tf_op jit(solution)/shard_map/merge/pallas_call | solution.py:311
  118.3 4.5 %basis.1.b_ref.refs_1_ = f32[32,4096]{1,0:T(8,128)S(1)} custom-call(s32[1]{0:T(128)} %bitcast.1.ids.core, f32[16,32,128]{2,1,0:T(8,128)S(1)} %all-to-all-done.1.mine, f32[16,32,128]{2,1,0:T(8,128)S(1)} %collective-permute-done.10.other), custom_call_target="tpu_custom_call" | custom-call | flops 6000000 | bytes 2000 | tf_op jit(solution)/shard_map/basis/pallas_call | solution.py:173
  122.9 10.5 %right_rows.1.refs_2_ = f32[32,1024]{1,0:T(8,128)S(1)} custom-call(s32[8]{0:T(128)S(1)} %stack.79.rows, f32[4096,1024]{1,0:T(8,128)} %merge.2.m_ref.refs_1_, f32[4096,1024]{1,0:T(8,128)} %bitcast.30, f32[32,4096]{1,0:T(8,128)S(1)} %basis.1.b_ref.refs_1_), custom_call_target="tpu_custom_call" | custom-call | flops 8000000 | bytes 16777 | tf_op jit(solution)/shard_map/right_rows/pallas_call | solution.py:211
  138.2 7.8 %right_grad.1 = f32[8,32,128]{2,1,0:T(8,128)} custom-call(s32[8]{0:T(128)S(1)} %stack.69.refs_0_, f32[32,4096]{1,0:T(8,128)S(1)} %basis.1.b_ref.refs_1_, f32[32,1024]{1,0:T(8,128)S(1)} %right_rows.1.refs_2_, bf16[1024,1024]{1,0:T(8,128)(2,1)} %refs_3_.4, bf16[256,1024]{1,0:T(8,128)(2,1)S(1)} %collective-permute-done.5.refs_4_, ...), custom_call_target="tpu_custom_call" | custom-call | flops 4000000 | bytes 8388 | tf_op jit(solution)/shard_map/right_grad/pallas_call | solution.py:275
  146.0 6.0 %all-to-all-start.2 = ((f32[8,32,128]{2,1,0:T(8,128)}), f32[8,32,128]{2,1,0:T(8,128)S(1)}, u32[]{:S(2)}, u32[]{:S(2)}) async-start(f32[8,32,128]{2,1,0:T(8,128)} %right_grad.1), calls=%async_computation.2 | async-start | bytes 262144 | tf_op jit(solution)/shard_map/all_to_all | solution.py:458
  152.0 13.4 %merge.3.m_ref = f32[4096,1024]{1,0:T(8,128)} custom-call(s32[8]{0:T(128)S(1)} %stack.69.refs_0_, f32[4096,1024]{1,0:T(8,128)} %merge.2.m_ref.refs_1_, f32[4096,1024]{1,0:T(8,128)} %bitcast.31, bf16[1024,1024]{1,0:T(8,128)(2,1)} %refs_3_.4, bf16[256,1024]{1,0:T(8,128)(2,1)S(1)} %collective-permute-done.5.refs_4_, ...), custom_call_target="tpu_custom_call", output_to_operand_aliasing={{}: (1, {})} | custom-call | flops 10000000000 | bytes 33554432 | tf_op jit(solution)/shard_map/merge/pallas_call | solution.py:311
  166.1 6.0 %all-to-all-start.3 = ((f32[8,32,128]{2,1,0:T(8,128)}), f32[8,32,128]{2,1,0:T(8,128)S(1)}, u32[]{:S(2)}, u32[]{:S(2)}) async-start(f32[8,32,128]{2,1,0:T(8,128)} %broadcast_in_dim.10), calls=%async_computation.3 | async-start | bytes 262144 | tf_op jit(solution)/shard_map/all_to_all | solution.py:458
  172.2 7.3 %all-to-all-done.3.q_ref = f32[8,32,128]{2,1,0:T(8,128)S(1)} async-done(((f32[8,32,128]{2,1,0:T(8,128)}), f32[8,32,128]{2,1,0:T(8,128)S(1)}, u32[]{:S(2)}, u32[]{:S(2)}) %all-to-all-start.3) | async-done | bytes 131104 | tf_op jit(solution)/shard_map/all_to_all | solution.py:458
  179.5 15.8 %update_error.1 = (f32[4096,1024]{1,0:T(8,128)}, f32[32,1024]{1,0:T(8,128)}) custom-call(f32[4096,1024]{1,0:T(8,128)} %merge.3.m_ref, f32[32,4096]{1,0:T(8,128)S(1)} %basis.1.b_ref.refs_1_, f32[8,32,128]{2,1,0:T(8,128)S(1)} %all-to-all-done.3.q_ref), custom_call_target="tpu_custom_call", output_to_operand_aliasing={{0}: (0, {})} | custom-call | flops 2000000 | bytes 33554 | tf_op jit(solution)/shard_map/update_error/pallas_call | solution.py:347
  195.3 6.5 %input_grad_far.2.refs_0_ = f32[1024,1024]{1,0:T(8,128)} custom-call(f32[1024,1024]{1,0:T(8,128)} %input_grad_near.1.refs_0_, bf16[1024,2048]{1,0:T(8,128)(2,1)} %all-gather.2.cloned.1.call-done.refs_1_, bf16[512,1024]{1,0:T(8,128)(2,1)} %collective-permute-done.15.refs_2_, ...), custom_call_target="tpu_custom_call", output_to_operand_aliasing={{}: (0, {})} | custom-call | flops 2147483 | bytes 10000 | tf_op jit(solution)/shard_map/input_grad_far/pallas_call | solution.py:413
  201.8 6.2 %input_grad_far.3 = f32[1024,1024]{1,0:T(8,128)} custom-call(f32[1024,1024]{1,0:T(8,128)} %input_grad_far.2.refs_0_, bf16[1024,2048]{1,0:T(8,128)(2,1)} %all-gather.2.cloned.1.call-done.refs_1_, bf16[512,1024]{1,0:T(8,128)(2,1)S(1)} %collective-permute-done.17.refs_2_, ...), custom_call_target="tpu_custom_call", output_to_operand_aliasing={{}: (0, {})} | custom-call | flops 2147483 | bytes 10000 | tf_op jit(solution)/shard_map/input_grad_far/pallas_call | solution.py:413
  (70 shorter events, 18.7 us)
Async XLA Ops:
  7.2 188.1 %all-gather.2.cloned.1.call-start = ((), (), s32[]{:S(2)}) async-start(), calls=%async_computation.4 | async-start | bytes 4718592 | tf_op jit(solution)/shard_map/all_gather | solution.py:485
  10.4 1.5 collective-permute-start.1
  19.2 14.2 %collective-permute-start.6 = (bf16[128,1024]{1,0:T(8,128)(2,1)S(1)}, bf16[128,1024]{1,0:T(8,128)(2,1)S(1)}, u32[]{:S(2)}, u32[]{:S(2)}) collective-permute-start(bf16[128,1024]{1,0:T(8,128)(2,1)S(1)} %get-tuple-element.35), channel_id=1, source_target_pairs={{0,2},{1,3},{2,0},{3,1},{4,6},{5,7},{6,4},{7,5},{8,10},{9,11},{10,... | collective-permute-start | bytes 786440 | tf_op jit(solution)/shard_map/ppermute | solution.py:455
  22.0 12.0 %collective-permute-start.7 = (bf16[128,1024]{1,0:T(8,128)(2,1)S(1)}, bf16[128,1024]{1,0:T(8,128)(2,1)S(1)}, u32[]{:S(2)}, u32[]{:S(2)}) collective-permute-start(bf16[128,1024]{1,0:T(8,128)(2,1)S(1)} %get-tuple-element.36), channel_id=1, source_target_pairs={{0,3},{1,2},{2,1},{3,0},{4,7},{5,6},{6,5},{7,4},{8,11},{9,10},{10,... | collective-permute-start | bytes 786440 | tf_op jit(solution)/shard_map/ppermute | solution.py:455
  38.0 27.2 %collective-permute-start.2 = (bf16[1024,1024]{1,0:T(8,128)(2,1)}, bf16[1024,1024]{1,0:T(8,128)(2,1)}, u32[]{:S(2)}, u32[]{:S(2)}) collective-permute-start(bf16[1024,1024]{1,0:T(8,128)(2,1)} %constant_dynamic-slice_fusion), channel_id=1, source_target_pairs={{0,1},{1,0},{2,3},{3,2},{4,5},{5,4},{6,7},{7,6},{8,9},{9,8},{10,11... | collective-permute-start | bytes 6291464 | tf_op jit(solution)/shard_map/ppermute | solution.py:451
  38.2 27.0 %collective-permute-start = (bf16[1024,1024]{1,0:T(8,128)(2,1)S(1)}, bf16[1024,1024]{1,0:T(8,128)(2,1)}, u32[]{:S(2)}, u32[]{:S(2)}) collective-permute-start(bf16[1024,1024]{1,0:T(8,128)(2,1)S(1)} %copy-done.1), channel_id=1, source_target_pairs={{0,1},{1,0},{2,3},{3,2},{4,5},{5,4},{6,7},{7,6},{8,9},{9,8},{10,11... | collective-permute-start | bytes 6291464 | tf_op jit(solution)/shard_map/ppermute | solution.py:451
  38.5 55.4 %collective-permute-start.8 = (bf16[1024,1024]{1,0:T(8,128)(2,1)}, bf16[1024,1024]{1,0:T(8,128)(2,1)}, u32[]{:S(2)}, u32[]{:S(2)}) collective-permute-start(bf16[1024,1024]{1,0:T(8,128)(2,1)} %bitcast.4.refs_3_), channel_id=1, source_target_pairs={{0,1},{1,0},{2,3},{3,2},{4,5},{5,4},{6,7},{7,6},{8,9},{9,8},{10,11... | collective-permute-start | bytes 6291464 | tf_op jit(solution)/shard_map/ppermute | solution.py:451
  38.7 17.0 %collective-permute-start.5 = (bf16[256,1024]{1,0:T(8,128)(2,1)S(1)}, bf16[256,1024]{1,0:T(8,128)(2,1)S(1)}, u32[]{:S(2)}, u32[]{:S(2)}) collective-permute-start(bf16[256,1024]{1,0:T(8,128)(2,1)S(1)} %copy-done.7), channel_id=1, source_target_pairs={{0,2},{1,3},{2,0},{3,1},{4,6},{5,7},{6,4},{7,5},{8,10},{9,11},{10,... | collective-permute-start | bytes 1572872 | tf_op jit(solution)/shard_map/ppermute | solution.py:455
  40.5 15.2 %collective-permute-start.4 = (f32[32,1024]{1,0:T(8,128)S(1)}, f32[32,1024]{1,0:T(8,128)S(1)}, u32[]{:S(2)}, u32[]{:S(2)}) collective-permute-start(f32[32,1024]{1,0:T(8,128)S(1)} %add.112.refs_4_), channel_id=1, source_target_pairs={{0,2},{1,3},{2,0},{3,1},{4,6},{5,7},{6,4},{7,5},{8,10},{9,11},{10,... | collective-permute-start | bytes 393224 | tf_op jit(solution)/shard_map/ppermute | solution.py:455
  55.7 1.5 collective-permute-start.3
  55.7 28.6 %collective-permute-start.9 = (bf16[512,1024]{1,0:T(8,128)(2,1)}, bf16[512,1024]{1,0:T(8,128)(2,1)}, u32[]{:S(2)}, u32[]{:S(2)}) collective-permute-start(bf16[512,1024]{1,0:T(8,128)(2,1)} %slice.21), channel_id=1, source_target_pairs={{0,2},{1,3},{2,0},{3,1},{4,6},{5,7},{6,4},{7,5},{8,10},{9,11},{10,... | collective-permute-start | bytes 3145736 | tf_op jit(solution)/shard_map/ppermute | solution.py:455
  58.4 25.9 %all-to-all-start = ((f32[16,32,128]{2,1,0:T(8,128)}), f32[16,32,128]{2,1,0:T(8,128)S(1)}, u32[]{:S(2)}, u32[]{:S(2)}) async-start(f32[16,32,128]{2,1,0:T(8,128)} %bitcast.18), calls=%async_computation | async-start | bytes 524288 | tf_op jit(solution)/shard_map/all_to_all | solution.py:458
  85.1 22.1 %all-to-all-start.1 = ((f32[16,32,128]{2,1,0:T(8,128)}), f32[16,32,128]{2,1,0:T(8,128)S(1)}, u32[]{:S(2)}, u32[]{:S(2)}) async-start(f32[16,32,128]{2,1,0:T(8,128)} %broadcast_in_dim.9), calls=%async_computation.1 | async-start | bytes 524288 | tf_op jit(solution)/shard_map/all_to_all | solution.py:458
  92.0 41.4 %collective-permute-start.13 = (bf16[256,1024]{1,0:T(8,128)(2,1)}, bf16[256,1024]{1,0:T(8,128)(2,1)}, u32[]{:S(2)}, u32[]{:S(2)}) collective-permute-start(bf16[256,1024]{1,0:T(8,128)(2,1)} %get-tuple-element.69), channel_id=1, source_target_pairs={{0,2},{1,3},{2,0},{3,1},{4,6},{5,7},{6,4},{7,5},{8,10},{9,11},{10,... | collective-permute-start | bytes 1572872 | tf_op jit(solution)/shard_map/ppermute | solution.py:455
  107.1 31.1 %collective-permute-start.12 = (bf16[512,1024]{1,0:T(8,128)(2,1)}, bf16[512,1024]{1,0:T(8,128)(2,1)}, u32[]{:S(2)}, u32[]{:S(2)}) collective-permute-start(bf16[512,1024]{1,0:T(8,128)(2,1)} %collective-permute-done.9.refs_6_), channel_id=1, source_target_pairs={{0,1},{1,0},{2,3},{3,2},{4,5},{5,4},{6,7},{7,6},{8,9},{9,8},{10,11... | collective-permute-start | bytes 3145736 | tf_op jit(solution)/shard_map/ppermute | solution.py:451
  107.1 11.2 %collective-permute-start.10 = (f32[16,32,128]{2,1,0:T(8,128)S(1)}, f32[16,32,128]{2,1,0:T(8,128)S(1)}, u32[]{:S(2)}, u32[]{:S(2)}) collective-permute-start(f32[16,32,128]{2,1,0:T(8,128)S(1)} %all-to-all-done.1.mine), channel_id=1, source_target_pairs={{0,1},{1,0},{2,3},{3,2},{4,5},{5,4},{6,7},{7,6},{8,9},{9,8},{10,11... | collective-permute-start | bytes 786440 | tf_op jit(solution)/shard_map/ppermute | solution.py:451
  118.3 19.9 %collective-permute-start.11 = (bf16[256,1024]{1,0:T(8,128)(2,1)S(1)}, bf16[256,1024]{1,0:T(8,128)(2,1)}, u32[]{:S(2)}, u32[]{:S(2)}) collective-permute-start(bf16[256,1024]{1,0:T(8,128)(2,1)S(1)} %collective-permute-done.5.refs_4_), channel_id=1, source_target_pairs={{0,1},{1,0},{2,3},{3,2},{4,5},{5,4},{6,7},{7,6},{8,9},{9,8},{10,11... | collective-permute-start | bytes 1572872 | tf_op jit(solution)/shard_map/ppermute | solution.py:451
  133.4 4.8 %collective-permute-start.14 = (bf16[256,1024]{1,0:T(8,128)(2,1)}, bf16[256,1024]{1,0:T(8,128)(2,1)}, u32[]{:S(2)}, u32[]{:S(2)}) collective-permute-start(bf16[256,1024]{1,0:T(8,128)(2,1)} %collective-permute-done.13.refs_8_), channel_id=1, source_target_pairs={{0,1},{1,0},{2,3},{3,2},{4,5},{5,4},{6,7},{7,6},{8,9},{9,8},{10,11... | collective-permute-start | bytes 1572872 | tf_op jit(solution)/shard_map/ppermute | solution.py:451
  135.1 37.0 %collective-permute-start.15 = (bf16[512,1024]{1,0:T(8,128)(2,1)}, bf16[512,1024]{1,0:T(8,128)(2,1)}, u32[]{:S(2)}, u32[]{:S(2)}) collective-permute-start(bf16[512,1024]{1,0:T(8,128)(2,1)} %slice.18), channel_id=1, source_target_pairs={{0,2},{1,3},{2,0},{3,1},{4,6},{5,7},{6,4},{7,5},{8,10},{9,11},{10,... | collective-permute-start | bytes 3145736 | tf_op jit(solution)/shard_map/ppermute | solution.py:455
  136.7 58.5 %collective-permute-start.17 = (bf16[512,1024]{1,0:T(8,128)(2,1)}, bf16[512,1024]{1,0:T(8,128)(2,1)S(1)}, u32[]{:S(2)}, u32[]{:S(2)}) collective-permute-start(bf16[512,1024]{1,0:T(8,128)(2,1)} %slice.19), channel_id=1, source_target_pairs={{0,2},{1,3},{2,0},{3,1},{4,6},{5,7},{6,4},{7,5},{8,10},{9,11},{10,... | collective-permute-start | bytes 3145736 | tf_op jit(solution)/shard_map/ppermute | solution.py:455
  146.0 19.4 %all-to-all-start.2 = ((f32[8,32,128]{2,1,0:T(8,128)}), f32[8,32,128]{2,1,0:T(8,128)S(1)}, u32[]{:S(2)}, u32[]{:S(2)}) async-start(f32[8,32,128]{2,1,0:T(8,128)} %right_grad.1), calls=%async_computation.2 | async-start | bytes 262144 | tf_op jit(solution)/shard_map/all_to_all | solution.py:458
  166.1 13.4 %all-to-all-start.3 = ((f32[8,32,128]{2,1,0:T(8,128)}), f32[8,32,128]{2,1,0:T(8,128)S(1)}, u32[]{:S(2)}, u32[]{:S(2)}) async-start(f32[8,32,128]{2,1,0:T(8,128)} %broadcast_in_dim.10), calls=%async_computation.3 | async-start | bytes 262144 | tf_op jit(solution)/shard_map/all_to_all | solution.py:458
  172.1 23.1 %collective-permute-start.16 = (bf16[512,1024]{1,0:T(8,128)(2,1)}, bf16[512,1024]{1,0:T(8,128)(2,1)S(1)}, u32[]{:S(2)}, u32[]{:S(2)}) collective-permute-start(bf16[512,1024]{1,0:T(8,128)(2,1)} %collective-permute-done.15.refs_2_), channel_id=1, source_target_pairs={{0,1},{1,0},{2,3},{3,2},{4,5},{5,4},{6,7},{7,6},{8,9},{9,8},{10,11... | collective-permute-start | bytes 3145736 | tf_op jit(solution)/shard_map/ppermute | solution.py:451
  195.3 6.5 %collective-permute-start.18 = (bf16[512,1024]{1,0:T(8,128)(2,1)S(1)}, bf16[512,1024]{1,0:T(8,128)(2,1)S(1)}, u32[]{:S(2)}, u32[]{:S(2)}) collective-permute-start(bf16[512,1024]{1,0:T(8,128)(2,1)S(1)} %collective-permute-done.17.refs_2_), channel_id=1, source_target_pairs={{0,1},{1,0},{2,3},{3,2},{4,5},{5,4},{6,7},{7,6},{8,9},{9,8},{10,11... | collective-permute-start | bytes 3145736 | tf_op jit(solution)/shard_map/ppermute | solution.py:451
  (8 other events, 46.8 us)
Sparse Core Ops, SparseCore 0:
  34.9 79.3 all-gather.1

commit v5 on v3

v5 whole, which is shorter than its diff:
```python
import functools
import math

import jax
import jax.numpy as jnp
from jax import lax
from jax.experimental import pallas as pl
from jax.experimental.pallas import tpu as pltpu
from jax.sharding import PartitionSpec as P

TOK_DEV = 1024
RANK = 32
MIB = 1 << 20
F32 = jnp.float32
BF16 = jnp.bfloat16


def dot(a, b, ca, cb, precision=None):
    return lax.dot_general(
        a, b, (((ca,), (cb,)), ((), ())), precision=precision, preferred_element_type=F32
    )


def split(a):
    high = a.astype(BF16)
    return high, (a - high.astype(F32)).astype(BF16)


def params(mib):
    return pltpu.CompilerParams(vmem_limit_bytes=mib * MIB)


def cost(flops, nbytes, weight=0.001):
    return pl.CostEstimate(
        flops=int(flops * weight), bytes_accessed=int(nbytes * weight), transcendentals=0
    )


def project_kernel(g_ref, qt_ref, y_ref):
    both = dot(jnp.concatenate(split(qt_ref[...]), axis=0), g_ref[...], 1, 1)
    y_ref[...] = both[0:RANK, :] + both[RANK:, :]


def project(out_grad, q_t):
    vm = pl.BlockSpec(memory_space=pltpu.VMEM)
    return pl.pallas_call(
        project_kernel,
        in_specs=[vm, vm],
        out_specs=vm,
        out_shape=jax.ShapeDtypeStruct((RANK, out_grad.shape[0]), F32),
        compiler_params=params(24),
        cost_estimate=cost(1e9, 2e6),
        name="project",
    )(out_grad, q_t)


def sketch_kernel(ids, e_ref, qt_ref, send_ref, keep_ref, qs_ref):
    phase = pl.program_id(0)

    @pl.when((phase == 0) & (pl.program_id(1) == 0))
    def _():
        high, low = split(qt_ref[...])
        qs_ref[0:RANK, :] = high
        qs_ref[RANK : 2 * RANK, :] = low

    high, low = split(e_ref[...])
    main = dot(high, qs_ref[...], 1, 1)
    rest = dot(low, qs_ref[0:RANK, :], 1, 1)
    rows = (main[:, 0:RANK] + main[:, RANK : 2 * RANK] + rest).T

    @pl.when(phase == 0)
    def _():
        send_ref[0] = rows

    @pl.when(phase == 1)
    def _():
        keep_ref[0] = rows


def local_sketch(core, error, q_t, chips, part):
    outs = error.shape[1]

    def e_map(p, y, ids):
        return (2 * y + jnp.where(p == 0, 1 - ids[0], ids[0]), 0)

    half = jax.ShapeDtypeStruct((chips, RANK, part), F32)
    return pl.pallas_call(
        sketch_kernel,
        grid_spec=pltpu.PrefetchScalarGridSpec(
            num_scalar_prefetch=1,
            grid=(2, chips),
            in_specs=[
                pl.BlockSpec((part, outs), e_map),
                pl.BlockSpec((RANK, outs), lambda p, y, ids: (0, 0)),
            ],
            out_specs=[
                pl.BlockSpec((1, RANK, part), lambda p, y, ids: (jnp.where(p == 0, y, chips - 1), 0, 0)),
                pl.BlockSpec((1, RANK, part), lambda p, y, ids: (jnp.where(p == 1, y, 0), 0, 0)),
            ],
            scratch_shapes=[pltpu.VMEM((2 * RANK, outs), BF16)],
        ),
        out_shape=[half, half],
        compiler_params=params(48),
        cost_estimate=cost(6e9, error.size * 4, 2),
        name="error_sketch",
    )(jnp.reshape(core, (1,)), error, q_t)


def sketch_rows_kernel(*refs, n_e, scale):
    e_refs, y_refs, x_ref, out = refs[:n_e], refs[n_e:-2], refs[-2], refs[-1]
    y = y_refs[0][...]
    for r in y_refs[1:]:
        y = y + r[...]
    both = dot(jnp.concatenate(split(y), axis=0), x_ref[...], 1, 0)
    total = (both[0:RANK, :] + both[RANK:, :]) * scale
    for r in e_refs:
        total = total + r[...]
    out[...] = total


def sketch_rows(e_list, y_list, acts, scale):
    vm = pl.BlockSpec(memory_space=pltpu.VMEM)
    return pl.pallas_call(
        functools.partial(sketch_rows_kernel, n_e=len(e_list), scale=scale),
        in_specs=[vm] * (1 + len(e_list) + len(y_list)),
        out_specs=vm,
        out_shape=jax.ShapeDtypeStruct((RANK, acts.shape[1]), F32),
        compiler_params=params(24),
        cost_estimate=cost(1e9, 3e6),
        name="sketch_rows",
    )(*e_list, *y_list, acts)


def basis_kernel(src, mine, other, out, sk, *, n_dp, chips, part):
    for k in range(chips):
        for e, ref in enumerate((mine, other)):
            at = pl.multiple_of(src[2 * k + e] * part, part)
            sk[:, pl.ds(at, part)] = ref[k] * (1.0 / n_dp)
    s = sk[...]
    gram = dot(s, s, 1, 1, lax.Precision.HIGHEST)
    row = lax.broadcasted_iota(jnp.int32, (RANK, RANK), 0)
    col = lax.broadcasted_iota(jnp.int32, (RANK, RANK), 1)
    eye = (row == col).astype(F32)
    m = jnp.concatenate([gram, eye, jnp.zeros((RANK, 2 * RANK), F32)], axis=1)
    index = lax.broadcasted_iota(jnp.int32, (RANK, 1), 0)
    for j in range(RANK - 1):
        factor = jnp.where(index > j, m[:, j : j + 1] / m[j : j + 1, j : j + 1], 0.0)
        m = m - factor * m[j : j + 1, :]
    diag = jnp.sum(jnp.where(row == col, m[:, 0:RANK], 0.0), axis=1, keepdims=True)
    inverse = m[:, RANK : 2 * RANK] / jnp.sqrt(diag)
    out[...] = dot(inverse, s, 1, 0, lax.Precision.HIGHEST)


def make_basis(src, mine, other, n_dp):
    chips, _, part = mine.shape
    din = 2 * chips * part
    vm = pl.BlockSpec(memory_space=pltpu.VMEM)
    return pl.pallas_call(
        functools.partial(basis_kernel, n_dp=n_dp, chips=chips, part=part),
        in_specs=[pl.BlockSpec(memory_space=pltpu.SMEM), vm, vm],
        out_specs=vm,
        out_shape=jax.ShapeDtypeStruct((RANK, din), F32),
        scratch_shapes=[pltpu.VMEM((RANK, din), F32)],
        compiler_params=params(24),
        cost_estimate=cost(6e9, 2e6),
        name="basis",
    )(src, mine, other)


def right_error_kernel(e_ref, b_ref, acc):
    @pl.when(pl.program_id(0) == 0)
    def _():
        acc[...] = jnp.zeros_like(acc)

    bh, bl = split(b_ref[...])
    eh, el = split(e_ref[...])
    main = dot(jnp.concatenate([bh, bl], axis=0), eh, 1, 0)
    acc[...] += main[0:RANK, :] + main[RANK:, :] + dot(bh, el, 1, 0)


def right_error(error, basis_t):
    din, outs = error.shape
    blk = 512
    return pl.pallas_call(
        right_error_kernel,
        grid=(din // blk,),
        in_specs=[
            pl.BlockSpec((blk, outs), lambda i: (i, 0)),
            pl.BlockSpec((RANK, blk), lambda i: (0, i)),
        ],
        out_specs=pl.BlockSpec((RANK, outs), lambda i: (0, 0)),
        out_shape=jax.ShapeDtypeStruct((RANK, outs), F32),
        compiler_params=params(48),
        cost_estimate=cost(8e9, error.size * 4, 1),
        name="right_error",
    )(error, basis_t)


def copies(sources, target, sems):
    made, at = [], 0
    for n, ref in enumerate(sources):
        size = ref.shape[0]
        made.append(pltpu.make_async_copy(ref, target.at[at : at + size], sems.at[n]))
        at += size
    return made


def right_grad_kernel(*refs, n_t, per, scale):
    b_ref, r_ref, g_ref = refs[1:4]
    x_refs = refs[4 : 4 + n_t * per]
    out, vacc, xbuf, sems = refs[4 + n_t * per :]
    r = pl.program_id(0)
    part = xbuf.shape[0] // n_t
    moves = copies(x_refs, xbuf, sems)

    @pl.when(r == 0)
    def _():
        for m in moves:
            m.start()
        vacc[...] = jnp.zeros_like(vacc)

    for n in range(n_t):

        @pl.when(r == n)
        def _(n=n):
            for m in moves[n * per : (n + 1) * per]:
                m.wait()

    both = jnp.concatenate(split(b_ref[...]), axis=0)
    v = dot(both, xbuf[pl.ds(pl.multiple_of(r * part, part), part), :], 1, 0)
    vacc[...] += v[0:RANK, :] + v[RANK:, :]

    @pl.when(r == n_t - 1)
    def _():
        w = dot(jnp.concatenate(split(vacc[...]), axis=0), g_ref[...], 1, 0)
        out[...] = r_ref[...] + (w[0:RANK, :] + w[RANK:, :]) * scale


def right_grad(src, basis_t, right_e, out_grad, pieces, scale):
    tok, outs = out_grad.shape
    n_t = src.shape[0]
    din = basis_t.shape[1]
    part = din // n_t
    same = lambda r, src: (0, 0)
    return pl.pallas_call(
        functools.partial(right_grad_kernel, n_t=n_t, per=len(pieces) // n_t, scale=scale),
        grid_spec=pltpu.PrefetchScalarGridSpec(
            num_scalar_prefetch=1,
            grid=(n_t,),
            in_specs=[
                pl.BlockSpec((RANK, part), lambda r, src: (0, src[r])),
                pl.BlockSpec((RANK, outs), same),
                pl.BlockSpec((tok, outs), same),
            ]
            + [pl.BlockSpec(memory_space=pl.ANY)] * len(pieces),
            out_specs=pl.BlockSpec((RANK, outs), same),
            scratch_shapes=[
                pltpu.VMEM((RANK, tok), F32),
                pltpu.VMEM((din, tok), BF16),
                pltpu.SemaphoreType.DMA((len(pieces),)),
            ],
        ),
        out_shape=jax.ShapeDtypeStruct((RANK, outs), F32),
        compiler_params=params(40),
        cost_estimate=cost(4e9, din * tok * 2, 1),
        name="right_grad",
    )(src, basis_t, right_e, out_grad, *pieces)


def update_kernel(*refs, n_t, per, n_dp, scale):
    e_ref, b_ref, g_ref, q_ref = refs[1:5]
    x_refs = refs[5 : 5 + n_t * per]
    out, qt_out, qs, xbuf, sems = refs[5 + n_t * per :]
    r = pl.program_id(0)
    part = xbuf.shape[0] // n_t
    moves = copies(x_refs, xbuf, sems)

    @pl.when(r == 0)
    def _():
        for m in moves:
            m.start()
        q_t = q_ref[...] * (1.0 / n_dp)
        qt_out[...] = q_t
        high, low = split(q_t)
        qs[0:RANK, :] = high
        qs[RANK : 2 * RANK, :] = low
        qs[2 * RANK : 3 * RANK, :] = high

    bh, bl = split(b_ref[...].T)
    low_rank = dot(jnp.concatenate([bh, bh, bl], axis=1), qs[...], 1, 0)
    for n in range(n_t):

        @pl.when(r == n)
        def _(n=n):
            for m in moves[n * per : (n + 1) * per]:
                m.wait()

    x = xbuf[pl.ds(pl.multiple_of(r * part, part), part), :]
    out[...] = e_ref[...] + dot(x, g_ref[...], 1, 0) * scale - low_rank


def update_error(src, error, basis_t, out_grad, pieces, q_t, n_dp, scale):
    tok, outs = out_grad.shape
    n_t = src.shape[0]
    din = error.shape[0]
    part = din // n_t
    block = pl.BlockSpec((part, outs), lambda r, src: (src[r], 0))
    same = lambda r, src: (0, 0)
    return pl.pallas_call(
        functools.partial(
            update_kernel, n_t=n_t, per=len(pieces) // n_t, n_dp=n_dp, scale=scale
        ),
        grid_spec=pltpu.PrefetchScalarGridSpec(
            num_scalar_prefetch=1,
            grid=(n_t,),
            in_specs=[
                block,
                pl.BlockSpec((RANK, part), lambda r, src: (0, src[r])),
                pl.BlockSpec((tok, outs), same),
                pl.BlockSpec((RANK, outs), same),
            ]
            + [pl.BlockSpec(memory_space=pl.ANY)] * len(pieces),
            out_specs=[block, pl.BlockSpec((RANK, outs), same)],
            scratch_shapes=[
                pltpu.VMEM((3 * RANK, outs), BF16),
                pltpu.VMEM((din, tok), BF16),
                pltpu.SemaphoreType.DMA((len(pieces),)),
            ],
        ),
        out_shape=[
            jax.ShapeDtypeStruct(error.shape, F32),
            jax.ShapeDtypeStruct((RANK, outs), F32),
        ],
        compiler_params=params(56),
        cost_estimate=cost(9e9, error.size * 8 + din * tok * 2, 1),
        name="update_error",
    )(src, error, basis_t, out_grad, q_t, *pieces)


def near_kernel(ids, g_ref, gs_ref, w_ref, ws_ref, out):
    out[...] = dot(g_ref[...], w_ref[...], 1, 1) + dot(gs_ref[...], ws_ref[...], 1, 1)


def near_input_grad(me_t, g_own, g_sib, weight, w_sib):
    tok, outs = g_own.shape
    part = w_sib.shape[0]
    blk = min(256, part)
    per = part // blk
    whole = pl.BlockSpec((tok, outs), lambda i, ids: (0, 0))
    return pl.pallas_call(
        near_kernel,
        grid_spec=pltpu.PrefetchScalarGridSpec(
            num_scalar_prefetch=1,
            grid=(per,),
            in_specs=[
                whole,
                whole,
                pl.BlockSpec((blk, outs), lambda i, ids: (ids[0] * per + i, 0)),
                pl.BlockSpec((blk, outs), lambda i, ids: (i, 0)),
            ],
            out_specs=pl.BlockSpec((tok, blk), lambda i, ids: (0, i)),
        ),
        out_shape=jax.ShapeDtypeStruct((tok, part), F32),
        compiler_params=params(48),
        cost_estimate=cost(4 * tok * outs * part, 12e6, 2),
        name="input_grad_near",
    )(jnp.reshape(me_t, (1,)), g_own, g_sib, weight, w_sib)


def far_kernel(*refs, n_far):
    prev, w_ref = refs[0], refs[1]
    g_refs = refs[2:-3]
    out, gbuf, sems = refs[-3:]
    tok = prev.shape[0]
    moves = copies(g_refs, gbuf, sems)

    @pl.when(pl.program_id(0) == 0)
    def _():
        for m in moves:
            m.start()
        for m in moves:
            m.wait()

    width = gbuf.shape[1]
    total = prev[...]
    for n in range(n_far):
        rows = gbuf[n * tok : (n + 1) * tok, :]
        total = total + dot(rows, w_ref[:, n * width : (n + 1) * width], 1, 1)
    out[...] = total


def far_input_grad(prev, w_far, gs):
    outs = gs[0].shape[1]
    tok, part = prev.shape
    n_far = w_far.shape[1] // outs
    blk = min(256, part)
    to = pl.BlockSpec((tok, blk), lambda i: (0, i))
    return pl.pallas_call(
        functools.partial(far_kernel, n_far=n_far),
        grid=(part // blk,),
        in_specs=[to, pl.BlockSpec((blk, w_far.shape[1]), lambda i: (i, 0))]
        + [pl.BlockSpec(memory_space=pl.ANY)] * len(gs),
        out_specs=to,
        out_shape=jax.ShapeDtypeStruct((tok, part), F32),
        scratch_shapes=[
            pltpu.VMEM((n_far * tok, outs), BF16),
            pltpu.SemaphoreType.DMA((len(gs),)),
        ],
        input_output_aliases={0: 0},
        compiler_params=params(48),
        cost_estimate=cost(2 * n_far * tok * outs * part, 10e6, 1),
        name="input_grad_far",
    )(prev, w_far, *gs)


def after(value, *others):
    return lax.optimization_barrier((value, others))[0]


def per_device(activations, out_grad, weight, error, q_start):
    scale = 1.0 / math.sqrt(TOK_DEV)
    n_dp = lax.axis_size("dp")
    chips = lax.axis_size("chip")
    n_t = 2 * chips
    d = lax.axis_index("dp").astype(jnp.int32)
    y = lax.axis_index("chip").astype(jnp.int32)
    c = lax.axis_index("core").astype(jnp.int32)
    t = 2 * y + c
    tok, part = activations.shape
    outs = out_grad.shape[1]
    din = weight.shape[0]
    error = error[0]
    q_t = q_start.T
    steps = range(1, chips)
    share = part // n_dp

    def to_sibling(a):
        return lax.ppermute(a, "core", [(0, 1), (1, 0)])

    def to_chip(a, k, flip=0):
        pairs = [(i, ((i // 2 + k) % chips) * 2 + ((i % 2) ^ flip)) for i in range(n_t)]
        return lax.ppermute(a, ("chip", "core"), pairs)

    def to_replica(a, k):
        return lax.ppermute(a, "dp", [(i, i ^ k) for i in range(n_dp)])

    def over_replicas(a, chunks):
        rounds = [1 << i for i in range(n_dp.bit_length() - 1)]
        for i, k in enumerate(rounds):
            if i == len(rounds) - 1:
                a = after(a, chunks)
            a = a + to_replica(a, k)
        return a

    src = jnp.stack([((y - k) % chips) * 2 + (c ^ e) for k in range(chips) for e in range(2)])
    src = src.astype(jnp.int32)

    y_t = project(out_grad, q_t)
    y_t = y_t + to_sibling(y_t)
    y_list = [y_t] + [to_chip(y_t, k) for k in steps]

    moves = [(k, e) for k in steps for e in range(2)]
    w_parts = []
    for k, e in moves:
        dest = ((y + k) % chips) * 2 + (c ^ e)
        w_parts.append(lax.dynamic_slice(weight, (dest * part + d * share, 0), (share, outs)))
    w_parts = after(w_parts, y_t)
    w_start = [to_chip(a, k, e) for a, (k, e) in zip(w_parts, moves)]
    send, keep = local_sketch(c, error, after(q_t, *w_parts), chips, part)
    w_parts, y_list = after((w_start, y_list), send)
    w_far = lax.all_gather(jnp.concatenate(w_parts, axis=1), "dp", axis=0, tiled=True)

    got = to_sibling(send)

    def block(k):
        at = (y + k) % chips
        return lax.dynamic_index_in_dim(keep, at, 0, False) + lax.dynamic_index_in_dim(got, at, 0, False)

    e_list = [block(0)] + [to_chip(block(k), k) for k in steps]
    sketch = sketch_rows(e_list, y_list, activations, scale)

    n_chunk = 4
    high = part // n_chunk
    acts = after(activations, send)
    x_rows = [acts[:, i * high : (i + 1) * high].T for i in range(n_chunk)]
    x_rows[0:2] = after(x_rows[0:2], e_list)
    x_far = [[to_chip(a, k) for k in steps] for a in x_rows[0:2]]
    sketch = after(over_replicas(sketch, x_far[0]), x_far[1])
    mine = jnp.stack([sketch] + [to_chip(sketch, k) for k in steps])
    x_rows[2:4] = after(x_rows[2:4], mine)
    x_far += [[to_chip(a, k) for k in steps] for a in x_rows[2:4]]
    basis_t = make_basis(src, mine, to_sibling(mine), n_dp)
    right_e = right_error(error, basis_t)

    g_sib = to_sibling(out_grad)
    w_sib = to_sibling(lax.dynamic_slice(after(weight, send), ((t ^ 1) * part, 0), (part, outs)))
    grad = near_input_grad(t, out_grad, g_sib, weight, after(w_sib, right_e, x_far[2]))

    x_far[0:2] = after(x_far[0:2], mine)
    x_far[2] = after(x_far[2], right_e)
    x_far[3] = after(x_far[3], grad)
    pieces = list(x_rows) + [to_sibling(a) for a in after(x_rows, mine)]
    for n in range(len(steps)):
        held = [a[n] for a in x_far]
        pieces += held + [to_sibling(a) for a in held]

    span = tok // n_chunk
    g_rows = after(out_grad, right_e)
    g_far = [
        [to_chip(g_rows[i * span : (i + 1) * span], k) for k in steps] for i in range(n_chunk)
    ]
    right = after(right_grad(src, basis_t, right_e, out_grad, pieces, scale), g_far[0])
    right = over_replicas(right, g_far[1])
    new_error, q_t = update_error(
        src, error, basis_t, out_grad, pieces, right, n_dp, scale
    )
    gs = []
    g_far = after(g_far, q_t)
    for n in range(len(steps)):
        held = [a[n] for a in g_far]
        gs += held + [to_sibling(a) for a in held]
    grad = far_input_grad(grad, w_far, gs)
    return (grad, new_error[None], q_t.T)


def solution(mesh):
    n_dp, n_t = mesh.devices.shape
    mesh = jax.sharding.Mesh(mesh.devices.reshape(n_dp, n_t // 2, 2), ("dp", "chip", "core"))
    tensor = ("chip", "core")
    placed = (
        P("dp", tensor),
        P("dp", tensor),
        P(None, tensor),
        P("dp", None, tensor),
        P(tensor, None),
    )
    return jax.shard_map(
        per_device,
        mesh=mesh,
        in_specs=placed,
        out_specs=(P("dp", tensor), P("dp", None, tensor), P(tensor, None)),
        check_vma=False,
    )
```

time: 217 us -> 184 us (0.85)
  blocking collectives: 30.1 us -> 0 us
  Pallas kernels: 80.2 us -> 67.5 us
  waiting for transfers between devices: 52.6 us -> 60.6 us
  starting transfers between devices: 21.3 us -> 26.1 us
  local copies, waits for them, and re-layouts: 17 us -> 13.5 us
    ppermute x0 -> x6, waiting for transfers between devices: none -> 37.2 us  [to_replica(): return lax.ppermute(a, 'dp', [(i, i ^ k) for i in range(n_dp)])]
    all_to_all x2 -> x0, blocking collectives: 30.1 us -> none  [exchange(): return lax.all_to_all(a, axes, 0, 0, tiled=True)]
    all_to_all x2 -> x0, waiting for transfers between devices: 19.4 us -> none  [exchange(): return lax.all_to_all(a, axes, 0, 0, tiled=True)]
    pallas_call x7 -> x6, Pallas kernels: 61.5 us -> 48.4 us  [the longest x1 20.8 us: update_error(): pl.pallas_call(functools.partial(update_kernel, n_t=n_t, per=len(pieces)...]
    all_to_all x2 -> x0, starting transfers between devices: 10.6 us -> none  [exchange(): return lax.all_to_all(a, axes, 0, 0, tiled=True)]
    ppermute x7 -> x13, waiting for transfers between devices: 30.6 us -> 20.3 us  [to_chip(): return lax.ppermute(a, ('chip', 'core'), pairs)]
    ppermute x7 -> x13, starting transfers between devices: 9.01 us -> 16.2 us  [to_chip(): return lax.ppermute(a, ('chip', 'core'), pairs)]
    ppermute x0 -> x6, starting transfers between devices: none -> 5.36 us  [to_replica(): return lax.ppermute(a, 'dp', [(i, i ^ k) for i in range(n_dp)])]
  transfers between devices with their start and end apart: 20 -> 37, of which waited for: 6 -> 15; matrix products, arithmetic and copies ran while one was open for 6% -> 4% of each run, Pallas kernels for 34% -> 31%
where the time goes in v5:
time: 184 us
  Pallas kernels  67.5 us (37%)
  waiting for transfers between devices  60.6 us (33%)
  starting transfers between devices  26.1 us (14%)
  between operations  14.6 us (8%)
  local copies, waits for them, and re-layouts  13.5 us (7%)
    ppermute x6, waiting for transfers between devices, to_replica(): return lax.ppermute(a, 'dp', [(i, i ^ k) for i in range(n_dp)])  37.2 us
    pallas_call x1, Pallas kernels, update_error(): pl.pallas_call(functools.partial(update_kernel, n_t=n_t, per=len(pieces)...  20.8 us
    ppermute x13, waiting for transfers between devices, to_chip(): return lax.ppermute(a, ('chip', 'core'), pairs)  20.3 us
    ppermute x13, starting transfers between devices, to_chip(): return lax.ppermute(a, ('chip', 'core'), pairs)  16.2 us
    pallas_call x1, Pallas kernels, right_error(): pl.pallas_call(right_error_kernel, grid=(din // blk,), in_specs=[pl.Block...  9.86 us
    pallas_call x1, Pallas kernels, local_sketch(): pl.pallas_call(sketch_kernel, grid_spec=pltpu.PrefetchScalarGridSpec(num_...  9.22 us
    pallas_call x1, Pallas kernels, far_input_grad(): pl.pallas_call(functools.partial(far_kernel, n_far=n_far), grid=(part //...  8.87 us
    pallas_call x1, Pallas kernels, near_input_grad(): pl.pallas_call(near_kernel, grid_spec=pltpu.PrefetchScalarGridSpec(num_sc...  8.51 us
  transfers between devices with their start and end apart: 37, of which 15 were waited for; matrix products, arithmetic and copies ran while one was open for 4% of the time, Pallas kernels for 31%

profile of v5, /device:TPU:0, one launch (start us, length us, event | category | flops | bytes accessed | tf_op | source)
XLA Modules:
  0.0 183.9 jit_solution(15579743517380809506)
XLA Ops:
  12.0 2.8 %collective-permute-start.5 = (bf16[128,1024]{1,0:T(8,128)(2,1)S(1)}, bf16[128,1024]{1,0:T(8,128)(2,1)S(1)}, u32[]{:S(2)}, u32[]{:S(2)}) collective-permute-start(bf16[128,1024]{1,0:T(8,128)(2,1)S(1)} %get-tuple-element.38), channel_id=1, source_target_pairs={{0,2},{1,3},{2,0},{3,1},{4,6},{5,7},{6,4},{7,5},{8,10},{9,11},{10,... | collective-permute-start | bytes 786440 | tf_op jit(solution)/shard_map/ppermute | solution.py:442
  16.5 9.2 %error_sketch.1 = (f32[2,32,1024]{2,1,0:T(8,128)S(1)}, f32[2,32,1024]{2,1,0:T(8,128)S(1)}) custom-call(s32[1]{0:T(128)} %bitcast.1.ids, f32[4096,1024]{1,0:T(8,128)} %bitcast.28, f32[32,1024]{1,0:T(8,128)S(1)} %bitcast.25), custom_call_target="tpu_custom_call" | custom-call | flops 12000000000 | bytes 33554432 | tf_op jit(solution)/shard_map/error_sketch/pallas_call | solution.py:87
  25.7 4.3 %collective-permute-done.7.refs_3_ = f32[32,1024]{1,0:T(8,128)S(1)} collective-permute-done((f32[32,1024]{1,0:T(8,128)S(1)}, f32[32,1024]{1,0:T(8,128)S(1)}, u32[]{:S(2)}, u32[]{:S(2)}) %collective-permute-start.7) | collective-permute-done | bytes 131104 | tf_op jit(solution)/shard_map/ppermute | solution.py:442
  31.5 2.5 %copy.9 = bf16[1024,1024]{0,1:T(8,128)(2,1)} copy(bf16[1024,1024]{1,0:T(8,128)(2,1)S(1)} %copy-done) | data formatting | bytes 4194304 | tf_op jit(solution)/shard_map/optimization_barrier | solution.py:417
  34.0 3.2 %constant_dynamic-slice_fusion = bf16[1024,1024]{1,0:T(8,128)(2,1)} fusion(bf16[4096,1024]{1,0:T(8,128)(2,1)} %w_ref.1, s32[]{:T(128)S(6)} %select_n.46), kind=kLoop, calls=%fused_computation.8 | loop fusion | bytes 4194308 | tf_op jit(solution)/shard_map/dynamic_slice | solution.py:496
  37.4 1.8 collective-permute-start.4
  39.4 3.9 %collective-permute-done.4.refs_1_ = f32[32,1024]{1,0:T(8,128)S(1)} collective-permute-done((f32[32,1024]{1,0:T(8,128)S(1)}, f32[32,1024]{1,0:T(8,128)S(1)}, u32[]{:S(2)}, u32[]{:S(2)}) %collective-permute-start.4) | collective-permute-done | bytes 131104 | tf_op jit(solution)/shard_map/ppermute | solution.py:442
  43.3 1.7 collective-permute-start.10
  45.8 1.8 collective-permute-start.8
  47.6 4.2 %collective-permute-done.8 = f32[32,1024]{1,0:T(8,128)S(1)} collective-permute-done((f32[32,1024]{1,0:T(8,128)S(1)}, f32[32,1024]{1,0:T(8,128)S(1)}, u32[]{:S(2)}, u32[]{:S(2)}) %collective-permute-start.8) | collective-permute-done | bytes 131104 | tf_op jit(solution)/shard_map/ppermute | solution.py:445
  53.3 10.0 %collective-permute-done.9 = f32[32,1024]{1,0:T(8,128)S(1)} collective-permute-done((f32[32,1024]{1,0:T(8,128)S(1)}, f32[32,1024]{1,0:T(8,128)S(1)}, u32[]{:S(2)}, u32[]{:S(2)}) %collective-permute-start.9) | collective-permute-done | bytes 131104 | tf_op jit(solution)/shard_map/ppermute | solution.py:445
  63.8 8.3 %collective-permute-done.11 = f32[32,1024]{1,0:T(8,128)S(1)} collective-permute-done((f32[32,1024]{1,0:T(8,128)S(1)}, f32[32,1024]{1,0:T(8,128)S(1)}, u32[]{:S(2)}, u32[]{:S(2)}) %collective-permute-start.11) | collective-permute-done | bytes 131104 | tf_op jit(solution)/shard_map/ppermute | solution.py:445
  72.1 1.6 collective-permute-start.13
  73.8 3.8 %collective-permute-done.13 = f32[32,1024]{1,0:T(8,128)S(1)} collective-permute-done((f32[32,1024]{1,0:T(8,128)S(1)}, f32[32,1024]{1,0:T(8,128)S(1)}, u32[]{:S(2)}, u32[]{:S(2)}) %collective-permute-start.13) | collective-permute-done | bytes 131104 | tf_op jit(solution)/shard_map/ppermute | solution.py:442
  79.8 5.1 %basis.1.b_ref.refs_1_.refs_2_ = f32[32,4096]{1,0:T(8,128)S(1)} custom-call(s32[4]{0:T(128)S(1)} %pad_add_fusion.src.refs_0_, f32[2,32,1024]{2,1,0:T(8,128)S(1)} %pad_maximum_fusion.1.mine, f32[2,32,1024]{2,1,0:T(8,128)S(1)} %collective-permute-done.14.other), custom_call_target="tpu_custom_call" | custom-call | flops 6000000 | bytes 2000 | tf_op jit(solution)/shard_map/basis/pallas_call | solution.py:158
  85.0 9.9 %right_error.1.refs_2_ = f32[32,1024]{1,0:T(8,128)S(1)} custom-call(f32[4096,1024]{1,0:T(8,128)} %bitcast.29, f32[32,4096]{1,0:T(8,128)S(1)} %basis.1.b_ref.refs_1_.refs_2_), custom_call_target="tpu_custom_call" | custom-call | flops 8000000000 | bytes 16777216 | tf_op jit(solution)/shard_map/right_error/pallas_call | solution.py:184
  96.0 8.5 %input_grad_near.1.refs_0_ = f32[1024,1024]{1,0:T(8,128)} custom-call(s32[1]{0:T(128)} %bitcast.ids, bf16[1024,1024]{1,0:T(8,128)(2,1)S(1)} %copy-done.2, bf16[1024,1024]{1,0:T(8,128)(2,1)} %collective-permute-done.gs_ref, bf16[4096,1024]{1,0:T(8,128)(2,1)} %w_ref.1, bf16[1024,1024]{1,0:T(8,128)(2,1)} %collective-permute-done.2.ws_ref), custom_call_target="tpu_custom_call" | custom-call | flops 8589934592 | bytes 24000000 | tf_op jit(solution)/shard_map/input_grad_near/pallas_call | solution.py:350
  108.9 3.8 %right_grad.1 = f32[32,1024]{1,0:T(8,128)S(1)} custom-call(s32[4]{0:T(128)S(1)} %pad_add_fusion.src.refs_0_, f32[32,4096]{1,0:T(8,128)S(1)} %basis.1.b_ref.refs_1_.refs_2_, f32[32,1024]{1,0:T(8,128)S(1)} %right_error.1.refs_2_, bf16[1024,1024]{1,0:T(8,128)(2,1)S(1)} %copy-done.2, bf16[256,1024]{1,0:T(8,128)(2,1)S(1)} %copy-done.13, ...), custom_call_target="tpu_custom_call" | custom-call | flops 4000000000 | bytes 8388608 | tf_op jit(solution)/shard_map/right_grad/pallas_call | solution.py:245
  112.8 7.9 %collective-permute-done.16.refs_2_ = bf16[256,1024]{1,0:T(8,128)(2,1)S(1)} collective-permute-done((bf16[256,1024]{1,0:T(8,128)(2,1)S(1)}, bf16[256,1024]{1,0:T(8,128)(2,1)S(1)}, u32[]{:S(2)}, u32[]{:S(2)}) %collective-permute-start.16) | collective-permute-done | bytes 524320 | tf_op jit(solution)/shard_map/ppermute | solution.py:442
  120.9 4.8 %collective-permute-done.29 = f32[32,1024]{1,0:T(8,128)S(1)} collective-permute-done((f32[32,1024]{1,0:T(8,128)S(1)}, f32[32,1024]{1,0:T(8,128)S(1)}, u32[]{:S(2)}, u32[]{:S(2)}) %collective-permute-start.29) | collective-permute-done | bytes 131104 | tf_op jit(solution)/shard_map/ppermute | solution.py:445
  125.8 5.0 %collective-permute-done.30 = f32[32,1024]{1,0:T(8,128)S(1)} collective-permute-done((f32[32,1024]{1,0:T(8,128)S(1)}, f32[32,1024]{1,0:T(8,128)S(1)}, u32[]{:S(2)}, u32[]{:S(2)}) %collective-permute-start.30) | collective-permute-done | bytes 131104 | tf_op jit(solution)/shard_map/ppermute | solution.py:445
  134.3 5.1 %collective-permute-done.31 = f32[32,1024]{1,0:T(8,128)S(1)} collective-permute-done((f32[32,1024]{1,0:T(8,128)S(1)}, f32[32,1024]{1,0:T(8,128)S(1)}, u32[]{:S(2)}, u32[]{:S(2)}) %collective-permute-start.31) | collective-permute-done | bytes 131104 | tf_op jit(solution)/shard_map/ppermute | solution.py:445
  140.1 20.8 %update_error.1 = (f32[4096,1024]{1,0:T(8,128)}, f32[32,1024]{1,0:T(8,128)}) custom-call(s32[4]{0:T(128)} %copy-done.16, f32[4096,1024]{1,0:T(8,128)} %bitcast.30, f32[32,4096]{1,0:T(8,128)} %copy-done.7, bf16[1024,1024]{1,0:T(8,128)(2,1)} %refs_3_.3, f32[32,1024]{1,0:T(8,128)} %add.126.refs_4_, bf16[256,1024]{1,0:T(8,128)(2,1)} %copy-done.12, ...), custom_call_target="tpu_custom_call" | custom-call | flops 8999999488 | bytes 41943040 | tf_op jit(solution)/shard_map/update_error/pallas_call | solution.py:309
  168.2 8.9 %input_grad_far.1 = f32[1024,1024]{1,0:T(8,128)} custom-call(f32[1024,1024]{1,0:T(8,128)} %input_grad_near.1.refs_0_, bf16[1024,2048]{1,0:T(8,128)(2,1)} %all-gather.2.cloned.1.call-done.refs_1_, bf16[256,1024]{1,0:T(8,128)(2,1)S(1)} %collective-permute-done.16.refs_2_, ...), custom_call_target="tpu_custom_call", output_to_operand_aliasing={{}: (0, {})} | custom-call | flops 4294967296 | bytes 10000000 | tf_op jit(solution)/shard_map/input_grad_far/pallas_call | solution.py:398
  (140 shorter events, 30.4 us)
Async XLA Ops:
  7.2 158.9 %all-gather.2.cloned.1.call-start = ((), (), s32[]{:S(2)}) async-start(), calls=%async_computation | async-start | bytes 4718592 | tf_op jit(solution)/shard_map/all_gather | solution.py:471
  12.0 18.0 %collective-permute-start.5 = (bf16[128,1024]{1,0:T(8,128)(2,1)S(1)}, bf16[128,1024]{1,0:T(8,128)(2,1)S(1)}, u32[]{:S(2)}, u32[]{:S(2)}) collective-permute-start(bf16[128,1024]{1,0:T(8,128)(2,1)S(1)} %get-tuple-element.38), channel_id=1, source_target_pairs={{0,2},{1,3},{2,0},{3,1},{4,6},{5,7},{6,4},{7,5},{8,10},{9,11},{10,... | collective-permute-start | bytes 786440 | tf_op jit(solution)/shard_map/ppermute | solution.py:442
  14.9 15.1 %collective-permute-start.6 = (bf16[128,1024]{1,0:T(8,128)(2,1)S(1)}, bf16[128,1024]{1,0:T(8,128)(2,1)S(1)}, u32[]{:S(2)}, u32[]{:S(2)}) collective-permute-start(bf16[128,1024]{1,0:T(8,128)(2,1)S(1)} %get-tuple-element.39), channel_id=1, source_target_pairs={{0,3},{1,2},{2,1},{3,0},{4,7},{5,6},{6,5},{7,4},{8,11},{9,10},{10,... | collective-permute-start | bytes 786440 | tf_op jit(solution)/shard_map/ppermute | solution.py:442
  14.9 15.1 %collective-permute-start.7 = (f32[32,1024]{1,0:T(8,128)S(1)}, f32[32,1024]{1,0:T(8,128)S(1)}, u32[]{:S(2)}, u32[]{:S(2)}) collective-permute-start(f32[32,1024]{1,0:T(8,128)S(1)} %add.107.refs_2_), channel_id=1, source_target_pairs={{0,2},{1,3},{2,0},{3,1},{4,6},{5,7},{6,4},{7,5},{8,10},{9,11},{10,... | collective-permute-start | bytes 393224 | tf_op jit(solution)/shard_map/ppermute | solution.py:442
  30.9 6.4 %collective-permute-start.3 = (f32[2,32,1024]{2,1,0:T(8,128)S(1)}, f32[2,32,1024]{2,1,0:T(8,128)S(1)}, u32[]{:S(2)}, u32[]{:S(2)}) collective-permute-start(f32[2,32,1024]{2,1,0:T(8,128)S(1)} %get-tuple-element.41), channel_id=1, source_target_pairs={{0,1},{1,0},{2,3},{3,2},{4,5},{5,4},{6,7},{7,6},{8,9},{9,8},{10,11... | collective-permute-start | bytes 786440 | tf_op jit(solution)/shard_map/ppermute | solution.py:438
  31.0 64.6 %collective-permute-start = (bf16[1024,1024]{1,0:T(8,128)(2,1)}, bf16[1024,1024]{1,0:T(8,128)(2,1)}, u32[]{:S(2)}, u32[]{:S(2)}) collective-permute-start(bf16[1024,1024]{1,0:T(8,128)(2,1)} %refs_3_.3), channel_id=1, source_target_pairs={{0,1},{1,0},{2,3},{3,2},{4,5},{5,4},{6,7},{7,6},{8,9},{9,8},{10,11... | collective-permute-start | bytes 6291464 | tf_op jit(solution)/shard_map/ppermute | solution.py:438
  37.2 58.2 %collective-permute-start.2 = (bf16[1024,1024]{1,0:T(8,128)(2,1)}, bf16[1024,1024]{1,0:T(8,128)(2,1)}, u32[]{:S(2)}, u32[]{:S(2)}) collective-permute-start(bf16[1024,1024]{1,0:T(8,128)(2,1)} %constant_dynamic-slice_fusion), channel_id=1, source_target_pairs={{0,1},{1,0},{2,3},{3,2},{4,5},{5,4},{6,7},{7,6},{8,9},{9,8},{10,11... | collective-permute-start | bytes 6291464 | tf_op jit(solution)/shard_map/ppermute | solution.py:438
  37.4 5.9 %collective-permute-start.4 = (f32[32,1024]{1,0:T(8,128)S(1)}, f32[32,1024]{1,0:T(8,128)S(1)}, u32[]{:S(2)}, u32[]{:S(2)}) collective-permute-start(f32[32,1024]{1,0:T(8,128)S(1)} %get-tuple-element.83), channel_id=1, source_target_pairs={{0,2},{1,3},{2,0},{3,1},{4,6},{5,7},{6,4},{7,5},{8,10},{9,11},{10,... | collective-permute-start | bytes 393224 | tf_op jit(solution)/shard_map/ppermute | solution.py:442
  43.3 20.0 %collective-permute-start.10 = (bf16[256,1024]{1,0:T(8,128)(2,1)S(1)}, bf16[256,1024]{1,0:T(8,128)(2,1)S(1)}, u32[]{:S(2)}, u32[]{:S(2)}) collective-permute-start(bf16[256,1024]{1,0:T(8,128)(2,1)S(1)} %get-tuple-element.57.refs_4_.refs_5_), channel_id=1, source_target_pairs={{0,2},{1,3},{2,0},{3,1},{4,6},{5,7},{6,4},{7,5},{8,10},{9,11},{10,... | collective-permute-start | bytes 1572872 | tf_op jit(solution)/shard_map/ppermute | solution.py:442
  45.0 27.1 %collective-permute-start.12 = (bf16[256,1024]{1,0:T(8,128)(2,1)S(1)}, bf16[256,1024]{1,0:T(8,128)(2,1)S(1)}, u32[]{:S(2)}, u32[]{:S(2)}) collective-permute-start(bf16[256,1024]{1,0:T(8,128)(2,1)S(1)} %get-tuple-element.58.refs_5_.refs_6_), channel_id=1, source_target_pairs={{0,2},{1,3},{2,0},{3,1},{4,6},{5,7},{6,4},{7,5},{8,10},{9,11},{10,... | collective-permute-start | bytes 1572872 | tf_op jit(solution)/shard_map/ppermute | solution.py:442
  45.8 5.9 %collective-permute-start.8 = (f32[32,1024]{1,0:T(8,128)S(1)}, f32[32,1024]{1,0:T(8,128)S(1)}, u32[]{:S(2)}, u32[]{:S(2)}) collective-permute-start(f32[32,1024]{1,0:T(8,128)S(1)} %sketch_rows.1), channel_id=1, source_target_pairs={{0,4},{4,0},{8,12},{12,8},{16,20},{20,16},{24,28},{28,24},{1,5},{5... | collective-permute-start | bytes 393224 | tf_op jit(solution)/shard_map/ppermute | solution.py:445
  51.7 11.5 %collective-permute-start.9 = (f32[32,1024]{1,0:T(8,128)S(1)}, f32[32,1024]{1,0:T(8,128)S(1)}, u32[]{:S(2)}, u32[]{:S(2)}) collective-permute-start(f32[32,1024]{1,0:T(8,128)S(1)} %add.121), channel_id=1, source_target_pairs={{0,8},{4,12},{8,0},{12,4},{16,24},{20,28},{24,16},{28,20},{1,9},{5... | collective-permute-start | bytes 393224 | tf_op jit(solution)/shard_map/ppermute | solution.py:445
  63.3 8.8 %collective-permute-start.11 = (f32[32,1024]{1,0:T(8,128)S(1)}, f32[32,1024]{1,0:T(8,128)S(1)}, u32[]{:S(2)}, u32[]{:S(2)}) collective-permute-start(f32[32,1024]{1,0:T(8,128)S(1)} %add.122), channel_id=1, source_target_pairs={{0,16},{4,20},{8,24},{12,28},{16,0},{20,4},{24,8},{28,12},{1,17},{... | collective-permute-start | bytes 393224 | tf_op jit(solution)/shard_map/ppermute | solution.py:445
  77.8 17.1 %collective-permute-start.15 = (bf16[256,1024]{1,0:T(8,128)(2,1)S(1)}, bf16[256,1024]{1,0:T(8,128)(2,1)S(1)}, u32[]{:S(2)}, u32[]{:S(2)}) collective-permute-start(bf16[256,1024]{1,0:T(8,128)(2,1)S(1)} %get-tuple-element.59.refs_6_.refs_7_), channel_id=1, source_target_pairs={{0,2},{1,3},{2,0},{3,1},{4,6},{5,7},{6,4},{7,5},{8,10},{9,11},{10,... | collective-permute-start | bytes 1572872 | tf_op jit(solution)/shard_map/ppermute | solution.py:442
  79.3 25.2 %collective-permute-start.24 = (bf16[256,1024]{1,0:T(8,128)(2,1)S(1)}, bf16[256,1024]{1,0:T(8,128)(2,1)S(1)}, u32[]{:S(2)}, u32[]{:S(2)}) collective-permute-start(bf16[256,1024]{1,0:T(8,128)(2,1)S(1)} %get-tuple-element.60.refs_7_.refs_8_), channel_id=1, source_target_pairs={{0,2},{1,3},{2,0},{3,1},{4,6},{5,7},{6,4},{7,5},{8,10},{9,11},{10,... | collective-permute-start | bytes 1572872 | tf_op jit(solution)/shard_map/ppermute | solution.py:442
  79.8 24.9 %collective-permute-start.25 = (bf16[256,1024]{1,0:T(8,128)(2,1)}, bf16[256,1024]{1,0:T(8,128)(2,1)S(1)}, u32[]{:S(2)}, u32[]{:S(2)}) collective-permute-start(bf16[256,1024]{1,0:T(8,128)(2,1)} %copy-done.17), channel_id=1, source_target_pairs={{0,1},{1,0},{2,3},{3,2},{4,5},{5,4},{6,7},{7,6},{8,9},{9,8},{10,11... | collective-permute-start | bytes 1572872 | tf_op jit(solution)/shard_map/ppermute | solution.py:438
  94.9 10.2 %collective-permute-start.26 = (bf16[256,1024]{1,0:T(8,128)(2,1)S(1)}, bf16[256,1024]{1,0:T(8,128)(2,1)S(1)}, u32[]{:S(2)}, u32[]{:S(2)}) collective-permute-start(bf16[256,1024]{1,0:T(8,128)(2,1)S(1)} %copy-done.20), channel_id=1, source_target_pairs={{0,1},{1,0},{2,3},{3,2},{4,5},{5,4},{6,7},{7,6},{8,9},{9,8},{10,11... | collective-permute-start | bytes 1572872 | tf_op jit(solution)/shard_map/ppermute | solution.py:438
  95.5 9.7 %collective-permute-start.20 = (bf16[256,1024]{1,0:T(8,128)(2,1)S(1)}, bf16[256,1024]{1,0:T(8,128)(2,1)S(1)}, u32[]{:S(2)}, u32[]{:S(2)}) collective-permute-start(bf16[256,1024]{1,0:T(8,128)(2,1)S(1)} %copy-done.13), channel_id=1, source_target_pairs={{0,1},{1,0},{2,3},{3,2},{4,5},{5,4},{6,7},{7,6},{8,9},{9,8},{10,11... | collective-permute-start | bytes 1572872 | tf_op jit(solution)/shard_map/ppermute | solution.py:438
  95.6 10.2 %collective-permute-start.21 = (bf16[256,1024]{1,0:T(8,128)(2,1)S(1)}, bf16[256,1024]{1,0:T(8,128)(2,1)S(1)}, u32[]{:S(2)}, u32[]{:S(2)}) collective-permute-start(bf16[256,1024]{1,0:T(8,128)(2,1)S(1)} %copy-done.11), channel_id=1, source_target_pairs={{0,1},{1,0},{2,3},{3,2},{4,5},{5,4},{6,7},{7,6},{8,9},{9,8},{10,11... | collective-permute-start | bytes 1572872 | tf_op jit(solution)/shard_map/ppermute | solution.py:438
  105.8 14.8 %collective-permute-start.16 = (bf16[256,1024]{1,0:T(8,128)(2,1)S(1)}, bf16[256,1024]{1,0:T(8,128)(2,1)S(1)}, u32[]{:S(2)}, u32[]{:S(2)}) collective-permute-start(bf16[256,1024]{1,0:T(8,128)(2,1)S(1)} %get-tuple-element.78), channel_id=1, source_target_pairs={{0,2},{1,3},{2,0},{3,1},{4,6},{5,7},{6,4},{7,5},{8,10},{9,11},{10,... | collective-permute-start | bytes 1572872 | tf_op jit(solution)/shard_map/ppermute | solution.py:442
  107.5 23.6 %collective-permute-start.17 = (bf16[256,1024]{1,0:T(8,128)(2,1)S(1)}, bf16[256,1024]{1,0:T(8,128)(2,1)S(1)}, u32[]{:S(2)}, u32[]{:S(2)}) collective-permute-start(bf16[256,1024]{1,0:T(8,128)(2,1)S(1)} %get-tuple-element.77), channel_id=1, source_target_pairs={{0,2},{1,3},{2,0},{3,1},{4,6},{5,7},{6,4},{7,5},{8,10},{9,11},{10,... | collective-permute-start | bytes 1572872 | tf_op jit(solution)/shard_map/ppermute | solution.py:442
  131.1 8.4 %collective-permute-start.31 = (f32[32,1024]{1,0:T(8,128)S(1)}, f32[32,1024]{1,0:T(8,128)S(1)}, u32[]{:S(2)}, u32[]{:S(2)}) collective-permute-start(f32[32,1024]{1,0:T(8,128)S(1)} %add.125), channel_id=1, source_target_pairs={{0,16},{4,20},{8,24},{12,28},{16,0},{20,4},{24,8},{28,12},{1,17},{... | collective-permute-start | bytes 393224 | tf_op jit(solution)/shard_map/ppermute | solution.py:445
  132.3 28.7 %collective-permute-start.18 = (bf16[256,1024]{1,0:T(8,128)(2,1)S(1)}, bf16[256,1024]{1,0:T(8,128)(2,1)S(1)}, u32[]{:S(2)}, u32[]{:S(2)}) collective-permute-start(bf16[256,1024]{1,0:T(8,128)(2,1)S(1)} %get-tuple-element.76), channel_id=1, source_target_pairs={{0,2},{1,3},{2,0},{3,1},{4,6},{5,7},{6,4},{7,5},{8,10},{9,11},{10,... | collective-permute-start | bytes 1572872 | tf_op jit(solution)/shard_map/ppermute | solution.py:442
  133.7 27.3 %collective-permute-start.19 = (bf16[256,1024]{1,0:T(8,128)(2,1)S(1)}, bf16[256,1024]{1,0:T(8,128)(2,1)S(1)}, u32[]{:S(2)}, u32[]{:S(2)}) collective-permute-start(bf16[256,1024]{1,0:T(8,128)(2,1)S(1)} %get-tuple-element.75), channel_id=1, source_target_pairs={{0,2},{1,3},{2,0},{3,1},{4,6},{5,7},{6,4},{7,5},{8,10},{9,11},{10,... | collective-permute-start | bytes 1572872 | tf_op jit(solution)/shard_map/ppermute | solution.py:442
  (45 other events, 467.4 us)
Sparse Core Ops, SparseCore 0:
  31.0 77.6 all-gather.1

commit v6 on v5

--- a/solution.py
+++ b/solution.py
@@ -36,29 +36,13 @@
     )
 
 
-def project_kernel(g_ref, qt_ref, y_ref):
-    both = dot(jnp.concatenate(split(qt_ref[...]), axis=0), g_ref[...], 1, 1)
-    y_ref[...] = both[0:RANK, :] + both[RANK:, :]
-
-
-def project(out_grad, q_t):
-    vm = pl.BlockSpec(memory_space=pltpu.VMEM)
-    return pl.pallas_call(
-        project_kernel,
-        in_specs=[vm, vm],
-        out_specs=vm,
-        out_shape=jax.ShapeDtypeStruct((RANK, out_grad.shape[0]), F32),
-        compiler_params=params(24),
-        cost_estimate=cost(1e9, 2e6),
-        name="project",
-    )(out_grad, q_t)
-
-
-def sketch_kernel(ids, e_ref, qt_ref, send_ref, keep_ref, qs_ref):
-    phase = pl.program_id(0)
-
-    @pl.when((phase == 0) & (pl.program_id(1) == 0))
-    def _():
+def sketch_kernel(ids, e_ref, qt_ref, g_hbm, send_ref, keep_ref, y_ref, qs_ref, g_ref, sem):
+    phase, y = pl.program_id(0), pl.program_id(1)
+    move = pltpu.make_async_copy(g_hbm, g_ref, sem)
+
+    @pl.when((phase == 0) & (y == 0))
+    def _():
+        move.start()
         high, low = split(qt_ref[...])
         qs_ref[0:RANK, :] = high
         qs_ref[RANK : 2 * RANK, :] = low
@@ -76,9 +60,15 @@
     def _():
         keep_ref[0] = rows
 
-
-def local_sketch(core, error, q_t, chips, part):
-    outs = error.shape[1]
+    @pl.when((phase == 1) & (y == pl.num_programs(1) - 1))
+    def _():
+        move.wait()
+        both = dot(qs_ref[...], g_ref[...], 1, 1)
+        y_ref[...] = both[0:RANK, :] + both[RANK : 2 * RANK, :]
+
+
+def local_sketch(core, error, q_t, out_grad, chips, part):
+    tok, outs = out_grad.shape
 
     def e_map(p, y, ids):
         return (2 * y + jnp.where(p == 0, 1 - ids[0], ids[0]), 0)
@@ -92,18 +82,24 @@
             in_specs=[
                 pl.BlockSpec((part, outs), e_map),
                 pl.BlockSpec((RANK, outs), lambda p, y, ids: (0, 0)),
+                pl.BlockSpec(memory_space=pl.ANY),
             ],
             out_specs=[
                 pl.BlockSpec((1, RANK, part), lambda p, y, ids: (jnp.where(p == 0, y, chips - 1), 0, 0)),
                 pl.BlockSpec((1, RANK, part), lambda p, y, ids: (jnp.where(p == 1, y, 0), 0, 0)),
+                pl.BlockSpec((RANK, tok), lambda p, y, ids: (0, 0)),
             ],
-            scratch_shapes=[pltpu.VMEM((2 * RANK, outs), BF16)],
+            scratch_shapes=[
+                pltpu.VMEM((2 * RANK, outs), BF16),
+                pltpu.VMEM((tok, outs), BF16),
+                pltpu.SemaphoreType.DMA,
+            ],
         ),
-        out_shape=[half, half],
+        out_shape=[half, half, jax.ShapeDtypeStruct((RANK, tok), F32)],
         compiler_params=params(48),
         cost_estimate=cost(6e9, error.size * 4, 2),
         name="error_sketch",
-    )(jnp.reshape(core, (1,)), error, q_t)
+    )(jnp.reshape(core, (1,)), error, q_t, out_grad)
 
 
 def sketch_rows_kernel(*refs, n_e, scale):
@@ -262,7 +258,7 @@
         ),
         out_shape=jax.ShapeDtypeStruct((RANK, outs), F32),
         compiler_params=params(40),
-        cost_estimate=cost(4e9, din * tok * 2, 1),
+        cost_estimate=cost(4e9, din * tok * 2),
         name="right_grad",
     )(src, basis_t, right_e, out_grad, *pieces)
 
@@ -277,7 +273,7 @@
 
     @pl.when(r == 0)
     def _():
-        for m in moves:
+        for m in moves[: 2 * per]:
             m.start()
         q_t = q_ref[...] * (1.0 / n_dp)
         qt_out[...] = q_t
@@ -292,6 +288,9 @@
 
         @pl.when(r == n)
         def _(n=n):
+            if n > 0:
+                for m in moves[(n + 1) * per : (n + 2) * per]:
+                    m.start()
             for m in moves[n * per : (n + 1) * per]:
                 m.wait()
 
@@ -407,7 +406,7 @@
             pltpu.SemaphoreType.DMA((len(gs),)),
         ],
         input_output_aliases={0: 0},
-        compiler_params=params(48),
+        compiler_params=params(24),
         cost_estimate=cost(2 * n_far * tok * outs * part, 10e6, 1),
         name="input_grad_far",
     )(prev, w_far, *gs)
@@ -455,36 +454,35 @@
     src = jnp.stack([((y - k) % chips) * 2 + (c ^ e) for k in range(chips) for e in range(2)])
     src = src.astype(jnp.int32)
 
-    y_t = project(out_grad, q_t)
-    y_t = y_t + to_sibling(y_t)
-    y_list = [y_t] + [to_chip(y_t, k) for k in steps]
-
     moves = [(k, e) for k in steps for e in range(2)]
     w_parts = []
     for k, e in moves:
         dest = ((y + k) % chips) * 2 + (c ^ e)
         w_parts.append(lax.dynamic_slice(weight, (dest * part + d * share, 0), (share, outs)))
-    w_parts = after(w_parts, y_t)
     w_start = [to_chip(a, k, e) for a, (k, e) in zip(w_parts, moves)]
-    send, keep = local_sketch(c, error, after(q_t, *w_parts), chips, part)
-    w_parts, y_list = after((w_start, y_list), send)
-    w_far = lax.all_gather(jnp.concatenate(w_parts, axis=1), "dp", axis=0, tiled=True)
+    send, keep, y_own = local_sketch(c, error, after(q_t, *w_parts), out_grad, chips, part)
 
     got = to_sibling(send)
+    y_t = y_own + to_sibling(y_own)
 
     def block(k):
         at = (y + k) % chips
         return lax.dynamic_index_in_dim(keep, at, 0, False) + lax.dynamic_index_in_dim(got, at, 0, False)
 
-    e_list = [block(0)] + [to_chip(block(k), k) for k in steps]
-    sketch = sketch_rows(e_list, y_list, activations, scale)
+    blocks = [block(k) for k in range(chips)]
+    e_list = [blocks[0]] + [to_chip(blocks[k], k) for k in steps]
+    y_list = [y_t] + [to_chip(y_t, k) for k in steps]
 
     n_chunk = 4
     high = part // n_chunk
-    acts = after(activations, send)
+    acts = after(activations, blocks, y_t)
     x_rows = [acts[:, i * high : (i + 1) * high].T for i in range(n_chunk)]
-    x_rows[0:2] = after(x_rows[0:2], e_list)
+    sketch = sketch_rows(e_list, y_list, activations, scale)
+    w_parts = after(w_start, sketch)
+    w_far = lax.all_gather(jnp.concatenate(w_parts, axis=1), "dp", axis=0, tiled=True)
+    x_rows[0:2] = after(x_rows[0:2], e_list, y_list)
     x_far = [[to_chip(a, k) for k in steps] for a in x_rows[0:2]]
+    w_sib = lax.dynamic_slice(after(weight, sketch), ((t ^ 1) * part, 0), (part, outs))
     sketch = after(over_replicas(sketch, x_far[0]), x_far[1])
     mine = jnp.stack([sketch] + [to_chip(sketch, k) for k in steps])
     x_rows[2:4] = after(x_rows[2:4], mine)
@@ -493,7 +491,7 @@
     right_e = right_error(error, basis_t)
 
     g_sib = to_sibling(out_grad)
-    w_sib = to_sibling(lax.dynamic_slice(after(weight, send), ((t ^ 1) * part, 0), (part, outs)))
+    w_sib = to_sibling(w_sib)
     grad = near_input_grad(t, out_grad, g_sib, weight, after(w_sib, right_e, x_far[2]))
 
     x_far[0:2] = after(x_far[0:2], mine)
@@ -505,17 +503,17 @@
         pieces += held + [to_sibling(a) for a in held]
 
     span = tok // n_chunk
-    g_rows = after(out_grad, right_e)
+    g_rows = after(out_grad, basis_t)
     g_far = [
         [to_chip(g_rows[i * span : (i + 1) * span], k) for k in steps] for i in range(n_chunk)
     ]
     right = after(right_grad(src, basis_t, right_e, out_grad, pieces, scale), g_far[0])
-    right = over_replicas(right, g_far[1])
+    right = after(over_replicas(right, ()), g_far[1])
     new_error, q_t = update_error(
         src, error, basis_t, out_grad, pieces, right, n_dp, scale
     )
     gs = []
-    g_far = after(g_far, q_t)
+    g_far[2:] = after(g_far[2:], q_t)
     for n in range(len(steps)):
         held = [a[n] for a in g_far]
         gs += held + [to_sibling(a) for a in held]

time: 184 us -> 192 us (1.043)
  waiting for transfers between devices: 60.6 us -> 67.1 us
  other arithmetic: 1.76 us -> 3.72 us
    ppermute x13, waiting for transfers between devices: 20.3 us -> 26.2 us  [to_chip(): return lax.ppermute(a, ('chip', 'core'), pairs)]
    unnamed x64 -> x48, local copies, waits for them, and re-layouts: 6.33 us -> 4.76 us
  transfers between devices with their start and end apart: 37 -> 37, of which waited for: 15 -> 13; matrix products, arithmetic and copies ran while one was open for 4% -> 4% of each run, Pallas kernels for 31% -> 26%
where the time goes in v6:
time: 192 us; the launch traced here: 191 us
  Pallas kernels  68.4 us (36%)
  waiting for transfers between devices  67.1 us (35%)
  starting transfers between devices  25.6 us (13%)
  between operations  14.6 us (8%)
  local copies, waits for them, and re-layouts  12 us (6%)
  other arithmetic  3.72 us (2%)
    ppermute x6, waiting for transfers between devices, to_replica(): return lax.ppermute(a, 'dp', [(i, i ^ k) for i in range(n_dp)])  37.9 us
    ppermute x13, waiting for transfers between devices, to_chip(): return lax.ppermute(a, ('chip', 'core'), pairs)  26.2 us
    pallas_call x1, Pallas kernels, update_error(): pl.pallas_call(functools.partial(update_kernel, n_t=n_t, per=len(pieces)...  21 us
    ppermute x13, starting transfers between devices, to_chip(): return lax.ppermute(a, ('chip', 'core'), pairs)  15 us
    pallas_call x1, Pallas kernels, local_sketch(): pl.pallas_call(sketch_kernel, grid_spec=pltpu.PrefetchScalarGridSpec(num_...  10.1 us
    pallas_call x1, Pallas kernels, right_error(): pl.pallas_call(right_error_kernel, grid=(din // blk,), in_specs=[pl.Block...  9.76 us
    pallas_call x1, Pallas kernels, far_input_grad(): pl.pallas_call(functools.partial(far_kernel, n_far=n_far), grid=(part //...  9.13 us
    pallas_call x1, Pallas kernels, near_input_grad(): pl.pallas_call(near_kernel, grid_spec=pltpu.PrefetchScalarGridSpec(num_sc...  8.51 us
  transfers between devices with their start and end apart: 37, of which 13 were waited for; matrix products, arithmetic and copies ran while one was open for 4% of the time, Pallas kernels for 26%

profile of v6, /device:TPU:0, one launch (start us, length us, event | category | flops | bytes accessed | tf_op | source)
XLA Modules:
  0.0 191.3 jit_solution(17756670565457073173)
XLA Ops:
  10.8 10.1 %error_sketch.1 = (f32[2,32,1024]{2,1,0:T(8,128)S(1)}, f32[2,32,1024]{2,1,0:T(8,128)S(1)}, f32[32,1024]{1,0:T(8,128)S(1)}) custom-call(s32[1]{0:T(128)} %bitcast.1.ids, f32[4096,1024]{1,0:T(8,128)} %bitcast.27, f32[32,1024]{1,0:T(8,128)S(1)} %bitcast.24, bf16[1024,1024]{1,0:T(8,128)(2,1)S(1)} %copy-done.1), custom_call_target="tpu_custom_call" | custom-call | flops 12000000000 | bytes 33554432 | tf_op jit(solution)/shard_map/error_sketch/pallas_call | solution.py:77
  21.5 2.9 %collective-permute-start.14 = (bf16[128,1024]{1,0:T(8,128)(2,1)S(1)}, bf16[128,1024]{1,0:T(8,128)(2,1)}, u32[]{:S(2)}, u32[]{:S(2)}) collective-permute-start(bf16[128,1024]{1,0:T(8,128)(2,1)S(1)} %get-tuple-element.64), channel_id=1, source_target_pairs={{0,2},{1,3},{2,0},{3,1},{4,6},{5,7},{6,4},{7,5},{8,10},{9,11},{10,... | collective-permute-start | bytes 786440 | tf_op jit(solution)/shard_map/ppermute | solution.py:441
  27.7 12.3 %collective-permute-done.4.refs_3_ = f32[32,1024]{1,0:T(8,128)S(1)} collective-permute-done((f32[32,1024]{1,0:T(8,128)S(1)}, f32[32,1024]{1,0:T(8,128)S(1)}, u32[]{:S(2)}, u32[]{:S(2)}) %collective-permute-start.4) | collective-permute-done | bytes 131104 | tf_op jit(solution)/shard_map/ppermute | solution.py:441
  40.0 2.3 %collective-permute-done.2.refs_1_ = f32[32,1024]{1,0:T(8,128)S(1)} collective-permute-done((f32[32,1024]{1,0:T(8,128)S(1)}, f32[32,1024]{1,0:T(8,128)S(1)}, u32[]{:S(2)}, u32[]{:S(2)}) %collective-permute-start.2) | collective-permute-done | bytes 131104 | tf_op jit(solution)/shard_map/ppermute | solution.py:441
  42.8 1.9 pad_maximum_fusion
  44.7 2.6 %copy.9 = bf16[1024,1024]{0,1:T(8,128)(2,1)} copy(bf16[1024,1024]{1,0:T(8,128)(2,1)S(1)} %copy-done) | data formatting | bytes 4194304 | tf_op jit(solution)/shard_map/optimization_barrier | solution.py:416
  47.3 3.2 %constant_dynamic-slice_fusion = bf16[1024,1024]{1,0:T(8,128)(2,1)} fusion(bf16[4096,1024]{1,0:T(8,128)(2,1)} %w_ref.1, s32[]{:T(128)S(6)} %select_n.49), kind=kLoop, calls=%fused_computation.8 | loop fusion | bytes 4194308 | tf_op jit(solution)/shard_map/dynamic_slice | solution.py:485
  51.2 1.8 collective-permute-start.8
  55.0 5.8 %collective-permute-done.6 = f32[32,1024]{1,0:T(8,128)S(1)} collective-permute-done((f32[32,1024]{1,0:T(8,128)S(1)}, f32[32,1024]{1,0:T(8,128)S(1)}, u32[]{:S(2)}, u32[]{:S(2)}) %collective-permute-start.6) | collective-permute-done | bytes 131104 | tf_op jit(solution)/shard_map/ppermute | solution.py:444
  60.8 2.1 %collective-permute-start.7 = (f32[32,1024]{1,0:T(8,128)S(1)}, f32[32,1024]{1,0:T(8,128)S(1)}, u32[]{:S(2)}, u32[]{:S(2)}) collective-permute-start(f32[32,1024]{1,0:T(8,128)S(1)} %add.121), channel_id=1, source_target_pairs={{0,8},{4,12},{8,0},{12,4},{16,24},{20,28},{24,16},{28,20},{1,9},{5... | collective-permute-start | bytes 393224 | tf_op jit(solution)/shard_map/ppermute | solution.py:444
  62.9 10.4 %collective-permute-done.7 = f32[32,1024]{1,0:T(8,128)S(1)} collective-permute-done((f32[32,1024]{1,0:T(8,128)S(1)}, f32[32,1024]{1,0:T(8,128)S(1)}, u32[]{:S(2)}, u32[]{:S(2)}) %collective-permute-start.7) | collective-permute-done | bytes 131104 | tf_op jit(solution)/shard_map/ppermute | solution.py:444
  74.1 9.1 %collective-permute-done.9 = f32[32,1024]{1,0:T(8,128)S(1)} collective-permute-done((f32[32,1024]{1,0:T(8,128)S(1)}, f32[32,1024]{1,0:T(8,128)S(1)}, u32[]{:S(2)}, u32[]{:S(2)}) %collective-permute-start.9) | collective-permute-done | bytes 131104 | tf_op jit(solution)/shard_map/ppermute | solution.py:444
  84.8 3.6 %collective-permute-done.11 = f32[32,1024]{1,0:T(8,128)S(1)} collective-permute-done((f32[32,1024]{1,0:T(8,128)S(1)}, f32[32,1024]{1,0:T(8,128)S(1)}, u32[]{:S(2)}, u32[]{:S(2)}) %collective-permute-start.11) | collective-permute-done | bytes 131104 | tf_op jit(solution)/shard_map/ppermute | solution.py:441
  90.6 5.5 %basis.1.b_ref.refs_1_.refs_2_ = f32[32,4096]{1,0:T(8,128)S(1)} custom-call(s32[4]{0:T(128)S(1)} %pad_add_fusion.src.refs_0_, f32[2,32,1024]{2,1,0:T(8,128)S(1)} %pad_maximum_fusion.1.mine, f32[2,32,1024]{2,1,0:T(8,128)} %collective-permute-done.12.other), custom_call_target="tpu_custom_call" | custom-call | flops 6000000 | bytes 2000 | tf_op jit(solution)/shard_map/basis/pallas_call | solution.py:154
  96.2 9.8 %right_error.1.refs_2_ = f32[32,1024]{1,0:T(8,128)S(1)} custom-call(f32[4096,1024]{1,0:T(8,128)} %bitcast.28, f32[32,4096]{1,0:T(8,128)S(1)} %basis.1.b_ref.refs_1_.refs_2_), custom_call_target="tpu_custom_call" | custom-call | flops 8000000000 | bytes 16777216 | tf_op jit(solution)/shard_map/right_error/pallas_call | solution.py:180
  107.1 8.5 %input_grad_near.1.refs_0_ = f32[1024,1024]{1,0:T(8,128)} custom-call(s32[1]{0:T(128)} %bitcast.ids, bf16[1024,1024]{1,0:T(8,128)(2,1)S(1)} %copy-done.2, bf16[1024,1024]{1,0:T(8,128)(2,1)} %collective-permute-done.gs_ref, bf16[4096,1024]{1,0:T(8,128)(2,1)} %w_ref.1, bf16[1024,1024]{1,0:T(8,128)(2,1)} %collective-permute-done.5.ws_ref), custom_call_target="tpu_custom_call" | custom-call | flops 8589934592 | bytes 24000000 | tf_op jit(solution)/shard_map/input_grad_near/pallas_call | solution.py:349
  119.9 3.8 %right_grad.1 = f32[32,1024]{1,0:T(8,128)S(1)} custom-call(s32[4]{0:T(128)S(1)} %pad_add_fusion.src.refs_0_, f32[32,4096]{1,0:T(8,128)S(1)} %basis.1.b_ref.refs_1_.refs_2_, f32[32,1024]{1,0:T(8,128)S(1)} %right_error.1.refs_2_, bf16[1024,1024]{1,0:T(8,128)(2,1)S(1)} %copy-done.2, bf16[256,1024]{1,0:T(8,128)(2,1)S(1)} %get-tuple-element.49.refs_4_.refs_5_, ...), custom_call_target="tpu_custom_call" | custom-call | flops 4000000 | bytes 8388 | tf_op jit(solution)/shard_map/right_grad/pallas_call | solution.py:241
  123.8 8.0 %collective-permute-done.16.refs_2_ = bf16[256,1024]{1,0:T(8,128)(2,1)} collective-permute-done((bf16[256,1024]{1,0:T(8,128)(2,1)S(1)}, bf16[256,1024]{1,0:T(8,128)(2,1)}, u32[]{:S(2)}, u32[]{:S(2)}) %collective-permute-start.16) | collective-permute-done | bytes 524320 | tf_op jit(solution)/shard_map/ppermute | solution.py:441
  133.3 3.5 %collective-permute-done.29 = f32[32,1024]{1,0:T(8,128)S(1)} collective-permute-done((f32[32,1024]{1,0:T(8,128)S(1)}, f32[32,1024]{1,0:T(8,128)S(1)}, u32[]{:S(2)}, u32[]{:S(2)}) %collective-permute-start.29) | collective-permute-done | bytes 131104 | tf_op jit(solution)/shard_map/ppermute | solution.py:444
  136.9 5.0 %collective-permute-done.30 = f32[32,1024]{1,0:T(8,128)S(1)} collective-permute-done((f32[32,1024]{1,0:T(8,128)S(1)}, f32[32,1024]{1,0:T(8,128)S(1)}, u32[]{:S(2)}, u32[]{:S(2)}) %collective-permute-start.30) | collective-permute-done | bytes 131104 | tf_op jit(solution)/shard_map/ppermute | solution.py:444
  144.6 4.1 %collective-permute-done.31 = f32[32,1024]{1,0:T(8,128)S(1)} collective-permute-done((f32[32,1024]{1,0:T(8,128)S(1)}, f32[32,1024]{1,0:T(8,128)S(1)}, u32[]{:S(2)}, u32[]{:S(2)}) %collective-permute-start.31) | collective-permute-done | bytes 131104 | tf_op jit(solution)/shard_map/ppermute | solution.py:444
  149.3 21.0 %update_error.1 = (f32[4096,1024]{1,0:T(8,128)}, f32[32,1024]{1,0:T(8,128)}) custom-call(s32[4]{0:T(128)} %copy-done.21, f32[4096,1024]{1,0:T(8,128)} %bitcast.29, f32[32,4096]{1,0:T(8,128)} %copy-done.4, bf16[1024,1024]{1,0:T(8,128)(2,1)} %refs_3_.3, f32[32,1024]{1,0:T(8,128)} %add.126.refs_4_, bf16[256,1024]{1,0:T(8,128)(2,1)} %copy-done.8, ...), custom_call_target="tpu_custom_call" | custom-call | flops 8999999488 | bytes 41943040 | tf_op jit(solution)/shard_map/update_error/pallas_call | solution.py:308
  173.1 2.2 %copy-done.3 = bf16[1024,2048]{1,0:T(8,128)(2,1)S(1)} copy-done((bf16[1024,2048]{1,0:T(8,128)(2,1)S(1)}, bf16[1024,2048]{1,0:T(8,128)(2,1)}, u32[]{:S(2)}) %copy-start.3) | copy-done | bytes 4194328
  175.3 9.1 %input_grad_far.1 = f32[1024,1024]{1,0:T(8,128)} custom-call(f32[1024,1024]{1,0:T(8,128)} %input_grad_near.1.refs_0_, bf16[1024,2048]{1,0:T(8,128)(2,1)S(1)} %copy-done.3, bf16[256,1024]{1,0:T(8,128)(2,1)} %collective-permute-done.16.refs_2_, bf16[256,1024]{1,0:T(8,128)(2,1)} %collective-permute-done.17.refs_3_, ...), custom_call_target="tpu_custom_call", output_to_operand_aliasing={{}: (0, {})} | custom-call | flops 4294967296 | bytes 10000000 | tf_op jit(solution)/shard_map/input_grad_far/pallas_call | solution.py:397
  (123 shorter events, 28.1 us)
Async XLA Ops:
  7.2 165.9 %all-gather.2.cloned.1.call-start = ((), (), s32[]{:S(2)}) async-start(), calls=%async_computation | async-start | bytes 4718592 | tf_op jit(solution)/shard_map/all_gather | solution.py:482
  21.5 21.2 %collective-permute-start.14 = (bf16[128,1024]{1,0:T(8,128)(2,1)S(1)}, bf16[128,1024]{1,0:T(8,128)(2,1)}, u32[]{:S(2)}, u32[]{:S(2)}) collective-permute-start(bf16[128,1024]{1,0:T(8,128)(2,1)S(1)} %get-tuple-element.64), channel_id=1, source_target_pairs={{0,2},{1,3},{2,0},{3,1},{4,6},{5,7},{6,4},{7,5},{8,10},{9,11},{10,... | collective-permute-start | bytes 786440 | tf_op jit(solution)/shard_map/ppermute | solution.py:441
  24.5 18.3 %collective-permute-start.15 = (bf16[128,1024]{1,0:T(8,128)(2,1)S(1)}, bf16[128,1024]{1,0:T(8,128)(2,1)}, u32[]{:S(2)}, u32[]{:S(2)}) collective-permute-start(bf16[128,1024]{1,0:T(8,128)(2,1)S(1)} %get-tuple-element.63), channel_id=1, source_target_pairs={{0,3},{1,2},{2,1},{3,0},{4,7},{5,6},{6,5},{7,4},{8,11},{9,10},{10,... | collective-permute-start | bytes 786440 | tf_op jit(solution)/shard_map/ppermute | solution.py:441
  24.5 15.5 %collective-permute-start.4 = (f32[32,1024]{1,0:T(8,128)S(1)}, f32[32,1024]{1,0:T(8,128)S(1)}, u32[]{:S(2)}, u32[]{:S(2)}) collective-permute-start(f32[32,1024]{1,0:T(8,128)S(1)} %add.114.refs_2_), channel_id=1, source_target_pairs={{0,2},{1,3},{2,0},{3,1},{4,6},{5,7},{6,4},{7,5},{8,10},{9,11},{10,... | collective-permute-start | bytes 393224 | tf_op jit(solution)/shard_map/ppermute | solution.py:441
  27.0 15.3 %collective-permute-start.2 = (f32[32,1024]{1,0:T(8,128)S(1)}, f32[32,1024]{1,0:T(8,128)S(1)}, u32[]{:S(2)}, u32[]{:S(2)}) collective-permute-start(f32[32,1024]{1,0:T(8,128)S(1)} %get-tuple-element.73), channel_id=1, source_target_pairs={{0,2},{1,3},{2,0},{3,1},{4,6},{5,7},{6,4},{7,5},{8,10},{9,11},{10,... | collective-permute-start | bytes 393224 | tf_op jit(solution)/shard_map/ppermute | solution.py:441
  44.7 62.0 %collective-permute-start = (bf16[1024,1024]{1,0:T(8,128)(2,1)}, bf16[1024,1024]{1,0:T(8,128)(2,1)}, u32[]{:S(2)}, u32[]{:S(2)}) collective-permute-start(bf16[1024,1024]{1,0:T(8,128)(2,1)} %refs_3_.3), channel_id=1, source_target_pairs={{0,1},{1,0},{2,3},{3,2},{4,5},{5,4},{6,7},{7,6},{8,9},{9,8},{10,11... | collective-permute-start | bytes 6291464 | tf_op jit(solution)/shard_map/ppermute | solution.py:437
  50.5 56.0 %collective-permute-start.5 = (bf16[1024,1024]{1,0:T(8,128)(2,1)}, bf16[1024,1024]{1,0:T(8,128)(2,1)}, u32[]{:S(2)}, u32[]{:S(2)}) collective-permute-start(bf16[1024,1024]{1,0:T(8,128)(2,1)} %constant_dynamic-slice_fusion), channel_id=1, source_target_pairs={{0,1},{1,0},{2,3},{3,2},{4,5},{5,4},{6,7},{7,6},{8,9},{9,8},{10,11... | collective-permute-start | bytes 6291464 | tf_op jit(solution)/shard_map/ppermute | solution.py:437
  51.2 22.1 %collective-permute-start.8 = (bf16[256,1024]{1,0:T(8,128)(2,1)S(1)}, bf16[256,1024]{1,0:T(8,128)(2,1)S(1)}, u32[]{:S(2)}, u32[]{:S(2)}) collective-permute-start(bf16[256,1024]{1,0:T(8,128)(2,1)S(1)} %get-tuple-element.49.refs_4_.refs_5_), channel_id=1, source_target_pairs={{0,2},{1,3},{2,0},{3,1},{4,6},{5,7},{6,4},{7,5},{8,10},{9,11},{10,... | collective-permute-start | bytes 1572872 | tf_op jit(solution)/shard_map/ppermute | solution.py:441
  53.0 30.2 %collective-permute-start.10 = (bf16[256,1024]{1,0:T(8,128)(2,1)S(1)}, bf16[256,1024]{1,0:T(8,128)(2,1)S(1)}, u32[]{:S(2)}, u32[]{:S(2)}) collective-permute-start(bf16[256,1024]{1,0:T(8,128)(2,1)S(1)} %get-tuple-element.50.refs_5_.refs_6_), channel_id=1, source_target_pairs={{0,2},{1,3},{2,0},{3,1},{4,6},{5,7},{6,4},{7,5},{8,10},{9,11},{10,... | collective-permute-start | bytes 1572872 | tf_op jit(solution)/shard_map/ppermute | solution.py:441
  53.3 7.5 %collective-permute-start.6 = (f32[32,1024]{1,0:T(8,128)S(1)}, f32[32,1024]{1,0:T(8,128)S(1)}, u32[]{:S(2)}, u32[]{:S(2)}) collective-permute-start(f32[32,1024]{1,0:T(8,128)S(1)} %sketch_rows.1), channel_id=1, source_target_pairs={{0,4},{4,0},{8,12},{12,8},{16,20},{20,16},{24,28},{28,24},{1,5},{5... | collective-permute-start | bytes 393224 | tf_op jit(solution)/shard_map/ppermute | solution.py:444
  60.8 12.5 %collective-permute-start.7 = (f32[32,1024]{1,0:T(8,128)S(1)}, f32[32,1024]{1,0:T(8,128)S(1)}, u32[]{:S(2)}, u32[]{:S(2)}) collective-permute-start(f32[32,1024]{1,0:T(8,128)S(1)} %add.121), channel_id=1, source_target_pairs={{0,8},{4,12},{8,0},{12,4},{16,24},{20,28},{24,16},{28,20},{1,9},{5... | collective-permute-start | bytes 393224 | tf_op jit(solution)/shard_map/ppermute | solution.py:444
  73.3 9.9 %collective-permute-start.9 = (f32[32,1024]{1,0:T(8,128)S(1)}, f32[32,1024]{1,0:T(8,128)S(1)}, u32[]{:S(2)}, u32[]{:S(2)}) collective-permute-start(f32[32,1024]{1,0:T(8,128)S(1)} %add.122), channel_id=1, source_target_pairs={{0,16},{4,20},{8,24},{12,28},{16,0},{20,4},{24,8},{28,12},{1,17},{... | collective-permute-start | bytes 393224 | tf_op jit(solution)/shard_map/ppermute | solution.py:444
  88.6 17.4 %collective-permute-start.13 = (bf16[256,1024]{1,0:T(8,128)(2,1)S(1)}, bf16[256,1024]{1,0:T(8,128)(2,1)S(1)}, u32[]{:S(2)}, u32[]{:S(2)}) collective-permute-start(bf16[256,1024]{1,0:T(8,128)(2,1)S(1)} %get-tuple-element.51.refs_6_.refs_7_), channel_id=1, source_target_pairs={{0,2},{1,3},{2,0},{3,1},{4,6},{5,7},{6,4},{7,5},{8,10},{9,11},{10,... | collective-permute-start | bytes 1572872 | tf_op jit(solution)/shard_map/ppermute | solution.py:441
  90.1 25.5 %collective-permute-start.24 = (bf16[256,1024]{1,0:T(8,128)(2,1)S(1)}, bf16[256,1024]{1,0:T(8,128)(2,1)S(1)}, u32[]{:S(2)}, u32[]{:S(2)}) collective-permute-start(bf16[256,1024]{1,0:T(8,128)(2,1)S(1)} %get-tuple-element.52.refs_7_.refs_8_), channel_id=1, source_target_pairs={{0,2},{1,3},{2,0},{3,1},{4,6},{5,7},{6,4},{7,5},{8,10},{9,11},{10,... | collective-permute-start | bytes 1572872 | tf_op jit(solution)/shard_map/ppermute | solution.py:441
  90.6 25.1 %collective-permute-start.25 = (bf16[256,1024]{1,0:T(8,128)(2,1)S(1)}, bf16[256,1024]{1,0:T(8,128)(2,1)S(1)}, u32[]{:S(2)}, u32[]{:S(2)}) collective-permute-start(bf16[256,1024]{1,0:T(8,128)(2,1)S(1)} %collective-permute-done.8.refs_12_.refs_13_), channel_id=1, source_target_pairs={{0,1},{1,0},{2,3},{3,2},{4,5},{5,4},{6,7},{7,6},{8,9},{9,8},{10,11... | collective-permute-start | bytes 1572872 | tf_op jit(solution)/shard_map/ppermute | solution.py:437
  106.0 10.2 %collective-permute-start.26 = (bf16[256,1024]{1,0:T(8,128)(2,1)S(1)}, bf16[256,1024]{1,0:T(8,128)(2,1)S(1)}, u32[]{:S(2)}, u32[]{:S(2)}) collective-permute-start(bf16[256,1024]{1,0:T(8,128)(2,1)S(1)} %collective-permute-done.10.refs_13_.refs_14_), channel_id=1, source_target_pairs={{0,1},{1,0},{2,3},{3,2},{4,5},{5,4},{6,7},{7,6},{8,9},{9,8},{10,11... | collective-permute-start | bytes 1572872 | tf_op jit(solution)/shard_map/ppermute | solution.py:437
  106.6 9.7 %collective-permute-start.20 = (bf16[256,1024]{1,0:T(8,128)(2,1)S(1)}, bf16[256,1024]{1,0:T(8,128)(2,1)S(1)}, u32[]{:S(2)}, u32[]{:S(2)}) collective-permute-start(bf16[256,1024]{1,0:T(8,128)(2,1)S(1)} %get-tuple-element.49.refs_4_.refs_5_), channel_id=1, source_target_pairs={{0,1},{1,0},{2,3},{3,2},{4,5},{5,4},{6,7},{7,6},{8,9},{9,8},{10,11... | collective-permute-start | bytes 1572872 | tf_op jit(solution)/shard_map/ppermute | solution.py:437
  106.6 10.2 %collective-permute-start.21 = (bf16[256,1024]{1,0:T(8,128)(2,1)S(1)}, bf16[256,1024]{1,0:T(8,128)(2,1)S(1)}, u32[]{:S(2)}, u32[]{:S(2)}) collective-permute-start(bf16[256,1024]{1,0:T(8,128)(2,1)S(1)} %get-tuple-element.50.refs_5_.refs_6_), channel_id=1, source_target_pairs={{0,1},{1,0},{2,3},{3,2},{4,5},{5,4},{6,7},{7,6},{8,9},{9,8},{10,11... | collective-permute-start | bytes 1572872 | tf_op jit(solution)/shard_map/ppermute | solution.py:437
  116.9 14.9 %collective-permute-start.16 = (bf16[256,1024]{1,0:T(8,128)(2,1)S(1)}, bf16[256,1024]{1,0:T(8,128)(2,1)}, u32[]{:S(2)}, u32[]{:S(2)}) collective-permute-start(bf16[256,1024]{1,0:T(8,128)(2,1)S(1)} %get-tuple-element.68), channel_id=1, source_target_pairs={{0,2},{1,3},{2,0},{3,1},{4,6},{5,7},{6,4},{7,5},{8,10},{9,11},{10,... | collective-permute-start | bytes 1572872 | tf_op jit(solution)/shard_map/ppermute | solution.py:441
  118.5 25.6 %collective-permute-start.17 = (bf16[256,1024]{1,0:T(8,128)(2,1)S(1)}, bf16[256,1024]{1,0:T(8,128)(2,1)}, u32[]{:S(2)}, u32[]{:S(2)}) collective-permute-start(bf16[256,1024]{1,0:T(8,128)(2,1)S(1)} %get-tuple-element.67), channel_id=1, source_target_pairs={{0,2},{1,3},{2,0},{3,1},{4,6},{5,7},{6,4},{7,5},{8,10},{9,11},{10,... | collective-permute-start | bytes 1572872 | tf_op jit(solution)/shard_map/ppermute | solution.py:441
  142.0 28.4 %collective-permute-start.18 = (bf16[256,1024]{1,0:T(8,128)(2,1)S(1)}, bf16[256,1024]{1,0:T(8,128)(2,1)S(1)}, u32[]{:S(2)}, u32[]{:S(2)}) collective-permute-start(bf16[256,1024]{1,0:T(8,128)(2,1)S(1)} %get-tuple-element.66), channel_id=1, source_target_pairs={{0,2},{1,3},{2,0},{3,1},{4,6},{5,7},{6,4},{7,5},{8,10},{9,11},{10,... | collective-permute-start | bytes 1572872 | tf_op jit(solution)/shard_map/ppermute | solution.py:441
  143.5 26.9 %collective-permute-start.19 = (bf16[256,1024]{1,0:T(8,128)(2,1)S(1)}, bf16[256,1024]{1,0:T(8,128)(2,1)S(1)}, u32[]{:S(2)}, u32[]{:S(2)}) collective-permute-start(bf16[256,1024]{1,0:T(8,128)(2,1)S(1)} %get-tuple-element.65), channel_id=1, source_target_pairs={{0,2},{1,3},{2,0},{3,1},{4,6},{5,7},{6,4},{7,5},{8,10},{9,11},{10,... | collective-permute-start | bytes 1572872 | tf_op jit(solution)/shard_map/ppermute | solution.py:441
  144.1 26.9 %collective-permute-start.32 = (bf16[256,1024]{1,0:T(8,128)(2,1)}, bf16[256,1024]{1,0:T(8,128)(2,1)S(1)}, u32[]{:S(2)}, u32[]{:S(2)}) collective-permute-start(bf16[256,1024]{1,0:T(8,128)(2,1)} %collective-permute-done.16.refs_2_), channel_id=1, source_target_pairs={{0,1},{1,0},{2,3},{3,2},{4,5},{5,4},{6,7},{7,6},{8,9},{9,8},{10,11... | collective-permute-start | bytes 1572872 | tf_op jit(solution)/shard_map/ppermute | solution.py:437
  144.1 26.9 %collective-permute-start.33 = (bf16[256,1024]{1,0:T(8,128)(2,1)}, bf16[256,1024]{1,0:T(8,128)(2,1)S(1)}, u32[]{:S(2)}, u32[]{:S(2)}) collective-permute-start(bf16[256,1024]{1,0:T(8,128)(2,1)} %collective-permute-done.17.refs_3_), channel_id=1, source_target_pairs={{0,1},{1,0},{2,3},{3,2},{4,5},{5,4},{6,7},{7,6},{8,9},{9,8},{10,11... | collective-permute-start | bytes 1572872 | tf_op jit(solution)/shard_map/ppermute | solution.py:437
  (37 other events, 568.2 us)
Sparse Core Ops, SparseCore 0:
  44.8 78.8 all-gather.1

commit v7 on v6

--- a/solution.py
+++ b/solution.py
@@ -96,7 +96,7 @@
             ],
         ),
         out_shape=[half, half, jax.ShapeDtypeStruct((RANK, tok), F32)],
-        compiler_params=params(48),
+        compiler_params=params(60),
         cost_estimate=cost(6e9, error.size * 4, 2),
         name="error_sketch",
     )(jnp.reshape(core, (1,)), error, q_t, out_grad)
@@ -388,12 +388,13 @@
     out[...] = total
 
 
-def far_input_grad(prev, w_far, gs):
+def far_input_grad(prev, w_far, gs, start):
     outs = gs[0].shape[1]
     tok, part = prev.shape
     n_far = w_far.shape[1] // outs
+    rows = sum(g.shape[0] for g in gs) // n_far
     blk = min(256, part)
-    to = pl.BlockSpec((tok, blk), lambda i: (0, i))
+    to = pl.BlockSpec((rows, blk), lambda i: (start // rows, i))
     return pl.pallas_call(
         functools.partial(far_kernel, n_far=n_far),
         grid=(part // blk,),
@@ -402,12 +403,12 @@
         out_specs=to,
         out_shape=jax.ShapeDtypeStruct((tok, part), F32),
         scratch_shapes=[
-            pltpu.VMEM((n_far * tok, outs), BF16),
+            pltpu.VMEM((n_far * rows, outs), BF16),
             pltpu.SemaphoreType.DMA((len(gs),)),
         ],
         input_output_aliases={0: 0},
         compiler_params=params(24),
-        cost_estimate=cost(2 * n_far * tok * outs * part, 10e6, 1),
+        cost_estimate=cost(2 * n_far * rows * outs * part, 10e6, 1),
         name="input_grad_far",
     )(prev, w_far, *gs)
 
@@ -443,12 +444,13 @@
     def to_replica(a, k):
         return lax.ppermute(a, "dp", [(i, i ^ k) for i in range(n_dp)])
 
-    def over_replicas(a, chunks):
+    def over_replicas(a, beside, chunks):
         rounds = [1 << i for i in range(n_dp.bit_length() - 1)]
         for i, k in enumerate(rounds):
             if i == len(rounds) - 1:
                 a = after(a, chunks)
-            a = a + to_replica(a, k)
+            got = to_replica(a, k)
+            a = a + (after(got, beside) if i == 0 else got)
         return a
 
     src = jnp.stack([((y - k) % chips) * 2 + (c ^ e) for k in range(chips) for e in range(2)])
@@ -462,6 +464,8 @@
     w_start = [to_chip(a, k, e) for a, (k, e) in zip(w_parts, moves)]
     send, keep, y_own = local_sketch(c, error, after(q_t, *w_parts), out_grad, chips, part)
 
+    w_parts = after(w_start, send)
+
     got = to_sibling(send)
     y_t = y_own + to_sibling(y_own)
 
@@ -477,13 +481,12 @@
     high = part // n_chunk
     acts = after(activations, blocks, y_t)
     x_rows = [acts[:, i * high : (i + 1) * high].T for i in range(n_chunk)]
-    sketch = sketch_rows(e_list, y_list, activations, scale)
-    w_parts = after(w_start, sketch)
+    sketch = sketch_rows(after(e_list, x_rows), y_list, activations, scale)
     w_far = lax.all_gather(jnp.concatenate(w_parts, axis=1), "dp", axis=0, tiled=True)
     x_rows[0:2] = after(x_rows[0:2], e_list, y_list)
     x_far = [[to_chip(a, k) for k in steps] for a in x_rows[0:2]]
     w_sib = lax.dynamic_slice(after(weight, sketch), ((t ^ 1) * part, 0), (part, outs))
-    sketch = after(over_replicas(sketch, x_far[0]), x_far[1])
+    sketch = after(over_replicas(sketch, w_sib, x_far[0]), x_far[1])
     mine = jnp.stack([sketch] + [to_chip(sketch, k) for k in steps])
     x_rows[2:4] = after(x_rows[2:4], mine)
     x_far += [[to_chip(a, k) for k in steps] for a in x_rows[2:4]]
@@ -502,22 +505,26 @@
         held = [a[n] for a in x_far]
         pieces += held + [to_sibling(a) for a in held]
 
-    span = tok // n_chunk
+    cuts = [0, tok // 8, tok // 2, 3 * tok // 4, tok]
     g_rows = after(out_grad, basis_t)
-    g_far = [
-        [to_chip(g_rows[i * span : (i + 1) * span], k) for k in steps] for i in range(n_chunk)
-    ]
+    g_far = [[to_chip(g_rows[lo:hi], k) for k in steps] for lo, hi in zip(cuts[:-1], cuts[1:])]
     right = after(right_grad(src, basis_t, right_e, out_grad, pieces, scale), g_far[0])
-    right = after(over_replicas(right, ()), g_far[1])
+    right = after(over_replicas(right, (), ()), g_far[1])
     new_error, q_t = update_error(
         src, error, basis_t, out_grad, pieces, right, n_dp, scale
     )
-    gs = []
-    g_far[2:] = after(g_far[2:], q_t)
-    for n in range(len(steps)):
-        held = [a[n] for a in g_far]
-        gs += held + [to_sibling(a) for a in held]
-    grad = far_input_grad(grad, w_far, gs)
+
+    def far(grad, chunks, start):
+        gs = []
+        for n in range(len(steps)):
+            held = [a[n] for a in chunks]
+            gs += held + [to_sibling(a) for a in held]
+        return far_input_grad(grad, w_far, gs, start)
+
+    g_far[2] = after(g_far[2], q_t)
+    grad = far(after(grad, q_t), g_far[0:2], 0)
+    for i in (2, 3):
+        grad = far(grad, [g_far[i] if i == 2 else after(g_far[i], grad)], cuts[i])
     return (grad, new_error[None], q_t.T)
 
 

time: 192 us -> 190 us (0.990)
  waiting for transfers between devices: 67.1 us -> 43.9 us
  Pallas kernels: 68.4 us -> 78.9 us
  starting transfers between devices: 25.6 us -> 31.1 us
  local copies, waits for them, and re-layouts: 12 us -> 16.2 us
    ppermute x6, waiting for transfers between devices: 37.9 us -> 24.7 us  [to_replica(): return lax.ppermute(a, 'dp', [(i, i ^ k) for i in range(n_dp)])]
    ppermute x13, waiting for transfers between devices: 26.2 us -> 14.4 us  [to_chip(): return lax.ppermute(a, ('chip', 'core'), pairs)]
    ppermute x6, starting transfers between devices: 6.11 us -> 13.4 us  [to_replica(): return lax.ppermute(a, 'dp', [(i, i ^ k) for i in range(n_dp)])]
    pallas_call x1 -> x3, Pallas kernels: 9.13 us -> 16.3 us  [far_input_grad(): pl.pallas_call(functools.partial(far_kernel, n_far=n_far), grid=(part //...]
    slice x1 -> x3, local copies, waits for them, and re-layouts: 0.17 us -> 4.34 us  [per_device(): g_rows[lo:hi]]
    unnamed x48 -> x56, local copies, waits for them, and re-layouts: 4.76 us -> 3.43 us
  transfers between devices with their start and end apart: 37 -> 37, of which waited for: 13 -> 15; matrix products, arithmetic and copies ran while one was open for 4% -> 8% of each run, Pallas kernels for 26% -> 39%
where the time goes in v7:
time: 190 us; the launch traced here: 189 us
  Pallas kernels  78.9 us (42%)
  waiting for transfers between devices  43.9 us (23%)
  starting transfers between devices  31.1 us (16%)
  local copies, waits for them, and re-layouts  16.2 us (9%)
  between operations  14.6 us (8%)
  other arithmetic  4.25 us (2%)
    ppermute x6, waiting for transfers between devices, to_replica(): return lax.ppermute(a, 'dp', [(i, i ^ k) for i in range(n_dp)])  24.7 us
    pallas_call x1, Pallas kernels, update_error(): pl.pallas_call(functools.partial(update_kernel, n_t=n_t, per=len(pieces)...  21.1 us
    pallas_call x3, Pallas kernels, far_input_grad(): pl.pallas_call(functools.partial(far_kernel, n_far=n_far), grid=(part //...  16.3 us
    ppermute x13, waiting for transfers between devices, to_chip(): return lax.ppermute(a, ('chip', 'core'), pairs)  14.4 us
    ppermute x13, starting transfers between devices, to_chip(): return lax.ppermute(a, ('chip', 'core'), pairs)  13.7 us
    ppermute x6, starting transfers between devices, to_replica(): return lax.ppermute(a, 'dp', [(i, i ^ k) for i in range(n_dp)])  13.4 us
    pallas_call x1, Pallas kernels, local_sketch(): pl.pallas_call(sketch_kernel, grid_spec=pltpu.PrefetchScalarGridSpec(num_...  10.7 us
    pallas_call x1, Pallas kernels, right_error(): pl.pallas_call(right_error_kernel, grid=(din // blk,), in_specs=[pl.Block...  9.73 us
  transfers between devices with their start and end apart: 37, of which 15 were waited for; matrix products, arithmetic and copies ran while one was open for 8% of the time, Pallas kernels for 39%

profile of v7, /device:TPU:0, one launch (start us, length us, event | category | flops | bytes accessed | tf_op | source)
XLA Modules:
  0.0 189.0 jit_solution(14523429626465594619)
XLA Ops:
  8.3 3.0 %collective-permute-start.28 = (bf16[128,1024]{1,0:T(8,128)(2,1)S(1)}, bf16[128,1024]{1,0:T(8,128)(2,1)S(1)}, u32[]{:S(2)}, u32[]{:S(2)}) collective-permute-start(bf16[128,1024]{1,0:T(8,128)(2,1)S(1)} %get-tuple-element.72), channel_id=1, source_target_pairs={{0,2},{1,3},{2,0},{3,1},{4,6},{5,7},{6,4},{7,5},{8,10},{9,11},{10,... | collective-permute-start | bytes 786440 | tf_op jit(solution)/shard_map/ppermute | solution.py:442
  11.3 10.7 %error_sketch.1 = (f32[2,32,1024]{2,1,0:T(8,128)}, f32[2,32,1024]{2,1,0:T(8,128)}, f32[32,1024]{1,0:T(8,128)}) custom-call(s32[1]{0:T(128)} %bitcast.1.ids, f32[4096,1024]{1,0:T(8,128)} %bitcast.26, f32[32,1024]{1,0:T(8,128)} %bitcast.29, bf16[1024,1024]{1,0:T(8,128)(2,1)} %refs_3_.3), custom_call_target="tpu_custom_call" | custom-call | flops 12000000000 | bytes 33554432 | tf_op jit(solution)/shard_map/error_sketch/pallas_call | solution.py:77
  30.3 2.5 %copy.11 = bf16[1024,1024]{0,1:T(8,128)(2,1)} copy(bf16[1024,1024]{1,0:T(8,128)(2,1)S(1)} %copy-done.1) | data formatting | bytes 4194304 | tf_op jit(solution)/shard_map/optimization_barrier | solution.py:417
  37.2 3.1 %constant_dynamic-slice_fusion = bf16[1024,1024]{1,0:T(8,128)(2,1)} fusion(bf16[4096,1024]{1,0:T(8,128)(2,1)} %w_ref.1, s32[]{:T(128)S(6)} %select_n.49), kind=kLoop, calls=%fused_computation.8 | loop fusion | bytes 4194308 | tf_op jit(solution)/shard_map/dynamic_slice | solution.py:488
  44.3 3.5 %collective-permute-done.6 = f32[32,1024]{1,0:T(8,128)S(1)} collective-permute-done((f32[32,1024]{1,0:T(8,128)S(1)}, f32[32,1024]{1,0:T(8,128)S(1)}, u32[]{:S(2)}, u32[]{:S(2)}) %collective-permute-start.6) | collective-permute-done | bytes 131104 | tf_op jit(solution)/shard_map/ppermute | solution.py:445
  49.4 6.5 %collective-permute-done.7 = f32[32,1024]{1,0:T(8,128)S(1)} collective-permute-done((f32[32,1024]{1,0:T(8,128)S(1)}, f32[32,1024]{1,0:T(8,128)S(1)}, u32[]{:S(2)}, u32[]{:S(2)}) %collective-permute-start.7) | collective-permute-done | bytes 131104 | tf_op jit(solution)/shard_map/ppermute | solution.py:445
  56.0 2.5 %collective-permute-start.9 = (f32[32,1024]{1,0:T(8,128)S(1)}, f32[32,1024]{1,0:T(8,128)S(1)}, u32[]{:S(2)}, u32[]{:S(2)}) collective-permute-start(f32[32,1024]{1,0:T(8,128)S(1)} %add.123), channel_id=1, source_target_pairs={{0,16},{4,20},{8,24},{12,28},{16,0},{20,4},{24,8},{28,12},{1,17},{... | collective-permute-start | bytes 393224 | tf_op jit(solution)/shard_map/ppermute | solution.py:445
  58.5 6.3 %collective-permute-done.9 = f32[32,1024]{1,0:T(8,128)S(1)} collective-permute-done((f32[32,1024]{1,0:T(8,128)S(1)}, f32[32,1024]{1,0:T(8,128)S(1)}, u32[]{:S(2)}, u32[]{:S(2)}) %collective-permute-start.9) | collective-permute-done | bytes 131104 | tf_op jit(solution)/shard_map/ppermute | solution.py:445
  67.1 3.7 %collective-permute-done.11 = f32[32,1024]{1,0:T(8,128)S(1)} collective-permute-done((f32[32,1024]{1,0:T(8,128)S(1)}, f32[32,1024]{1,0:T(8,128)S(1)}, u32[]{:S(2)}, u32[]{:S(2)}) %collective-permute-start.11) | collective-permute-done | bytes 131104 | tf_op jit(solution)/shard_map/ppermute | solution.py:442
  73.1 5.1 %basis.1.b_ref.refs_1_.refs_2_ = f32[32,4096]{1,0:T(8,128)S(1)} custom-call(s32[4]{0:T(128)S(1)} %pad_add_fusion.src.refs_0_, f32[2,32,1024]{2,1,0:T(8,128)S(1)} %pad_maximum_fusion.1.mine, f32[2,32,1024]{2,1,0:T(8,128)S(1)} %collective-permute-done.12.other), custom_call_target="tpu_custom_call" | custom-call | flops 6000000 | bytes 2000 | tf_op jit(solution)/shard_map/basis/pallas_call | solution.py:154
  78.2 9.7 %right_error.1.refs_2_ = f32[32,1024]{1,0:T(8,128)S(1)} custom-call(f32[4096,1024]{1,0:T(8,128)} %bitcast.27, f32[32,4096]{1,0:T(8,128)S(1)} %basis.1.b_ref.refs_1_.refs_2_), custom_call_target="tpu_custom_call" | custom-call | flops 8000000000 | bytes 16777216 | tf_op jit(solution)/shard_map/right_error/pallas_call | solution.py:180
  88.7 7.9 %collective-permute-done.18.refs_15_.refs_16_ = bf16[256,1024]{1,0:T(8,128)(2,1)S(1)} collective-permute-done((bf16[256,1024]{1,0:T(8,128)(2,1)S(1)}, bf16[256,1024]{1,0:T(8,128)(2,1)S(1)}, u32[]{:S(2)}, u32[]{:S(2)}) %collective-permute-start.18) | collective-permute-done | bytes 524320 | tf_op jit(solution)/shard_map/ppermute | solution.py:442
  97.1 9.2 %input_grad_near.1.refs_0_ = f32[1024,1024]{1,0:T(8,128)} custom-call(s32[1]{0:T(128)} %bitcast.ids, bf16[1024,1024]{1,0:T(8,128)(2,1)} %refs_3_.3, bf16[1024,1024]{1,0:T(8,128)(2,1)} %collective-permute-done.gs_ref, bf16[4096,1024]{1,0:T(8,128)(2,1)} %w_ref.1, bf16[1024,1024]{1,0:T(8,128)(2,1)} %collective-permute-done.5.ws_ref), custom_call_target="tpu_custom_call" | custom-call | flops 8589934592 | bytes 24000000 | tf_op jit(solution)/shard_map/input_grad_near/pallas_call | solution.py:349
  111.6 5.4 %right_grad.1 = f32[32,1024]{1,0:T(8,128)S(1)} custom-call(s32[4]{0:T(128)S(1)} %pad_add_fusion.src.refs_0_, f32[32,4096]{1,0:T(8,128)S(1)} %basis.1.b_ref.refs_1_.refs_2_, f32[32,1024]{1,0:T(8,128)S(1)} %right_error.1.refs_2_, bf16[1024,1024]{1,0:T(8,128)(2,1)} %refs_3_.3, bf16[256,1024]{1,0:T(8,128)(2,1)S(1)} %copy-done.8, ...), custom_call_target="tpu_custom_call" | custom-call | flops 4000000 | bytes 8388 | tf_op jit(solution)/shard_map/right_grad/pallas_call | solution.py:241
  118.8 3.5 %collective-permute-done.24 = f32[32,1024]{1,0:T(8,128)S(1)} collective-permute-done((f32[32,1024]{1,0:T(8,128)S(1)}, f32[32,1024]{1,0:T(8,128)S(1)}, u32[]{:S(2)}, u32[]{:S(2)}) %collective-permute-start.24) | collective-permute-done | bytes 131104 | tf_op jit(solution)/shard_map/ppermute | solution.py:445
  122.3 2.7 %collective-permute-start.25 = (f32[32,1024]{1,0:T(8,128)S(1)}, f32[32,1024]{1,0:T(8,128)S(1)}, u32[]{:S(2)}, u32[]{:S(2)}) collective-permute-start(f32[32,1024]{1,0:T(8,128)S(1)} %add.125), channel_id=1, source_target_pairs={{0,8},{4,12},{8,0},{12,4},{16,24},{20,28},{24,16},{28,20},{1,9},{5... | collective-permute-start | bytes 393224 | tf_op jit(solution)/shard_map/ppermute | solution.py:445
  125.0 2.9 %collective-permute-done.25 = f32[32,1024]{1,0:T(8,128)S(1)} collective-permute-done((f32[32,1024]{1,0:T(8,128)S(1)}, f32[32,1024]{1,0:T(8,128)S(1)}, u32[]{:S(2)}, u32[]{:S(2)}) %collective-permute-start.25) | collective-permute-done | bytes 131104 | tf_op jit(solution)/shard_map/ppermute | solution.py:445
  128.0 3.5 %collective-permute-start.26 = (f32[32,1024]{1,0:T(8,128)S(1)}, f32[32,1024]{1,0:T(8,128)S(1)}, u32[]{:S(2)}, u32[]{:S(2)}) collective-permute-start(f32[32,1024]{1,0:T(8,128)S(1)} %add.126), channel_id=1, source_target_pairs={{0,16},{4,20},{8,24},{12,28},{16,0},{20,4},{24,8},{28,12},{1,17},{... | collective-permute-start | bytes 393224 | tf_op jit(solution)/shard_map/ppermute | solution.py:445
  131.5 2.1 %fusion = (bf16[256,1024]{1,0:T(8,128)(2,1)}, bf16[256,1024]{1,0:T(8,128)(2,1)S(1)}) fusion(bf16[1024,1024]{1,0:T(8,128)(2,1)} %refs_3_.3), kind=kLoop, calls=%fused_computation.12 | loop fusion | bytes 2097152 | tf_op jit(solution)/shard_map/slice | solution.py:510
  136.8 21.1 %update_error.1 = (f32[4096,1024]{1,0:T(8,128)}, f32[32,1024]{1,0:T(8,128)}) custom-call(s32[4]{0:T(128)} %copy-done.27, f32[4096,1024]{1,0:T(8,128)} %bitcast.28, f32[32,4096]{1,0:T(8,128)} %copy-done.2, bf16[1024,1024]{1,0:T(8,128)(2,1)} %refs_3_.3, f32[32,1024]{1,0:T(8,128)} %add.127.refs_4_, bf16[256,1024]{1,0:T(8,128)(2,1)} %copy-done.7, ...), custom_call_target="tpu_custom_call" | custom-call | flops 8999999488 | bytes 41943040 | tf_op jit(solution)/shard_map/update_error/pallas_call | solution.py:308
  160.3 2.2 %copy-done = bf16[1024,2048]{1,0:T(8,128)(2,1)S(1)} copy-done((bf16[1024,2048]{1,0:T(8,128)(2,1)S(1)}, bf16[1024,2048]{1,0:T(8,128)(2,1)}, u32[]{:S(2)}) %copy-start) | copy-done | bytes 4194328
  163.7 5.6 %input_grad_far.3.refs_0_ = f32[1024,1024]{1,0:T(8,128)} custom-call(f32[1024,1024]{1,0:T(8,128)} %input_grad_near.1.refs_0_, bf16[1024,2048]{1,0:T(8,128)(2,1)S(1)} %copy-done, bf16[128,1024]{1,0:T(8,128)(2,1)S(1)} %copy-done.26, bf16[384,1024]{1,0:T(8,128)(2,1)S(1)} %copy-done.10, ...), custom_call_target="tpu_custom_call", output_to_operand_aliasing={{}: (0, {})} | custom-call | flops 2147483648 | bytes 10000000 | tf_op jit(solution)/shard_map/input_grad_far/pallas_call | solution.py:398
  169.2 5.4 %input_grad_far.4.refs_0_ = f32[1024,1024]{1,0:T(8,128)} custom-call(f32[1024,1024]{1,0:T(8,128)} %input_grad_far.3.refs_0_, bf16[1024,2048]{1,0:T(8,128)(2,1)S(1)} %copy-done, bf16[256,1024]{1,0:T(8,128)(2,1)S(1)} %collective-permute-done.32.refs_2_, bf16[256,1024]{1,0:T(8,128)(2,1)} %collective-permute-done.33.refs_3_), custom_call_target="tpu_custom_call", output_to_operand_aliasing={{}: (0, {})} | custom-call | flops 1073741824 | bytes 10000000 | tf_op jit(solution)/shard_map/input_grad_far/pallas_call | solution.py:398
  176.8 5.3 %input_grad_far.5 = f32[1024,1024]{1,0:T(8,128)} custom-call(f32[1024,1024]{1,0:T(8,128)} %input_grad_far.4.refs_0_, bf16[1024,2048]{1,0:T(8,128)(2,1)S(1)} %copy-done, bf16[256,1024]{1,0:T(8,128)(2,1)} %collective-permute-done.34.refs_2_, bf16[256,1024]{1,0:T(8,128)(2,1)S(1)} %collective-permute-done.35.refs_3_), custom_call_target="tpu_custom_call", output_to_operand_aliasing={{}: (0, {})} | custom-call | flops 1073741824 | bytes 10000000 | tf_op jit(solution)/shard_map/input_grad_far/pallas_call | solution.py:398
  (135 shorter events, 40.8 us)
Async XLA Ops:
  7.2 153.2 %all-gather.2.cloned.1.call-start = ((), (), s32[]{:S(2)}) async-start(), calls=%async_computation | async-start | bytes 4718592 | tf_op jit(solution)/shard_map/all_gather | solution.py:485
  8.3 13.7 %collective-permute-start.28 = (bf16[128,1024]{1,0:T(8,128)(2,1)S(1)}, bf16[128,1024]{1,0:T(8,128)(2,1)S(1)}, u32[]{:S(2)}, u32[]{:S(2)}) collective-permute-start(bf16[128,1024]{1,0:T(8,128)(2,1)S(1)} %get-tuple-element.72), channel_id=1, source_target_pairs={{0,2},{1,3},{2,0},{3,1},{4,6},{5,7},{6,4},{7,5},{8,10},{9,11},{10,... | collective-permute-start | bytes 786440 | tf_op jit(solution)/shard_map/ppermute | solution.py:442
  11.3 11.2 %collective-permute-start.29 = (bf16[128,1024]{1,0:T(8,128)(2,1)S(1)}, bf16[128,1024]{1,0:T(8,128)(2,1)S(1)}, u32[]{:S(2)}, u32[]{:S(2)}) collective-permute-start(bf16[128,1024]{1,0:T(8,128)(2,1)S(1)} %get-tuple-element.71), channel_id=1, source_target_pairs={{0,3},{1,2},{2,1},{3,0},{4,7},{5,6},{6,5},{7,4},{8,11},{9,10},{10,... | collective-permute-start | bytes 786440 | tf_op jit(solution)/shard_map/ppermute | solution.py:442
  26.5 9.3 %collective-permute-start.4 = (f32[32,1024]{1,0:T(8,128)S(1)}, f32[32,1024]{1,0:T(8,128)S(1)}, u32[]{:S(2)}, u32[]{:S(2)}) collective-permute-start(f32[32,1024]{1,0:T(8,128)S(1)} %add.115.refs_2_), channel_id=1, source_target_pairs={{0,2},{1,3},{2,0},{3,1},{4,6},{5,7},{6,4},{7,5},{8,10},{9,11},{10,... | collective-permute-start | bytes 393224 | tf_op jit(solution)/shard_map/ppermute | solution.py:442
  40.3 48.4 %collective-permute-start.5 = (bf16[1024,1024]{1,0:T(8,128)(2,1)}, bf16[1024,1024]{1,0:T(8,128)(2,1)}, u32[]{:S(2)}, u32[]{:S(2)}) collective-permute-start(bf16[1024,1024]{1,0:T(8,128)(2,1)} %constant_dynamic-slice_fusion), channel_id=1, source_target_pairs={{0,1},{1,0},{2,3},{3,2},{4,5},{5,4},{6,7},{7,6},{8,9},{9,8},{10,11... | collective-permute-start | bytes 6291464 | tf_op jit(solution)/shard_map/ppermute | solution.py:438
  40.3 56.3 %collective-permute-start = (bf16[1024,1024]{1,0:T(8,128)(2,1)}, bf16[1024,1024]{1,0:T(8,128)(2,1)}, u32[]{:S(2)}, u32[]{:S(2)}) collective-permute-start(bf16[1024,1024]{1,0:T(8,128)(2,1)} %refs_3_.3), channel_id=1, source_target_pairs={{0,1},{1,0},{2,3},{3,2},{4,5},{5,4},{6,7},{7,6},{8,9},{9,8},{10,11... | collective-permute-start | bytes 6291464 | tf_op jit(solution)/shard_map/ppermute | solution.py:438
  40.8 15.2 %collective-permute-start.8 = (bf16[256,1024]{1,0:T(8,128)(2,1)S(1)}, bf16[256,1024]{1,0:T(8,128)(2,1)S(1)}, u32[]{:S(2)}, u32[]{:S(2)}) collective-permute-start(bf16[256,1024]{1,0:T(8,128)(2,1)S(1)} %get-tuple-element.53.refs_4_.refs_5_), channel_id=1, source_target_pairs={{0,2},{1,3},{2,0},{3,1},{4,6},{5,7},{6,4},{7,5},{8,10},{9,11},{10,... | collective-permute-start | bytes 1572872 | tf_op jit(solution)/shard_map/ppermute | solution.py:442
  42.0 23.8 %collective-permute-start.10 = (bf16[256,1024]{1,0:T(8,128)(2,1)S(1)}, bf16[256,1024]{1,0:T(8,128)(2,1)S(1)}, u32[]{:S(2)}, u32[]{:S(2)}) collective-permute-start(bf16[256,1024]{1,0:T(8,128)(2,1)S(1)} %get-tuple-element.54.refs_5_.refs_6_), channel_id=1, source_target_pairs={{0,2},{1,3},{2,0},{3,1},{4,6},{5,7},{6,4},{7,5},{8,10},{9,11},{10,... | collective-permute-start | bytes 1572872 | tf_op jit(solution)/shard_map/ppermute | solution.py:442
  47.8 8.2 %collective-permute-start.7 = (f32[32,1024]{1,0:T(8,128)S(1)}, f32[32,1024]{1,0:T(8,128)S(1)}, u32[]{:S(2)}, u32[]{:S(2)}) collective-permute-start(f32[32,1024]{1,0:T(8,128)S(1)} %add.122), channel_id=1, source_target_pairs={{0,8},{4,12},{8,0},{12,4},{16,24},{20,28},{24,16},{28,20},{1,9},{5... | collective-permute-start | bytes 393224 | tf_op jit(solution)/shard_map/ppermute | solution.py:445
  56.0 8.8 %collective-permute-start.9 = (f32[32,1024]{1,0:T(8,128)S(1)}, f32[32,1024]{1,0:T(8,128)S(1)}, u32[]{:S(2)}, u32[]{:S(2)}) collective-permute-start(f32[32,1024]{1,0:T(8,128)S(1)} %add.123), channel_id=1, source_target_pairs={{0,16},{4,20},{8,24},{12,28},{16,0},{20,4},{24,8},{28,12},{1,17},{... | collective-permute-start | bytes 393224 | tf_op jit(solution)/shard_map/ppermute | solution.py:445
  71.0 16.9 %collective-permute-start.13 = (bf16[256,1024]{1,0:T(8,128)(2,1)S(1)}, bf16[256,1024]{1,0:T(8,128)(2,1)S(1)}, u32[]{:S(2)}, u32[]{:S(2)}) collective-permute-start(bf16[256,1024]{1,0:T(8,128)(2,1)S(1)} %get-tuple-element.55.refs_6_.refs_7_), channel_id=1, source_target_pairs={{0,2},{1,3},{2,0},{3,1},{4,6},{5,7},{6,4},{7,5},{8,10},{9,11},{10,... | collective-permute-start | bytes 1572872 | tf_op jit(solution)/shard_map/ppermute | solution.py:442
  72.3 24.3 %collective-permute-start.18 = (bf16[256,1024]{1,0:T(8,128)(2,1)S(1)}, bf16[256,1024]{1,0:T(8,128)(2,1)S(1)}, u32[]{:S(2)}, u32[]{:S(2)}) collective-permute-start(bf16[256,1024]{1,0:T(8,128)(2,1)S(1)} %get-tuple-element.56.refs_7_.refs_8_), channel_id=1, source_target_pairs={{0,2},{1,3},{2,0},{3,1},{4,6},{5,7},{6,4},{7,5},{8,10},{9,11},{10,... | collective-permute-start | bytes 1572872 | tf_op jit(solution)/shard_map/ppermute | solution.py:442
  73.1 33.2 %collective-permute-start.14 = (bf16[256,1024]{1,0:T(8,128)(2,1)}, bf16[256,1024]{1,0:T(8,128)(2,1)S(1)}, u32[]{:S(2)}, u32[]{:S(2)}) collective-permute-start(bf16[256,1024]{1,0:T(8,128)(2,1)} %copy-done.7), channel_id=1, source_target_pairs={{0,1},{1,0},{2,3},{3,2},{4,5},{5,4},{6,7},{7,6},{8,9},{9,8},{10,11... | collective-permute-start | bytes 1572872 | tf_op jit(solution)/shard_map/ppermute | solution.py:438
  88.0 18.5 %collective-permute-start.15 = (bf16[256,1024]{1,0:T(8,128)(2,1)S(1)}, bf16[256,1024]{1,0:T(8,128)(2,1)S(1)}, u32[]{:S(2)}, u32[]{:S(2)}) collective-permute-start(bf16[256,1024]{1,0:T(8,128)(2,1)S(1)} %copy-done.6), channel_id=1, source_target_pairs={{0,1},{1,0},{2,3},{3,2},{4,5},{5,4},{6,7},{7,6},{8,9},{9,8},{10,11... | collective-permute-start | bytes 1572872 | tf_op jit(solution)/shard_map/ppermute | solution.py:438
  88.6 18.3 %collective-permute-start.16 = (bf16[256,1024]{1,0:T(8,128)(2,1)S(1)}, bf16[256,1024]{1,0:T(8,128)(2,1)S(1)}, u32[]{:S(2)}, u32[]{:S(2)}) collective-permute-start(bf16[256,1024]{1,0:T(8,128)(2,1)S(1)} %get-tuple-element.55.refs_6_.refs_7_), channel_id=1, source_target_pairs={{0,1},{1,0},{2,3},{3,2},{4,5},{5,4},{6,7},{7,6},{8,9},{9,8},{10,11... | collective-permute-start | bytes 1572872 | tf_op jit(solution)/shard_map/ppermute | solution.py:438
  96.6 11.5 %collective-permute-start.17 = (bf16[256,1024]{1,0:T(8,128)(2,1)S(1)}, bf16[256,1024]{1,0:T(8,128)(2,1)S(1)}, u32[]{:S(2)}, u32[]{:S(2)}) collective-permute-start(bf16[256,1024]{1,0:T(8,128)(2,1)S(1)} %get-tuple-element.56.refs_7_.refs_8_), channel_id=1, source_target_pairs={{0,1},{1,0},{2,3},{3,2},{4,5},{5,4},{6,7},{7,6},{8,9},{9,8},{10,11... | collective-permute-start | bytes 1572872 | tf_op jit(solution)/shard_map/ppermute | solution.py:438
  96.6 14.0 %collective-permute-start.19 = (bf16[256,1024]{1,0:T(8,128)(2,1)S(1)}, bf16[256,1024]{1,0:T(8,128)(2,1)S(1)}, u32[]{:S(2)}, u32[]{:S(2)}) collective-permute-start(bf16[256,1024]{1,0:T(8,128)(2,1)S(1)} %collective-permute-done.8.refs_12_.refs_13_), channel_id=1, source_target_pairs={{0,1},{1,0},{2,3},{3,2},{4,5},{5,4},{6,7},{7,6},{8,9},{9,8},{10,11... | collective-permute-start | bytes 1572872 | tf_op jit(solution)/shard_map/ppermute | solution.py:438
  108.1 9.2 %collective-permute-start.23 = (bf16[128,1024]{1,0:T(8,128)(2,1)S(1)}, bf16[128,1024]{1,0:T(8,128)(2,1)S(1)}, u32[]{:S(2)}, u32[]{:S(2)}) collective-permute-start(bf16[128,1024]{1,0:T(8,128)(2,1)S(1)} %slice.28), channel_id=1, source_target_pairs={{0,2},{1,3},{2,0},{3,1},{4,6},{5,7},{6,4},{7,5},{8,10},{9,11},{10,... | collective-permute-start | bytes 786440 | tf_op jit(solution)/shard_map/ppermute | solution.py:442
  110.6 23.5 %collective-permute-start.27 = (bf16[384,1024]{1,0:T(8,128)(2,1)S(1)}, bf16[384,1024]{1,0:T(8,128)(2,1)S(1)}, u32[]{:S(2)}, u32[]{:S(2)}) collective-permute-start(bf16[384,1024]{1,0:T(8,128)(2,1)S(1)} %slice.29), channel_id=1, source_target_pairs={{0,2},{1,3},{2,0},{3,1},{4,6},{5,7},{6,4},{7,5},{8,10},{9,11},{10,... | collective-permute-start | bytes 2359304 | tf_op jit(solution)/shard_map/ppermute | solution.py:442
  128.0 8.2 %collective-permute-start.26 = (f32[32,1024]{1,0:T(8,128)S(1)}, f32[32,1024]{1,0:T(8,128)S(1)}, u32[]{:S(2)}, u32[]{:S(2)}) collective-permute-start(f32[32,1024]{1,0:T(8,128)S(1)} %add.126), channel_id=1, source_target_pairs={{0,16},{4,20},{8,24},{12,28},{16,0},{20,4},{24,8},{28,12},{1,17},{... | collective-permute-start | bytes 393224 | tf_op jit(solution)/shard_map/ppermute | solution.py:445
  133.6 24.3 %collective-permute-start.32 = (bf16[256,1024]{1,0:T(8,128)(2,1)S(1)}, bf16[256,1024]{1,0:T(8,128)(2,1)S(1)}, u32[]{:S(2)}, u32[]{:S(2)}) collective-permute-start(bf16[256,1024]{1,0:T(8,128)(2,1)S(1)} %get-tuple-element.74), channel_id=1, source_target_pairs={{0,2},{1,3},{2,0},{3,1},{4,6},{5,7},{6,4},{7,5},{8,10},{9,11},{10,... | collective-permute-start | bytes 1572872 | tf_op jit(solution)/shard_map/ppermute | solution.py:442
  134.2 26.2 %collective-permute-start.31 = (bf16[384,1024]{1,0:T(8,128)(2,1)S(1)}, bf16[384,1024]{1,0:T(8,128)(2,1)S(1)}, u32[]{:S(2)}, u32[]{:S(2)}) collective-permute-start(bf16[384,1024]{1,0:T(8,128)(2,1)S(1)} %collective-permute-done.27.refs_3_), channel_id=1, source_target_pairs={{0,1},{1,0},{2,3},{3,2},{4,5},{5,4},{6,7},{7,6},{8,9},{9,8},{10,11... | collective-permute-start | bytes 2359304 | tf_op jit(solution)/shard_map/ppermute | solution.py:438
  158.0 11.2 %collective-permute-start.33 = (bf16[256,1024]{1,0:T(8,128)(2,1)S(1)}, bf16[256,1024]{1,0:T(8,128)(2,1)}, u32[]{:S(2)}, u32[]{:S(2)}) collective-permute-start(bf16[256,1024]{1,0:T(8,128)(2,1)S(1)} %collective-permute-done.32.refs_2_), channel_id=1, source_target_pairs={{0,1},{1,0},{2,3},{3,2},{4,5},{5,4},{6,7},{7,6},{8,9},{9,8},{10,11... | collective-permute-start | bytes 1572872 | tf_op jit(solution)/shard_map/ppermute | solution.py:438
  158.6 16.1 %collective-permute-start.34 = (bf16[256,1024]{1,0:T(8,128)(2,1)}, bf16[256,1024]{1,0:T(8,128)(2,1)}, u32[]{:S(2)}, u32[]{:S(2)}) collective-permute-start(bf16[256,1024]{1,0:T(8,128)(2,1)} %get-tuple-element.73), channel_id=1, source_target_pairs={{0,2},{1,3},{2,0},{3,1},{4,6},{5,7},{6,4},{7,5},{8,10},{9,11},{10,... | collective-permute-start | bytes 1572872 | tf_op jit(solution)/shard_map/ppermute | solution.py:442
  (41 other events, 623.1 us)
Sparse Core Ops, SparseCore 0:
  23.5 77.8 all-gather.1
